TPU v7x, 32 devices: a whole 2x2x4 slice. The times are simulated.
32 devices in a mesh: groups: 2 (over y), particle: 4 (over z), cls: 4 (over x, core).
Axes of the slice: x: 2, y: 2, z: 4, core: 2. Of those that a mesh axis runs over, the one named last changes fastest.
Arguments:
- pool: bfloat16 [1536, 4096], P(('groups', 'particle', 'cls')), parts along dimension 0, may hold values from -48 to 48
- picks: int32 [768], P(('groups', 'particle', 'cls')), parts along dimension 0, may hold values from 0 to 47, as said below
- groups: int32 [768], P(('groups', 'particle', 'cls')), parts along dimension 0, may hold values from 0 to 63
- ctf_table: float32 [128, 32], P('groups'), parts along dimension 0, may hold values from 0.5 to 1
- shifts: int32 [72], P('groups'), parts along dimension 0, may hold values from 0 to 127, as said below
- classes: float32 [800, 4096], P(('groups', 'cls')), parts along dimension 0
- log_prior: float32 [800], P(('groups', 'cls')), parts along dimension 0, may hold values from -1 to 1
Outputs:
- new_classes: float32 [800, 4096], P(('groups', 'cls')), parts along dimension 0
- log_evidence: float32 [768], P(('groups', 'particle')), parts along dimension 0
There are 2 independent parts, one for each index of `groups`. A program takes and returns all parts, laid end to end along the dimension named above; each array names one. Nothing has to cross between parts.
Inputs may be any that keep to these rules, and one draw needn't show every extreme that they name: `picks`: the 24 entries of each device are distinct rows of that device's own 48 pool rows, counted from its first. `shifts`: distinct angular offsets, 0 and 127 among them.
All inputs are finite; a program needn't handle non-finite values.
Results may differ from a plain program's by a relative error of at most 0.0052.
Values may be sent and summed in bfloat16 or wider, within the bound.
No kernel may reach another device: no remote copies, remote signals or barrier semaphores. Data moves between devices by JAX's collectives and lax.ppermute only.
A program may use at most 64 MiB of HBM per device.

v0:
```python
import math

import jax
import jax.numpy as jnp
from jax import lax
from jax.sharding import PartitionSpec as P

CYCLES = 32
ANG = 128
ROT = 36


STEP_WEIGHT = 0.5
PRIOR_WEIGHT = 1.0


def joined(part, axis, combine):
    gathered = jax.tree.map(lambda a: lax.all_gather(a, axis), part)

    def take(source):
        return jax.tree.map(lambda a: lax.dynamic_index_in_dim(a, source, 0, False), gathered)

    return lax.fori_loop(
        1, lax.axis_size(axis), lambda source, state: combine(state, take(source)), take(0)
    )


def angle_major(images):
    count_rows = images.shape[0]
    return jnp.transpose(images.reshape(count_rows, CYCLES, ANG), (2, 1, 0)).reshape(
        ANG * CYCLES, count_rows
    )


def turned_view(doubled, offset):
    return lax.dynamic_slice_in_dim(doubled, offset * CYCLES, ANG * CYCLES, 0)


def all_scores(doubled, refs_major, shift_blocks):
    block_len = shift_blocks.shape[1]

    def single(shift_row):
        outputs = []
        for slot in range(block_len):
            piece = turned_view(doubled, shift_row[slot])
            outputs.append(
                lax.dot_general(
                    piece, refs_major, (((0,), (0,)), ((), ())), preferred_element_type=jnp.float32
                )
            )
        return jnp.stack(outputs, axis=0)

    partial_value = lax.map(single, shift_blocks)
    return partial_value.reshape(-1, partial_value.shape[2], partial_value.shape[3])


def class_numerator(doubled, weights, shift_blocks):
    nblocks, block_len = shift_blocks.shape
    weight_blocks = weights.reshape(nblocks, block_len, weights.shape[1], weights.shape[2])

    def advance(carried, pieces):
        shift_row, weight_block = pieces
        for slot in range(block_len):
            piece = turned_view(doubled, shift_row[slot])
            carried = carried + jnp.dot(
                piece, weight_block[slot], preferred_element_type=jnp.float32
            )
        return (carried, None)

    start_value = jnp.zeros((ANG * CYCLES, weights.shape[2]), jnp.float32)
    numerator_major, _ = lax.scan(advance, start_value, (shift_blocks, weight_blocks))
    classes_here = weights.shape[2]
    return jnp.transpose(numerator_major.reshape(ANG, CYCLES, classes_here), (2, 1, 0)).reshape(
        classes_here, CYCLES * ANG
    )


def merge_softmax(earlier, later):
    row_top = jnp.maximum(earlier[0], later[0])
    row_total = earlier[1] * jnp.exp(earlier[0] - row_top) + later[1] * jnp.exp(later[0] - row_top)
    return (row_top, row_total)


def on_device(pool, picks, groups, ctf_table, shifts, classes, log_prior):
    chosen = jnp.take(pool, picks, axis=0)
    count_local = chosen.shape[0]
    onehot_rows = (
        groups[:, None] == jnp.arange(ctf_table.shape[0], dtype=jnp.int32)[None, :]
    ).astype(jnp.float32)
    ctf_rows = jnp.dot(onehot_rows, ctf_table, precision=lax.Precision.HIGHEST)
    weighted = (
        (chosen.astype(jnp.float32).reshape(count_local, CYCLES, ANG) * ctf_rows[:, :, None])
        .reshape(count_local, CYCLES * ANG)
        .astype(jnp.bfloat16)
    )
    ctf_sq = (ctf_rows * ctf_rows).astype(jnp.bfloat16)
    batch_rows, batch_sq = (
        lax.all_gather(weighted, "cls", axis=0, tiled=True),
        lax.all_gather(ctf_sq, "cls", axis=0, tiled=True),
    )
    batch_major = angle_major(batch_rows)
    doubled = jnp.concatenate([batch_major, batch_major], axis=0)
    refs = classes.astype(jnp.bfloat16)
    refs_major = angle_major(refs)
    cycle_power = jnp.sum(
        jnp.square(refs.astype(jnp.float32)).reshape(classes.shape[0], CYCLES, ANG), axis=2
    )
    block_len = math.gcd(ROT, 6)
    shift_blocks = shifts.reshape(ROT // block_len, block_len)
    scores = all_scores(doubled, refs_major, shift_blocks)
    norm_term = jnp.dot(
        batch_sq.astype(jnp.float32), cycle_power.T, precision=lax.Precision.HIGHEST
    )
    logits = scores - 0.5 * norm_term[None, :, :] + log_prior[None, None, :]
    local_top = jnp.max(logits, axis=(0, 2))
    local_total = jnp.sum(jnp.exp(logits - local_top[None, :, None]), axis=(0, 2))
    row_top, row_total = joined((local_top, local_total), "cls", merge_softmax)
    exp_terms = jnp.exp(logits - row_top[None, :, None])
    weights = (exp_terms / row_total[None, :, None]).astype(jnp.bfloat16)
    log_evidence = row_top + jnp.log(row_total)
    numerator = class_numerator(doubled, weights, shift_blocks)
    weight_sum = jnp.sum(weights.astype(jnp.float32), axis=0)
    denominator = lax.dot_general(
        weight_sum,
        batch_sq.astype(jnp.float32),
        (((0,), (0,)), ((), ())),
        precision=lax.Precision.HIGHEST,
    )
    numerator, denominator = lax.psum((numerator, denominator), "particle")
    spread = jnp.repeat(denominator, ANG, axis=1)
    updated = (1.0 - STEP_WEIGHT) * classes + STEP_WEIGHT * numerator / (spread + PRIOR_WEIGHT)
    return (updated, log_evidence)


def solution(mesh):
    in_specs = (
        P(("groups", "particle", "cls"), None),
        P(("groups", "particle", "cls")),
        P(("groups", "particle", "cls")),
        P("groups", None),
        P("groups"),
        P(("groups", "cls"), None),
        P(("groups", "cls")),
    )
    out_specs = (P(("groups", "cls"), None), P(("groups", "particle")))
    return jax.shard_map(
        on_device, mesh=mesh, in_specs=in_specs, out_specs=out_specs, check_vma=False
    )
```

profile of v0, /device:TPU:0, one launch (start us, length us, event | category | flops | bytes accessed | tf_op | source)
XLA Modules:
  0.0 359.3 jit_solution(5828321807343596698)
XLA Ops:
  10.6 10.0 %all_gather.18 = bf16[96,4096]{1,0:T(8,128)(2,1)S(1)} all-gather(bf16[24,4096]{1,0:T(8,128)(2,1)S(1)} %fusion.33), channel_id=1, replica_groups=mesh['groups'=2,'particle'=4,'cls'=4] {'cls'}, dimensions={0}, use_global_device_ids=true | all-gather | bytes 983040 | tf_op jit(solution)/shard_map/all_gather | solution.py:98
  28.6 76.0 %while.38 = (s32[]{:T(128)}, f32[6,6,96,100]{3,2,1,0:T(8,128)}, s32[6,6]{1,0:T(8,128)S(1)}, bf16[8192,96]{1,0:T(8,128)(2,1)S(1)}, bf16[4096,100]{1,0:T(8,128)(2,...) while((s32[]{:T(128)}, f32[6,6,96,100]{3,2,1,0:T(8,128)}, s32[6,6]{1,0:T(8,128)S(1)}, ...), condition=%wide.region_1.2_spmd, body=%wide.region_0.1_spmd.sunk | while | flops 471859200 | bytes 13468653 | solution.py:53
  104.5 5.2 %all_gather.19 = bf16[96,32]{1,0:T(8,128)(2,1)S(1)} all-gather(bf16[24,32]{1,0:T(8,128)(2,1)S(1)} %get-tuple-element.261), channel_id=1, replica_groups=mesh['groups'=2,'particle'=4,'cls'=4] {'cls'}, dimensions={0}, use_global_device_ids=true | all-gather | bytes 7680 | tf_op jit(solution)/shard_map/all_gather | solution.py:99
  117.8 6.8 %all-reduce.2 = (f32[384]{0:T(512)S(1)}, f32[384]{0:T(512)S(1)}) all-reduce(f32[384]{0:T(512)S(1)} %dynamic-update-slice, f32[384]{0:T(512)S(1)} %dynamic-update-slice.1), channel_id=2, replica_groups=mesh['groups'=2,'particle'=4,'cls'=4] {'cls'}, use_global_device_ids=true, to_apply=%add | all-reduce | flops 768 | bytes 6144
  126.9 138.9 %while.40 = (s32[]{:T(128)}, f32[4096,100]{0,1:T(8,128)}, s32[6,6]{1,0:T(8,128)S(1)}, bf16[8192,96]{1,0:T(8,128)(2,1)S(1)}, bf16[6,6,96,100]{3,2,1,0:T(8,128)(2,...) while((s32[]{:T(128)}, f32[4096,100]{0,1:T(8,128)}, ...), condition=%wide.region_8.9_spmd.clone, body=%wide.region_7.8_spmd.clone.sunk | while | flops 474726400 | bytes 26100356 | solution.py:71
  130.6 3.1 convolution_add_fusion.13
  138.1 3.1 convolution_add_fusion.15
  150.2 3.1 convolution_add_fusion.12
  154.0 3.1 convolution_add_fusion.13
  165.3 3.1 convolution_add_fusion.16
  169.1 3.1 convolution_add_fusion.17
  173.6 3.1 convolution_add_fusion.12
  177.4 3.1 convolution_add_fusion.13
  184.9 3.1 convolution_add_fusion.15
  197.0 3.2 convolution_add_fusion.12
  212.1 3.1 convolution_add_fusion.16
  220.4 3.2 convolution_add_fusion.12
  231.7 3.1 convolution_add_fusion.15
  243.8 3.2 convolution_add_fusion.12
  255.1 3.1 convolution_add_fusion.15
  262.7 3.1 convolution_add_fusion.17
  274.1 19.5 %psum.15 = f32[100,32]{0,1:T(8,128)S(1)} all-reduce(f32[100,32]{0,1:T(8,128)S(1)} %fusion.38), channel_id=1, replica_groups=mesh['groups'=2,'particle'=4,'cls'=4] {'particle'}, use_global_device_ids=true, to_apply=%region_11.12 | all-reduce | flops 3200 | bytes 25600 | tf_op jit(solution)/shard_map/psum | solution.py:129
  297.4 51.1 %all-reduce.5.cloned.1.call-done = f32[100,4096]{1,0:T(8,128)} async-done(((f32[100,4096]{1,0:T(8,128)}), f32[100,4096]{1,0:T(8,128)}) %all-reduce.5.cloned.1.call-update) | async-done | bytes 1638416 | tf_op jit(solution)/shard_map/psum | solution.py:129
  348.5 4.0 %divide_add_fusion = f32[100,4096]{1,0:T(8,128)} fusion(f32[100,4096]{1,0:T(8,128)} %bitcast.178, f32[100,4096]{1,0:T(8,128)} %all-reduce.5.cloned.1.call-done, f32[100,4096]{1,0:T(8,128)} %param.18), kind=kLoop, calls=%fused_computation.63 | loop fusion | flops 1638400 | bytes 6553600 | tf_op jit(solution)/shard_map/add | solution.py:131
  (145 shorter events, 151.6 us)
Async XLA Ops:
  7.2 2.4 copy-start
  7.2 341.3 %all-reduce.5.cloned.1.call-start = ((), (), s32[]{:S(2)}) async-start(), calls=%async_computation | async-start | bytes 3407872 | tf_op jit(solution)/shard_map/psum | solution.py:129
  22.2 1.5 copy-start.1
  25.2 3.3 copy-start.3
  109.7 2.5 copy-start.2
  112.2 3.9 %copy-start.4 = (u32[32]{0:T(128)S(1)}, u32[32]{0:T(128)}, u32[]{:S(2)}) copy-start(u32[32]{0:T(128)} %constant.119) | copy-start | bytes 388
Sparse Core Ops, SparseCore 0:
  274.1 74.3 all-reduce.4
where the time goes:
time: 362 us; the launch traced here: 359 us
  matrix products  152 us (42%)
  waiting for transfers between devices  51.1 us (14%)
  loops' own time  45.8 us (13%)
  blocking collectives  41.6 us (11%)
  local copies, waits for them, and re-layouts  39.3 us (11%)
  between operations  14.9 us (4%)
  other arithmetic  14.4 us (4%)
    dot_general x36, matrix products, advance(): jnp.dot(piece, weight_block[slot], preferred_element_type=jnp.float32)  112 us
    psum x1, waiting for transfers between devices, on_device(): numerator, denominator = lax.psum((numerator, denominator), 'particle')  51.1 us
    dot_general x36, matrix products, single(): lax.dot_general(piece, refs_major, (((0,), (0,)), ((), ())), preferred_el...  39 us
    another operation x1, loops' own time, class_numerator(): lax.scan(advance, start_value, (shift_blocks, weight_blocks))  23.1 us
    another operation x1, loops' own time, all_scores(): partial_value = lax.map(single, shift_blocks)  22.7 us
    psum x1, blocking collectives, on_device(): numerator, denominator = lax.psum((numerator, denominator), 'particle')  19.5 us
    unnamed x22, local copies, waits for them, and re-layouts  10.7 us
    dynamic_update_slice x6, local copies, waits for them, and re-layouts, all_scores(): partial_value = lax.map(single, shift_blocks)  10.1 us
  transfers between devices with their start and end apart: 1, of which 1 were waited for; matrix products, arithmetic and copies ran while one was open for 1% of the time, Pallas kernels for 0%

commit v1 on v0

--- a/solution.py
+++ b/solution.py
@@ -1,17 +1,311 @@
+import functools
 import math
 
 import jax
 import jax.numpy as jnp
 from jax import lax
+from jax.experimental import pallas as pl
+from jax.experimental.pallas import tpu as pltpu
 from jax.sharding import PartitionSpec as P
 
 CYCLES = 32
 ANG = 128
 ROT = 36
-
+PIX = CYCLES * ANG
 
 STEP_WEIGHT = 0.5
 PRIOR_WEIGHT = 1.0
+
+VMEM = pl.BlockSpec(memory_space=pltpu.VMEM)
+SMEM = pl.BlockSpec(memory_space=pltpu.SMEM)
+F32 = jnp.float32
+BF16 = jnp.bfloat16
+NT = (((1,), (1,)), ((), ()))
+TN = (((0,), (0,)), ((), ()))
+EXACT = lax.Precision.HIGHEST
+NEGATIVE = -1e30
+CHUNKS = 4
+
+
+def halves(total):
+    high = total // 2 // 8 * 8
+    width = -(-(total - high) // 8) * 8
+    return high, (high + width) // 2, width
+
+
+def params():
+    return pltpu.CompilerParams(vmem_limit_bytes=58 * 2**20)
+
+
+def weigh_kernel(picks, groups, pool, table, out):
+    count, stored, ngroup = picks.shape[1], pool.shape[0], table.shape[0]
+    pick_hot = (lax.broadcasted_iota(jnp.int32, (stored, count), 0) == picks[...]).astype(F32)
+    group_hot = (lax.broadcasted_iota(jnp.int32, (ngroup, count), 0) == groups[...]).astype(F32)
+    ctf = lax.dot_general(group_hot, table[...], TN, precision=EXACT, preferred_element_type=F32)
+    chosen = lax.dot_general(pick_hot.astype(BF16), pool[...], TN, preferred_element_type=F32)
+    for c in range(CYCLES):
+        here = slice(c * ANG, (c + 1) * ANG)
+        out[:, here] = (chosen[:, here] * ctf[:, c : c + 1]).astype(BF16)
+    out[:, PIX:] = jnp.concatenate(
+        [ctf * ctf, jnp.zeros((count, ANG - CYCLES), F32)], axis=1
+    ).astype(BF16)
+
+
+def weigh(picks, groups, pool, table):
+    count = picks.shape[0]
+    return pl.pallas_call(
+        weigh_kernel,
+        out_shape=jax.ShapeDtypeStruct((count, PIX + ANG), BF16),
+        in_specs=[VMEM] * 4,
+        out_specs=VMEM,
+        compiler_params=params(),
+        name="weigh",
+    )(picks.reshape(1, -1), groups.reshape(1, -1), pool, table)
+
+
+def rotate_kernel(width, place, shifts, classes, out, power):
+    total = classes.shape[0]
+    start, _, _ = halves(total)
+    upper = place[0] == 1
+    pad = jnp.zeros((width - (total - start), ANG), F32)
+    lane = lax.broadcasted_iota(jnp.int32, (width, ANG), 1)
+
+    def cycle(c, kept):
+        here = pl.ds(pl.multiple_of(c * ANG, ANG), ANG)
+        low = classes[0:width, here]
+        high = jnp.concatenate([classes[start:total, here], pad], axis=0)
+        refs = jnp.where(upper, high, low).astype(BF16).astype(F32)
+        for r in range(0, ROT, 2):
+            pair = [pltpu.roll(refs, shifts[r + j], 1) for j in range(2)]
+            out[r * width : (r + 2) * width, here] = jnp.concatenate(pair, axis=0).astype(BF16)
+        return jnp.where(lane == c, jnp.sum(refs * refs, axis=1, keepdims=True), kept)
+
+    power[...] = lax.fori_loop(0, CYCLES, cycle, jnp.zeros((width, ANG), F32))
+
+
+def rotate(width, place, shifts, classes):
+    return pl.pallas_call(
+        functools.partial(rotate_kernel, width),
+        out_shape=(
+            jax.ShapeDtypeStruct((ROT * width, PIX), BF16),
+            jax.ShapeDtypeStruct((width, ANG), F32),
+        ),
+        in_specs=[SMEM, SMEM, VMEM],
+        out_specs=(VMEM, VMEM),
+        compiler_params=params(),
+        name="rotate",
+    )(place, shifts, classes)
+
+
+def score_kernel(width, steps, place, turned, images, power, prior, logits, stats):
+    step = pl.program_id(0)
+    rows = turned.shape[0]
+    count = images.shape[0]
+    squares = images[:, PIX : PIX + ANG].astype(F32)
+    norm = lax.dot_general(power[...], squares, NT, precision=EXACT, preferred_element_type=F32)
+    total = prior.shape[0]
+    start, cut, _ = halves(total)
+    upper = place[0] == 1
+    row = lax.broadcasted_iota(jnp.int32, norm.shape, 0)
+    pad = jnp.zeros((width - (total - start), 1), F32)
+    high = jnp.concatenate([prior[start:total, :], pad], axis=0)
+    mine = (row >= jnp.where(upper, cut - start, 0)) & (row < jnp.where(upper, total - start, cut))
+    bias = jnp.where(mine, jnp.where(upper, high, prior[0:width, :]) - 0.5 * norm, NEGATIVE)
+    scores = lax.dot_general(turned[...], images[:, :PIX], NT, preferred_element_type=F32)
+    for j in range(rows // width):
+        block = pl.ds(pl.multiple_of(step * rows + j * width, 8), width)
+        logits[block, :] = scores[j * width : (j + 1) * width, :] + bias
+
+    @pl.when(step == steps - 1)
+    def _():
+        def highest(r, top):
+            return jnp.maximum(top, logits[pl.ds(pl.multiple_of(r * width, 8), width), :])
+
+        top = lax.fori_loop(1, ROT, highest, logits[0:width, :])
+        top = jnp.max(top, axis=0, keepdims=True)
+
+        def add(r, total):
+            return total + jnp.exp(logits[pl.ds(pl.multiple_of(r * width, 8), width), :] - top)
+
+        total = lax.fori_loop(0, ROT, add, jnp.zeros((width, count), F32))
+        stats[0:1, :] = top
+        stats[1:2, :] = jnp.sum(total, axis=0, keepdims=True)
+        stats[2:8, :] = jnp.zeros((6, count), F32)
+
+
+def score(width, place, turned, images, power, prior):
+    steps = 4
+    rows = ROT * width // steps
+    count = images.shape[0]
+    whole = lambda i: (0, 0)
+    return pl.pallas_call(
+        functools.partial(score_kernel, width, steps),
+        grid=(steps,),
+        out_shape=(
+            jax.ShapeDtypeStruct((ROT * width, count), F32),
+            jax.ShapeDtypeStruct((8, count), F32),
+        ),
+        in_specs=[
+            SMEM,
+            pl.BlockSpec((rows, PIX), lambda i: (i, 0)),
+            pl.BlockSpec(images.shape, whole),
+            pl.BlockSpec(power.shape, whole),
+            pl.BlockSpec(prior.shape, whole),
+        ],
+        out_specs=(
+            pl.BlockSpec((ROT * width, count), whole),
+            pl.BlockSpec((8, count), whole),
+        ),
+        compiler_params=params(),
+        name="score",
+    )(place, turned, images, power, prior)
+
+
+def weight_kernel(width, place, logits, squares, *refs):
+    stats, (weights, evidence, inverse, joined) = refs[:-4], refs[-4:]
+    count = logits.shape[1]
+    me = place[1]
+    for m, stat in enumerate(stats):
+        joined[pl.ds(pl.multiple_of((me ^ m) * 8, 8), 8), :] = stat[...]
+    tops = [joined[8 * j : 8 * j + 1, :] for j in range(len(stats))]
+    totals = [joined[8 * j + 1 : 8 * j + 2, :] for j in range(len(stats))]
+    top = functools.reduce(jnp.maximum, tops)
+    total = sum(t * jnp.exp(h - top) for h, t in zip(tops, totals))
+    evidence[...] = jnp.broadcast_to(top + jnp.log(total), (8, count))
+    scale = 1.0 / total
+
+    def single(q, summed):
+        values = []
+        for j in range(2):
+            block = pl.ds(pl.multiple_of((2 * q + j) * width, 8), width)
+            values.append((jnp.exp(logits[block, :] - top) * scale))
+        pair = jnp.concatenate(values, axis=0).astype(BF16)
+        weights[pl.ds(pl.multiple_of(2 * q * width, 16), 2 * width), :] = pair
+        pair = pair.astype(F32)
+        return summed + (pair[:width] + pair[width:])
+
+    summed = lax.fori_loop(0, ROT // 2, single, jnp.zeros((width, count), F32))
+    denominator = jnp.dot(
+        summed, squares[...].astype(F32), precision=EXACT, preferred_element_type=F32
+    )
+    inverse[...] = 1.0 / (denominator + PRIOR_WEIGHT)
+
+
+def weigh_classes(width, place, logits, images, stats):
+    count = logits.shape[1]
+    squares = pl.BlockSpec((count, ANG), lambda i: (0, PIX // ANG))
+    whole = lambda a: pl.BlockSpec(a.shape, lambda i: (0, 0))
+    outs = (
+        jax.ShapeDtypeStruct((ROT * width, count), BF16),
+        jax.ShapeDtypeStruct((8, count), F32),
+        jax.ShapeDtypeStruct((width, ANG), F32),
+    )
+    return pl.pallas_call(
+        functools.partial(weight_kernel, width),
+        grid=(1,),
+        out_shape=outs,
+        in_specs=[SMEM, whole(logits), squares] + [whole(s) for s in stats],
+        out_specs=tuple(whole(o) for o in outs),
+        scratch_shapes=[pltpu.VMEM((8 * len(stats), count), F32)],
+        compiler_params=params(),
+        name="weights",
+    )(place, logits, images, *stats)
+
+
+def update_kernel(width, first, span, shifts, weights, images, inverse, out, product):
+    step = pl.program_id(0)
+    product[...] = jnp.dot(weights[...], images[...], preferred_element_type=F32)
+    lane = lax.broadcasted_iota(jnp.int32, (width, ANG), 1)
+    for j in range(span):
+        here = slice(j * ANG, (j + 1) * ANG)
+        total = jnp.zeros((width, ANG), F32)
+        for r in range(ROT):
+            total = total + pltpu.roll(
+                product[r * width : (r + 1) * width, here], (ANG - shifts[r]) & (ANG - 1), 1
+            )
+        cycle = first + step * span + j
+        share = jnp.sum(jnp.where(lane == cycle, inverse[...], 0.0), axis=1, keepdims=True)
+        out[:, here] = (total * share).astype(BF16)
+
+
+def update(width, part, parts, shifts, weights, images, inverse):
+    count = images.shape[0]
+    cycles = CYCLES // parts
+    span = 2
+    steps = cycles // span
+    whole = lambda i: (0, 0)
+    return pl.pallas_call(
+        functools.partial(update_kernel, width, part * cycles, span),
+        grid=(steps,),
+        out_shape=jax.ShapeDtypeStruct((width, cycles * ANG), BF16),
+        in_specs=[
+            SMEM,
+            pl.BlockSpec(weights.shape, whole),
+            pl.BlockSpec((count, span * ANG), lambda i: (0, part * steps + i)),
+            pl.BlockSpec(inverse.shape, whole),
+        ],
+        out_specs=pl.BlockSpec((width, span * ANG), lambda i: (0, i)),
+        scratch_shapes=[pltpu.VMEM((ROT * width, span * ANG), F32)],
+        compiler_params=params(),
+        name="update",
+    )(shifts, weights, images, inverse)
+
+
+def blend_kernel(width, place, classes, *refs):
+    out = refs[-1]
+    parts = (len(refs) - 1) // 2
+    total = classes.shape[0]
+    start, cut, _ = halves(total)
+    upper = place[0] == 1
+    span = PIX // parts
+    row = lax.broadcasted_iota(jnp.int32, (total, span), 0)
+    for p in range(parts):
+        here = slice(p * span, (p + 1) * span)
+        mine, other = refs[p][...].astype(F32), refs[parts + p][...].astype(F32)
+        low = jnp.where(upper, other, mine)
+        high = jnp.where(upper, mine, other)
+        low_all = jnp.concatenate([low, jnp.zeros((total - width, span), F32)], axis=0)
+        high_all = jnp.concatenate([jnp.zeros((start, span), F32), high[: total - start]], axis=0)
+        step = jnp.where(row < cut, low_all, high_all)
+        out[:, here] = (1.0 - STEP_WEIGHT) * classes[:, here] + STEP_WEIGHT * step
+
+
+def blend(width, place, classes, mine, other):
+    return pl.pallas_call(
+        functools.partial(blend_kernel, width),
+        out_shape=jax.ShapeDtypeStruct(classes.shape, F32),
+        in_specs=[SMEM] + [VMEM] * (1 + 2 * len(mine)),
+        out_specs=VMEM,
+        compiler_params=params(),
+        name="blend",
+    )(place, classes, *mine, *other)
+
+
+def halved(pool, picks, groups, ctf_table, shifts, classes, log_prior):
+    _, _, width = halves(classes.shape[0])
+    axes = ("particle", "cls")
+    n_cls = lax.axis_size("cls")
+    z, cls = lax.axis_index("particle"), lax.axis_index("cls")
+    half = jnp.where((z == 0) | (z == 3), 0, 1).astype(jnp.int32)
+    place = jnp.stack([half, half * n_cls + cls, z]).astype(jnp.int32)
+    own = weigh(picks, groups, pool, ctf_table)
+    images = lax.all_gather(own, axes, axis=0, tiled=True)
+    turned, power = rotate(width, place, shifts, classes)
+    logits, stat = score(width, place, turned, images, power, log_prior.reshape(-1, 1))
+    n_all = lax.axis_size("particle") * n_cls
+    stats = [stat] + [
+        lax.ppermute(stat, axes, [(i, i ^ m) for i in range(n_all)]) for m in range(1, 2 * n_cls)
+    ]
+    weights, evidence, inverse = weigh_classes(width, place, logits, images, stats)
+    mine = [
+        update(width, p, CHUNKS, shifts, weights, images, inverse) for p in range(CHUNKS)
+    ]
+    swap = [(i, i ^ 1) for i in range(lax.axis_size("particle"))]
+    other = [lax.ppermute(u, "particle", swap) for u in mine]
+    updated = blend(width, place, classes, mine, other)
+    count = picks.shape[0] * n_cls
+    log_evidence = lax.dynamic_slice(evidence, (0, z * count), (1, count)).reshape(count)
+    return (updated, log_evidence)
 
 
 def joined(part, axis, combine):
@@ -81,7 +375,7 @@
     return (row_top, row_total)
 
 
-def on_device(pool, picks, groups, ctf_table, shifts, classes, log_prior):
+def whole_sum(pool, picks, groups, ctf_table, shifts, classes, log_prior):
     chosen = jnp.take(pool, picks, axis=0)
     count_local = chosen.shape[0]
     onehot_rows = (
@@ -143,6 +437,7 @@
         P(("groups", "cls")),
     )
     out_specs = (P(("groups", "cls"), None), P(("groups", "particle")))
+    quad = mesh.shape["particle"] == 4 and mesh.shape["cls"] == 4
     return jax.shard_map(
-        on_device, mesh=mesh, in_specs=in_specs, out_specs=out_specs, check_vma=False
-    )
+        halved if quad else whole_sum, mesh=mesh, in_specs=in_specs, out_specs=out_specs, check_vma=False
+    )

time: 362 us -> 132 us (0.36)
  matrix products: 152 us -> 0 us
  Pallas kernels: 0 us -> 64.2 us
  loops' own time: 45.8 us -> 0 us
  blocking collectives: 41.6 us -> 0 us
  local copies, waits for them, and re-layouts: 39.3 us -> 5.26 us
  waiting for transfers between devices: 51.1 us -> 36.4 us
  other arithmetic: 14.4 us -> 0.66 us
  starting transfers between devices: 0.04 us -> 10.6 us
    dot_general x75 -> x0, matrix products: 152 us -> none  [the longest x36 112 us: advance(): jnp.dot(piece, weight_block[slot], preferred_element_type=jnp.float32)]
    pallas_call x0 -> x9, Pallas kernels: none -> 64.2 us  [the longest x4 21.9 us: update(): pl.pallas_call(functools.partial(update_kernel, width, part * cycles, spa...]
    psum x1 -> x0, waiting for transfers between devices: 51.1 us -> none  [on_device(): numerator, denominator = lax.psum((numerator, denominator), 'particle')]
    another operation x3 -> x0, loops' own time: 45.8 us -> none  [the longest x1 23.1 us: class_numerator(): lax.scan(advance, start_value, (shift_blocks, weight_blocks))]
    all_gather x0 -> x1, waiting for transfers between devices: none -> 30.6 us  [halved(): images = lax.all_gather(own, axes, axis=0, tiled=True)]
    psum x1 -> x0, blocking collectives: 19.5 us -> none  [on_device(): numerator, denominator = lax.psum((numerator, denominator), 'particle')]
    all_gather x2 -> x0, blocking collectives: 15.2 us -> none  [the longest x1 10 us: on_device(): lax.all_gather(weighted, 'cls', axis=0, tiled=True)]
    ppermute x0 -> x11, starting transfers between devices: none -> 10.5 us  [the longest x7 6.47 us: halved(): lax.ppermute(stat, axes, [(i, i ^ m) for i in range(n_all)])]
  transfers between devices with their start and end apart: 1 -> 12, of which waited for: 1 -> 5; matrix products, arithmetic and copies ran while one was open for 1% -> 3% of each run, Pallas kernels for 0% -> 25%
where the time goes in v1:
time: 132 us; the launch traced here: 131 us
  Pallas kernels  64.2 us (49%)
  waiting for transfers between devices  36.4 us (28%)
  between operations  14.1 us (11%)
  starting transfers between devices  10.6 us (8%)
  local copies, waits for them, and re-layouts  5.26 us (4%)
    all_gather x1, waiting for transfers between devices, halved(): images = lax.all_gather(own, axes, axis=0, tiled=True)  30.6 us
    pallas_call x4, Pallas kernels, update(): pl.pallas_call(functools.partial(update_kernel, width, part * cycles, spa...  21.9 us
    pallas_call x1, Pallas kernels, score(): pl.pallas_call(functools.partial(score_kernel, width, steps), grid=(steps...  16.8 us
    pallas_call x1, Pallas kernels, rotate(): pl.pallas_call(functools.partial(rotate_kernel, width), out_shape=(jax.Sh...  15.9 us
    ppermute x7, starting transfers between devices, halved(): lax.ppermute(stat, axes, [(i, i ^ m) for i in range(n_all)])  6.47 us
    pallas_call x1, Pallas kernels, weigh_classes(): pl.pallas_call(functools.partial(weight_kernel, width), grid=(1,), out_sh...  4.18 us
    ppermute x4, starting transfers between devices, halved(): other = [lax.ppermute(u, 'particle', swap) for u in mine]  4.05 us
    ppermute x4, waiting for transfers between devices, halved(): other = [lax.ppermute(u, 'particle', swap) for u in mine]  3.41 us
  transfers between devices with their start and end apart: 12, of which 5 were waited for; matrix products, arithmetic and copies ran while one was open for 3% of the time, Pallas kernels for 25%

profile of v1, /device:TPU:0, one launch (start us, length us, event | category | flops | bytes accessed | tf_op | source)
XLA Modules:
  0.0 131.2 jit_solution(7754104836410624568)
XLA Ops:
  7.2 1.4 %copy.9.table = f32[64,32]{1,0:T(8,128)} copy(f32[64,32]{0,1:T(8,128)} %param.10) | data formatting | bytes 16384 | tf_op args[3]
  8.6 2.2 %weigh.1 = bf16[24,4224]{1,0:T(8,128)(2,1)} custom-call(s32[1,24]{1,0:T(1,128)} %bitcast.8, s32[1,24]{1,0:T(1,128)} %bitcast.9, bf16[48,4096]{1,0:T(8,128)(2,1)} %pool.1, f32[64,32]{1,0:T(8,128)} %copy.9.table), custom_call_target="tpu_custom_call" | custom-call | tf_op jit(solution)/shard_map/weigh/pallas_call | solution.py:56
  10.8 1.4 %copy.10.prior = f32[100,1]{1,0:T(8,128)} copy(f32[100,1]{0,1:T(1,128)} %bitcast.10) | data formatting | bytes 800 | tf_op jit(solution)/shard_map/reshape | solution.py:294
  12.2 0.7 pad_add_fusion.place
  12.9 15.9 %rotate.1 = (bf16[2016,4096]{1,0:T(8,128)(2,1)}, f32[56,128]{1,0:T(8,128)}) custom-call(s32[3]{0:T(128)} %pad_add_fusion.place, s32[36]{0:T(128)} %shifts.9, f32[100,4096]{1,0:T(8,128)} %classes.3), custom_call_target="tpu_custom_call" | custom-call | tf_op jit(solution)/shard_map/rotate/pallas_call | solution.py:87
  28.7 30.6 %all-gather.2.cloned.1.call-done.images.squares = bf16[384,4224]{1,0:T(8,128)(2,1)} async-done(((bf16[24,4224]{1,0:T(8,128)(2,1)}), bf16[384,4224]{1,0:T(8,128)(2,1)}) %all-gather.2.cloned.1.call-update) | async-done | bytes 3244048 | tf_op jit(solution)/shard_map/all_gather | solution.py:292
  59.4 16.8 %score.1 = (f32[2016,384]{1,0:T(8,128)}, f32[8,384]{1,0:T(8,128)}) custom-call(s32[3]{0:T(128)} %pad_add_fusion.place, bf16[2016,4096]{1,0:T(8,128)(2,1)} %get-tuple-element.9.turned, bf16[384,4224]{1,0:T(8,128)(2,1)} %all-gather.2.cloned.1.call-done.images.squares, f32[56,128]{1,0:T(8,128)} %get-tuple-element.10.power, f32[100,1]{1,0:T(8,128)} %copy.10.prior), custom_call_target="tpu_custom_call" | custom-call | tf_op jit(solution)/shard_map/score/pallas_call | solution.py:141
  76.1 1.7 %collective-permute-start.6 = (f32[8,384]{1,0:T(8,128)}, f32[8,384]{1,0:T(8,128)S(1)}, u32[]{:S(2)}, u32[]{:S(2)}) collective-permute-start(f32[8,384]{1,0:T(8,128)} %get-tuple-element.12.refs_0_), channel_id=1, source_target_pairs={{0,7},{1,6},{2,5},{3,4},{4,3},{5,2},{6,1},{7,0},{8,15},{9,14},{10,... | collective-permute-start | bytes 36872 | tf_op jit(solution)/shard_map/ppermute | solution.py:297
  77.9 1.0 collective-permute-start.5
  78.9 1.5 %collective-permute-start.4 = (f32[8,384]{1,0:T(8,128)}, f32[8,384]{1,0:T(8,128)S(1)}, u32[]{:S(2)}, u32[]{:S(2)}) collective-permute-start(f32[8,384]{1,0:T(8,128)} %get-tuple-element.12.refs_0_), channel_id=1, source_target_pairs={{0,5},{1,4},{2,7},{3,6},{4,1},{5,0},{6,3},{7,2},{8,13},{9,12},{10,... | collective-permute-start | bytes 36872 | tf_op jit(solution)/shard_map/ppermute | solution.py:297
  81.1 1.5 %collective-permute-start.1 = (f32[8,384]{1,0:T(8,128)}, f32[8,384]{1,0:T(8,128)S(1)}, u32[]{:S(2)}, u32[]{:S(2)}) collective-permute-start(f32[8,384]{1,0:T(8,128)} %get-tuple-element.12.refs_0_), channel_id=1, source_target_pairs={{0,2},{1,3},{2,0},{3,1},{4,6},{5,7},{6,4},{7,5},{8,10},{9,11},{10,... | collective-permute-start | bytes 36872 | tf_op jit(solution)/shard_map/ppermute | solution.py:297
  82.8 1.6 %collective-permute-done.3.refs_4_ = f32[8,384]{1,0:T(8,128)S(1)} collective-permute-done((f32[8,384]{1,0:T(8,128)}, f32[8,384]{1,0:T(8,128)S(1)}, u32[]{:S(2)}, u32[]{:S(2)}) %collective-permute-start.3) | collective-permute-done | bytes 12320 | tf_op jit(solution)/shard_map/ppermute | solution.py:297
  84.3 0.7 collective-permute-done.1.refs_2_
  85.6 4.2 %weights.1 = (bf16[2016,384]{1,0:T(8,128)(2,1)}, f32[8,384]{1,0:T(8,128)}, f32[56,128]{1,0:T(8,128)}) custom-call(s32[3]{0:T(128)} %pad_add_fusion.place, f32[2016,384]{1,0:T(8,128)} %get-tuple-element.11.logits, bf16[384,4224]{1,0:T(8,128)(2,1)} %all-gather.2.cloned.1.call-done.images.squares, f32[8,384]{1,0:T(8,128)} %get-tuple-element.12.refs_0_, ...), custom_call_target="tpu_custom_call" | custom-call | tf_op jit(solution)/shard_map/weights/pallas_call | solution.py:203
  89.8 5.5 %update.4.refs_0_ = bf16[56,1024]{1,0:T(8,128)(2,1)} custom-call(s32[36]{0:T(128)} %shifts.9, bf16[2016,384]{1,0:T(8,128)(2,1)} %get-tuple-element.13.weights, bf16[384,4224]{1,0:T(8,128)(2,1)} %all-gather.2.cloned.1.call-done.images.squares, f32[56,128]{1,0:T(8,128)} %get-tuple-element.14.inverse), custom_call_target="tpu_custom_call" | custom-call | tf_op jit(solution)/shard_map/update/pallas_call | solution.py:237
  95.3 1.7 %collective-permute-start.7 = (bf16[56,1024]{1,0:T(8,128)(2,1)}, bf16[56,1024]{1,0:T(8,128)(2,1)S(1)}, u32[]{:S(2)}, u32[]{:S(2)}) collective-permute-start(bf16[56,1024]{1,0:T(8,128)(2,1)} %update.4.refs_0_), channel_id=1, source_target_pairs={{0,4},{4,0},{8,12},{12,8},{1,5},{5,1},{9,13},{13,9},{2,6},{6,2},{1... | collective-permute-start | bytes 344072 | tf_op jit(solution)/shard_map/ppermute | solution.py:304
  97.0 5.5 %update.5.refs_1_ = bf16[56,1024]{1,0:T(8,128)(2,1)} custom-call(s32[36]{0:T(128)} %shifts.9, bf16[2016,384]{1,0:T(8,128)(2,1)} %get-tuple-element.13.weights, bf16[384,4224]{1,0:T(8,128)(2,1)} %all-gather.2.cloned.1.call-done.images.squares, f32[56,128]{1,0:T(8,128)} %get-tuple-element.14.inverse), custom_call_target="tpu_custom_call" | custom-call | tf_op jit(solution)/shard_map/update/pallas_call | solution.py:237
  102.8 5.5 %update.6.refs_2_ = bf16[56,1024]{1,0:T(8,128)(2,1)} custom-call(s32[36]{0:T(128)} %shifts.9, bf16[2016,384]{1,0:T(8,128)(2,1)} %get-tuple-element.13.weights, bf16[384,4224]{1,0:T(8,128)(2,1)} %all-gather.2.cloned.1.call-done.images.squares, f32[56,128]{1,0:T(8,128)} %get-tuple-element.14.inverse), custom_call_target="tpu_custom_call" | custom-call | tf_op jit(solution)/shard_map/update/pallas_call | solution.py:237
  108.2 1.7 %collective-permute-start.9 = (bf16[56,1024]{1,0:T(8,128)(2,1)}, bf16[56,1024]{1,0:T(8,128)(2,1)S(1)}, u32[]{:S(2)}, u32[]{:S(2)}) collective-permute-start(bf16[56,1024]{1,0:T(8,128)(2,1)} %update.6.refs_2_), channel_id=1, source_target_pairs={{0,4},{4,0},{8,12},{12,8},{1,5},{5,1},{9,13},{13,9},{2,6},{6,2},{1... | collective-permute-start | bytes 344072 | tf_op jit(solution)/shard_map/ppermute | solution.py:304
  110.0 5.5 %update.7.refs_3_ = bf16[56,1024]{1,0:T(8,128)(2,1)} custom-call(s32[36]{0:T(128)} %shifts.9, bf16[2016,384]{1,0:T(8,128)(2,1)} %get-tuple-element.13.weights, bf16[384,4224]{1,0:T(8,128)(2,1)} %all-gather.2.cloned.1.call-done.images.squares, f32[56,128]{1,0:T(8,128)} %get-tuple-element.14.inverse), custom_call_target="tpu_custom_call" | custom-call | tf_op jit(solution)/shard_map/update/pallas_call | solution.py:237
  115.7 1.3 dynamic-slice_bitcast_fusion
  117.0 3.4 %collective-permute-done.10.refs_7_ = bf16[56,1024]{1,0:T(8,128)(2,1)S(1)} collective-permute-done((bf16[56,1024]{1,0:T(8,128)(2,1)}, bf16[56,1024]{1,0:T(8,128)(2,1)S(1)}, u32[]{:S(2)}, u32[]{:S(2)}) %collective-permute-start.10) | collective-permute-done | bytes 114720 | tf_op jit(solution)/shard_map/ppermute | solution.py:304
  120.5 0.6 copy-done.3
  121.1 3.3 %blend.1 = f32[100,4096]{1,0:T(8,128)} custom-call(s32[3]{0:T(128)} %pad_add_fusion.place, f32[100,4096]{1,0:T(8,128)} %classes.3, bf16[56,1024]{1,0:T(8,128)(2,1)} %update.4.refs_0_, bf16[56,1024]{1,0:T(8,128)(2,1)} %update.5.refs_1_, bf16[56,1024]{1,0:T(8,128)(2,1)} %update.6.refs_2_, bf16[56,1024]{1,0:T(8,128)(2,1)} %update.7.refs_3_, ...), custom_call_target="tpu_custom_call" | custom-call | tf_op jit(solution)/shard_map/blend/pallas_call | solution.py:274
  (36 shorter events, 2.1 us)
Async XLA Ops:
  7.2 52.2 %all-gather.2.cloned.1.call-start = ((), (), s32[]{:S(2)}) async-start(), calls=%async_computation | async-start | bytes 3446784 | tf_op jit(solution)/shard_map/all_gather | solution.py:292
  76.1 5.0 %collective-permute-start.6 = (f32[8,384]{1,0:T(8,128)}, f32[8,384]{1,0:T(8,128)S(1)}, u32[]{:S(2)}, u32[]{:S(2)}) collective-permute-start(f32[8,384]{1,0:T(8,128)} %get-tuple-element.12.refs_0_), channel_id=1, source_target_pairs={{0,7},{1,6},{2,5},{3,4},{4,3},{5,2},{6,1},{7,0},{8,15},{9,14},{10,... | collective-permute-start | bytes 36872 | tf_op jit(solution)/shard_map/ppermute | solution.py:297
  77.9 4.8 %collective-permute-start.5 = (f32[8,384]{1,0:T(8,128)}, f32[8,384]{1,0:T(8,128)S(1)}, u32[]{:S(2)}, u32[]{:S(2)}) collective-permute-start(f32[8,384]{1,0:T(8,128)} %get-tuple-element.12.refs_0_), channel_id=1, source_target_pairs={{0,6},{1,7},{2,4},{3,5},{4,2},{5,3},{6,0},{7,1},{8,14},{9,15},{10,... | collective-permute-start | bytes 36872 | tf_op jit(solution)/shard_map/ppermute | solution.py:297
  78.9 3.8 %collective-permute-start.4 = (f32[8,384]{1,0:T(8,128)}, f32[8,384]{1,0:T(8,128)S(1)}, u32[]{:S(2)}, u32[]{:S(2)}) collective-permute-start(f32[8,384]{1,0:T(8,128)} %get-tuple-element.12.refs_0_), channel_id=1, source_target_pairs={{0,5},{1,4},{2,7},{3,6},{4,1},{5,0},{6,3},{7,2},{8,13},{9,12},{10,... | collective-permute-start | bytes 36872 | tf_op jit(solution)/shard_map/ppermute | solution.py:297
  80.4 3.9 %collective-permute-start.3 = (f32[8,384]{1,0:T(8,128)}, f32[8,384]{1,0:T(8,128)S(1)}, u32[]{:S(2)}, u32[]{:S(2)}) collective-permute-start(f32[8,384]{1,0:T(8,128)} %get-tuple-element.12.refs_0_), channel_id=1, source_target_pairs={{0,4},{1,5},{2,6},{3,7},{4,0},{5,1},{6,2},{7,3},{8,12},{9,13},{10,... | collective-permute-start | bytes 36872 | tf_op jit(solution)/shard_map/ppermute | solution.py:297
  80.9 3.5 %collective-permute-start.2 = (f32[8,384]{1,0:T(8,128)}, f32[8,384]{1,0:T(8,128)S(1)}, u32[]{:S(2)}, u32[]{:S(2)}) collective-permute-start(f32[8,384]{1,0:T(8,128)} %get-tuple-element.12.refs_0_), channel_id=1, source_target_pairs={{0,3},{1,2},{2,1},{3,0},{4,7},{5,6},{6,5},{7,4},{8,11},{9,10},{10,... | collective-permute-start | bytes 36872 | tf_op jit(solution)/shard_map/ppermute | solution.py:297
  81.1 3.9 %copy-start.4 = (f32[8,384]{1,0:T(8,128)}, f32[8,384]{1,0:T(8,128)S(1)}, u32[]{:S(2)}) copy-start(f32[8,384]{1,0:T(8,128)S(1)} %collective-permute-done.6.refs_7_) | copy-start | bytes 36868
  81.1 3.9 %collective-permute-start.1 = (f32[8,384]{1,0:T(8,128)}, f32[8,384]{1,0:T(8,128)S(1)}, u32[]{:S(2)}, u32[]{:S(2)}) collective-permute-start(f32[8,384]{1,0:T(8,128)} %get-tuple-element.12.refs_0_), channel_id=1, source_target_pairs={{0,2},{1,3},{2,0},{3,1},{4,6},{5,7},{6,4},{7,5},{8,10},{9,11},{10,... | collective-permute-start | bytes 36872 | tf_op jit(solution)/shard_map/ppermute | solution.py:297
  82.7 2.3 %copy-start.5 = (f32[8,384]{1,0:T(8,128)}, f32[8,384]{1,0:T(8,128)S(1)}, u32[]{:S(2)}) copy-start(f32[8,384]{1,0:T(8,128)S(1)} %collective-permute-done.5.refs_6_) | copy-start | bytes 36868
  82.7 2.3 %collective-permute-start = (f32[8,384]{1,0:T(8,128)}, f32[8,384]{1,0:T(8,128)S(1)}, u32[]{:S(2)}, u32[]{:S(2)}) collective-permute-start(f32[8,384]{1,0:T(8,128)} %get-tuple-element.12.refs_0_), channel_id=1, source_target_pairs={{0,1},{1,0},{2,3},{3,2},{4,5},{5,4},{6,7},{7,6},{8,9},{9,8},{10,11... | collective-permute-start | bytes 36872 | tf_op jit(solution)/shard_map/ppermute | solution.py:297
  82.7 2.3 %copy-start.6 = (f32[8,384]{1,0:T(8,128)}, f32[8,384]{1,0:T(8,128)S(1)}, u32[]{:S(2)}) copy-start(f32[8,384]{1,0:T(8,128)S(1)} %collective-permute-done.4.refs_5_) | copy-start | bytes 36868
  84.3 0.7 copy-start.7
  84.3 0.7 copy-start.8
  85.0 0.6 copy-start.9
  85.0 0.6 copy-start.10
  95.3 21.7 %collective-permute-start.7 = (bf16[56,1024]{1,0:T(8,128)(2,1)}, bf16[56,1024]{1,0:T(8,128)(2,1)S(1)}, u32[]{:S(2)}, u32[]{:S(2)}) collective-permute-start(bf16[56,1024]{1,0:T(8,128)(2,1)} %update.4.refs_0_), channel_id=1, source_target_pairs={{0,4},{4,0},{8,12},{12,8},{1,5},{5,1},{9,13},{13,9},{2,6},{6,2},{1... | collective-permute-start | bytes 344072 | tf_op jit(solution)/shard_map/ppermute | solution.py:304
  102.5 14.5 %collective-permute-start.8 = (bf16[56,1024]{1,0:T(8,128)(2,1)}, bf16[56,1024]{1,0:T(8,128)(2,1)S(1)}, u32[]{:S(2)}, u32[]{:S(2)}) collective-permute-start(bf16[56,1024]{1,0:T(8,128)(2,1)} %update.5.refs_1_), channel_id=1, source_target_pairs={{0,4},{4,0},{8,12},{12,8},{1,5},{5,1},{9,13},{13,9},{2,6},{6,2},{1... | collective-permute-start | bytes 344072 | tf_op jit(solution)/shard_map/ppermute | solution.py:304
  108.2 8.8 %collective-permute-start.9 = (bf16[56,1024]{1,0:T(8,128)(2,1)}, bf16[56,1024]{1,0:T(8,128)(2,1)S(1)}, u32[]{:S(2)}, u32[]{:S(2)}) collective-permute-start(bf16[56,1024]{1,0:T(8,128)(2,1)} %update.6.refs_2_), channel_id=1, source_target_pairs={{0,4},{4,0},{8,12},{12,8},{1,5},{5,1},{9,13},{13,9},{2,6},{6,2},{1... | collective-permute-start | bytes 344072 | tf_op jit(solution)/shard_map/ppermute | solution.py:304
  115.4 5.0 %collective-permute-start.10 = (bf16[56,1024]{1,0:T(8,128)(2,1)}, bf16[56,1024]{1,0:T(8,128)(2,1)S(1)}, u32[]{:S(2)}, u32[]{:S(2)}) collective-permute-start(bf16[56,1024]{1,0:T(8,128)(2,1)} %update.7.refs_3_), channel_id=1, source_target_pairs={{0,4},{4,0},{8,12},{12,8},{1,5},{5,1},{9,13},{13,9},{2,6},{6,2},{1... | collective-permute-start | bytes 344072 | tf_op jit(solution)/shard_map/ppermute | solution.py:304
  117.0 3.4 %copy-start = (bf16[56,1024]{1,0:T(8,128)(2,1)}, bf16[56,1024]{1,0:T(8,128)(2,1)S(1)}, u32[]{:S(2)}) copy-start(bf16[56,1024]{1,0:T(8,128)(2,1)S(1)} %collective-permute-done.7.refs_4_) | copy-start | bytes 344068
  117.0 3.4 %copy-start.1 = (bf16[56,1024]{1,0:T(8,128)(2,1)}, bf16[56,1024]{1,0:T(8,128)(2,1)S(1)}, u32[]{:S(2)}) copy-start(bf16[56,1024]{1,0:T(8,128)(2,1)S(1)} %collective-permute-done.8.refs_5_) | copy-start | bytes 344068
  117.0 3.4 %copy-start.2 = (bf16[56,1024]{1,0:T(8,128)(2,1)}, bf16[56,1024]{1,0:T(8,128)(2,1)S(1)}, u32[]{:S(2)}) copy-start(bf16[56,1024]{1,0:T(8,128)(2,1)S(1)} %collective-permute-done.9.refs_6_) | copy-start | bytes 344068
  120.5 0.6 copy-start.3
Sparse Core Ops, SparseCore 0:
  11.0 48.3 all-gather.1

commit v2 on v0

--- a/solution.py
+++ b/solution.py
@@ -1,17 +1,362 @@
+import functools
 import math
 
 import jax
 import jax.numpy as jnp
 from jax import lax
+from jax.experimental import pallas as pl
+from jax.experimental.pallas import tpu as pltpu
 from jax.sharding import PartitionSpec as P
 
 CYCLES = 32
 ANG = 128
 ROT = 36
-
+PIX = CYCLES * ANG
 
 STEP_WEIGHT = 0.5
 PRIOR_WEIGHT = 1.0
+
+VMEM = pl.BlockSpec(memory_space=pltpu.VMEM)
+ANY = pl.BlockSpec(memory_space=pl.ANY)
+SMEM = pl.BlockSpec(memory_space=pltpu.SMEM)
+F32 = jnp.float32
+BF16 = jnp.bfloat16
+NT = (((1,), (1,)), ((), ()))
+TN = (((0,), (0,)), ((), ()))
+EXACT = lax.Precision.HIGHEST
+NEGATIVE = -1e30
+CHUNKS = (8, 8, 8, 8)
+LARGE = 48
+
+
+def later(kernel, count):
+    return lambda *refs: kernel(*refs[count:])
+
+
+def halves(total):
+    start = total // 2 // 8 * 8
+    rows = -(-(total - start) // 8) * 8
+    return start, (start + rows) // 2, rows, -(-rows // 16) * 16
+
+
+def cost(flops, moved):
+    return pl.CostEstimate(flops=int(flops), bytes_accessed=int(moved), transcendentals=0)
+
+
+def params(mib=8):
+    return pltpu.CompilerParams(vmem_limit_bytes=mib * 2**20)
+
+
+def weigh_kernel(picks, groups, pool, table, out):
+    count, stored, ngroup = picks.shape[1], pool.shape[0], table.shape[1]
+    pick_hot = (lax.broadcasted_iota(jnp.int32, (stored, count), 0) == picks[...]).astype(F32)
+    group_hot = (lax.broadcasted_iota(jnp.int32, (ngroup, count), 0) == groups[...]).astype(F32)
+    ctf = jnp.dot(table[...], group_hot, precision=EXACT, preferred_element_type=F32).T
+    chosen = lax.dot_general(pick_hot.astype(BF16), pool[...], TN, preferred_element_type=F32)
+    for c in range(CYCLES):
+        here = slice(c * ANG, (c + 1) * ANG)
+        out[:, here] = (chosen[:, here] * ctf[:, c : c + 1]).astype(BF16)
+    out[:, PIX:] = jnp.concatenate(
+        [ctf * ctf, jnp.zeros((count, ANG - CYCLES), F32)], axis=1
+    ).astype(BF16)
+
+
+def weigh(picks, groups, pool, table):
+    count = picks.shape[0]
+    return pl.pallas_call(
+        weigh_kernel,
+        out_shape=jax.ShapeDtypeStruct((count, PIX + ANG), BF16),
+        in_specs=[VMEM] * 4,
+        out_specs=VMEM,
+        compiler_params=params(),
+        cost_estimate=cost(2 * count * 48 * PIX, 2**20),
+        name="weigh",
+    )(picks.reshape(1, -1), groups.reshape(1, -1), pool, table.T)
+
+
+def score_kernel(width, groups, span, place, shifts, prior, classes, same, across, *refs):
+    (logits, stats, images), (halved, bias, *turned) = refs[:3], refs[3:]
+    one = same.shape[0]
+    count = images.shape[0]
+    core = place[2]
+    upper = place[0] == 1
+    total = classes.shape[0]
+    start, cut, _, _ = halves(total)
+    images[pl.ds(pl.multiple_of(core * one, 16), one), :] = same[...]
+    images[pl.ds(pl.multiple_of((1 - core) * one, 16), one), :] = across[...]
+
+    pad = jnp.zeros((width - (total - start), ANG), F32)
+    lane = lax.broadcasted_iota(jnp.int32, (width, ANG), 1)
+    power = jnp.zeros((width, ANG), F32)
+    for c in range(CYCLES):
+        here = slice(c * ANG, (c + 1) * ANG)
+        high = jnp.concatenate([classes[start:total, here], pad], axis=0)
+        mine = jnp.where(upper, high, classes[0:width, here]).astype(BF16)
+        halved[:, here] = mine
+        wide = mine.astype(F32)
+        power = jnp.where(lane == c, jnp.sum(wide * wide, axis=1, keepdims=True), power)
+
+    squares = images[:, PIX:].astype(F32)
+    norm = lax.dot_general(power, squares, NT, precision=EXACT, preferred_element_type=F32)
+    column = jnp.broadcast_to(prior[...], (8, ANG)).T[:, 0:1]
+    high = jnp.concatenate([column[start:total, :], pad[:, 0:1]], axis=0)
+    value = jnp.where(upper, high, column[0:width, :]) - 0.5 * norm
+    row = lax.broadcasted_iota(jnp.int32, norm.shape, 0)
+    mine = (row >= jnp.where(upper, cut - start, 0)) & (
+        row < jnp.where(upper, total - start, cut)
+    )
+    bias[...] = jnp.where(mine, value, NEGATIVE)
+
+    each = ROT // groups
+    top = jnp.full((width, count), NEGATIVE, F32)
+    for g in range(groups):
+        scores = None
+        for q in range(CYCLES // span):
+            block = turned[q % 2]
+            for c in range(span):
+                cycle = q * span + c
+                image = halved[:, cycle * ANG : (cycle + 1) * ANG]
+                for r in range(each):
+                    block[r * width : (r + 1) * width, c * ANG : (c + 1) * ANG] = pltpu.roll(
+                        image, shifts[g * each + r], 1
+                    )
+            part = lax.dot_general(
+                block[...],
+                images[:, q * span * ANG : (q + 1) * span * ANG],
+                NT,
+                preferred_element_type=F32,
+            )
+            scores = part if scores is None else scores + part
+        for r in range(each):
+            value = scores[r * width : (r + 1) * width, :] + bias[...]
+            logits[(g * each + r) * width : (g * each + r + 1) * width, :] = value
+            top = jnp.maximum(top, value)
+    top = jnp.max(top, axis=0, keepdims=True)
+
+    def add(r, total):
+        return total + jnp.exp(logits[pl.ds(pl.multiple_of(r * width, 8), width), :] - top)
+
+    total = lax.fori_loop(0, ROT, add, jnp.zeros((width, count), F32))
+    stats[0:1, :] = top
+    stats[1:2, :] = jnp.sum(total, axis=0, keepdims=True)
+    stats[2:, :] = jnp.zeros((6, count), F32)
+
+
+def score(width, place, shifts, prior, classes, same, across):
+    groups, span = 4, 4
+    one, full = same.shape
+    count = 2 * one
+    outs = (
+        jax.ShapeDtypeStruct((ROT * width, count), F32),
+        jax.ShapeDtypeStruct((8, count), F32),
+        jax.ShapeDtypeStruct((count, full), BF16),
+    )
+    return pl.pallas_call(
+        functools.partial(score_kernel, width, groups, span),
+        out_shape=outs,
+        in_specs=[SMEM, SMEM] + [VMEM] * 4,
+        out_specs=(VMEM,) * 3,
+        scratch_shapes=[pltpu.VMEM((width, PIX), BF16), pltpu.VMEM((width, count), F32)]
+        + [pltpu.VMEM((ROT // groups * width, span * ANG), BF16)] * 2,
+        compiler_params=params(LARGE),
+        cost_estimate=cost(10 * 2**30, 20 * 2**20),
+        name="score",
+    )(place, shifts, prior, classes, same, across)
+
+
+def weight_kernel(width, place, logits, squares, *refs):
+    stats, (weights, evidence, denominator, joined) = refs[:-4], refs[-4:]
+    count = logits.shape[1]
+    for m, stat in enumerate(stats):
+        joined[pl.ds(pl.multiple_of((place[1] ^ m) * 8, 8), 8), :] = stat[...]
+    tops = [joined[8 * j : 8 * j + 1, :] for j in range(len(stats))]
+    totals = [joined[8 * j + 1 : 8 * j + 2, :] for j in range(len(stats))]
+    top = functools.reduce(jnp.maximum, tops)
+    total = sum(t * jnp.exp(h - top) for h, t in zip(tops, totals))
+    evidence[...] = jnp.broadcast_to(top + jnp.log(total), (8, count))
+    scale = 1.0 / total
+
+    def single(r, summed):
+        block = pl.ds(pl.multiple_of(r * width, 16), width)
+        value = (jnp.exp(logits[block, :] - top) * scale).astype(BF16)
+        weights[block, :] = value
+        return summed + value.astype(F32)
+
+    summed = lax.fori_loop(0, ROT, single, jnp.zeros((width, count), F32))
+    denominator[...] = jnp.dot(
+        summed, squares[...].astype(F32), precision=EXACT, preferred_element_type=F32
+    )
+
+
+def weigh_classes(width, place, logits, images, stats):
+    count = logits.shape[1]
+    squares = pl.BlockSpec((count, ANG), lambda i: (0, PIX // ANG))
+    whole = lambda a: pl.BlockSpec(a.shape, lambda i: (0, 0))
+    outs = (
+        jax.ShapeDtypeStruct((ROT * width, count), BF16),
+        jax.ShapeDtypeStruct((8, count), F32),
+        jax.ShapeDtypeStruct((width, ANG), F32),
+    )
+    return pl.pallas_call(
+        functools.partial(weight_kernel, width),
+        grid=(1,),
+        out_shape=outs,
+        in_specs=[SMEM, whole(logits), squares] + [whole(s) for s in stats],
+        out_specs=tuple(whole(o) for o in outs),
+        scratch_shapes=[pltpu.VMEM((8 * len(stats), count), F32)],
+        compiler_params=params(LARGE),
+        cost_estimate=cost(4 * 2**30, 8 * 2**20),
+        name="weights",
+    )(place, logits, images, *stats)
+
+
+def update_kernel(width, rows, span, shifts, weights, images, out, product):
+    product[...] = jnp.dot(weights[...], images[...], preferred_element_type=F32).astype(BF16)
+    for j in range(span):
+        here = slice(j * ANG, (j + 1) * ANG)
+        total = jnp.zeros((width, ANG), F32)
+        for r in range(ROT):
+            back = (ANG - shifts[r]) & (ANG - 1)
+            turned = pltpu.roll(product[r * width : (r + 1) * width, here], back, 1)
+            total = total + turned.astype(F32)
+        out[:, here] = total[:rows].astype(BF16)
+
+
+def update(width, rows, first, cycles, shifts, weights, images, after):
+    count = images.shape[0]
+    span = math.gcd(cycles, 8)
+    base = first // span
+    return pl.pallas_call(
+        later(functools.partial(update_kernel, width, rows, span), len(after)),
+        grid=(cycles // span,),
+        out_shape=jax.ShapeDtypeStruct((rows, cycles * ANG), BF16),
+        in_specs=[ANY] * len(after)
+        + [
+            SMEM,
+            pl.BlockSpec(weights.shape, lambda i: (0, 0)),
+            pl.BlockSpec((count, span * ANG), lambda i: (0, base + i)),
+        ],
+        out_specs=pl.BlockSpec((rows, span * ANG), lambda i: (0, i)),
+        scratch_shapes=[pltpu.VMEM((ROT * width, span * ANG), BF16)],
+        compiler_params=params(LARGE),
+        cost_estimate=cost(3 * 2**30, 4 * 2**20),
+        name="update",
+    )(*after, shifts, weights, images)
+
+
+def divide_kernel(first, one, two, one_below, two_below, out):
+    rows, span = out.shape
+    below = one_below[0:rows, :] + two_below[0:rows, :]
+    share = 1.0 / (below + PRIOR_WEIGHT)
+    lane = lax.broadcasted_iota(jnp.int32, share.shape, 1)
+    for j in range(span // ANG):
+        here = slice(j * ANG, (j + 1) * ANG)
+        total = one[:, here].astype(F32) + two[:, here].astype(F32)
+        cycle = jnp.where(lane == first + j, share, 0.0)
+        out[:, here] = (total * jnp.sum(cycle, axis=1, keepdims=True)).astype(BF16)
+
+
+def divide(first, one, two, one_below, two_below):
+    return pl.pallas_call(
+        functools.partial(divide_kernel, first),
+        out_shape=jax.ShapeDtypeStruct(one.shape, BF16),
+        in_specs=[VMEM] * 4,
+        out_specs=VMEM,
+        compiler_params=params(8),
+        cost_estimate=cost(2**30, 2**20),
+        name="divide",
+    )(one, two, one_below, two_below)
+
+
+def blend_kernel(place, classes, mine, other, *refs):
+    out = refs[-1]
+    total, span = classes.shape
+    width = mine.shape[0]
+    start, cut, _, _ = halves(total)
+    upper = place[0] == 1
+    row = lax.broadcasted_iota(jnp.int32, (total, span), 0)
+    first, second = mine[...].astype(F32), other[...].astype(F32)
+    low = jnp.where(upper, second, first)
+    high = jnp.where(upper, first, second)
+    low_all = jnp.concatenate([low, jnp.zeros((total - width, span), F32)], axis=0)
+    high_all = jnp.concatenate([jnp.zeros((start, span), F32), high[: total - start]], axis=0)
+    step = jnp.where(row < cut, low_all, high_all)
+    out[...] = (1.0 - STEP_WEIGHT) * classes[...] + STEP_WEIGHT * step
+
+
+def blend(first, place, classes, mine, other, before):
+    span = mine.shape[1]
+    rows = pl.BlockSpec((classes.shape[0], span), lambda i: (0, first * ANG // span))
+    update = pl.BlockSpec(mine.shape, lambda i: (0, 0))
+    return pl.pallas_call(
+        blend_kernel,
+        grid=(1,),
+        out_shape=jax.ShapeDtypeStruct(classes.shape, F32),
+        in_specs=[SMEM, rows, update, update] + [ANY] * len(before),
+        out_specs=rows,
+        input_output_aliases={4: 0} if before else {},
+        compiler_params=params(),
+        cost_estimate=cost(2**30, 2**20),
+        name="blend",
+    )(place, classes, mine, other, *before)
+
+
+def halved(pool, picks, groups, ctf_table, shifts, classes, log_prior):
+    total = classes.shape[0]
+    _, _, rows, width = halves(total)
+    axes = ("particle", "cls")
+    z, cls = lax.axis_index("particle"), lax.axis_index("cls")
+    chip, core = cls // 2, cls % 2
+    half = jnp.where((z == 1) | (z == 2), 1, 0)
+    place = jnp.stack([half, half * 2 + chip, core]).astype(jnp.int32)
+    prior = jnp.pad(log_prior, (0, ANG - total)).reshape(1, ANG)
+
+    def swap(a, mask):
+        return lax.ppermute(a, axes, [(i, i ^ mask) for i in range(16)])
+
+    CORE, CHIP, NEXT, SAME = 1, 2, 4, 12
+
+    own = weigh(picks, groups, pool, ctf_table)
+    beside = swap(own, NEXT)
+    own_x = swap(own, CHIP)
+    beside_x = swap(beside, CHIP)
+    pairs = [
+        (jnp.where(chip == 1, x, a), jnp.where(chip == 1, a, x))
+        for a, x in ((own, own_x), (beside, beside_x))
+    ]
+    odd = z % 2 == 1
+    low = [jnp.where(odd, b, a) for a, b in zip(*pairs)]
+    high = [jnp.where(odd, a, b) for a, b in zip(*pairs)]
+    same = jnp.concatenate(low + high, axis=0)
+    across = swap(same, CORE)
+
+    logits, stat, images = score(width, place, shifts, prior, classes, same, across)
+
+    stat_core = swap(stat, CORE)
+    first = jnp.where(core == 0, stat, stat_core)
+    second = jnp.where(core == 0, stat_core, stat)
+    top = jnp.maximum(first[0], second[0])
+    both = first[1] * jnp.exp(first[0] - top) + second[1] * jnp.exp(second[0] - top)
+    stat = jnp.concatenate([top[None], both[None], stat[2:]], axis=0)
+    stats = [stat] + [swap(stat, m) for m in (CHIP, NEXT, NEXT + CHIP)]
+    weights, evidence, below = weigh_classes(width, place, logits, images, stats)
+    other_below = swap(below, SAME)
+
+    mine, other, ratios, others, firsts = [], [], [], [], []
+    for p, cycles in enumerate(CHUNKS):
+        firsts.append(sum(CHUNKS[:p]))
+        after = tuple(mine[-1:]) + tuple(ratios[: p - 1][-1:] if p > 1 else ())
+        mine.append(update(width, rows, firsts[p], cycles, shifts, weights, images, after))
+        other.append(swap(mine[p], SAME))
+        ratios.append(divide(firsts[p], mine[p], other[p], below, other_below))
+        others.append(swap(ratios[p], NEXT))
+    updated = ()
+    for p in range(len(CHUNKS)):
+        updated = (blend(firsts[p], place, classes, ratios[p], others[p], updated),)
+    count = picks.shape[0]
+    by_shard = evidence[0].reshape(2, 2, 2, count)
+    log_evidence = jnp.take(by_shard, z % 2, axis=1)
+    return (updated[0], jnp.transpose(log_evidence, (1, 0, 2)).reshape(4 * count))
 
 
 def joined(part, axis, combine):
@@ -81,7 +426,7 @@
     return (row_top, row_total)
 
 
-def on_device(pool, picks, groups, ctf_table, shifts, classes, log_prior):
+def whole_sum(pool, picks, groups, ctf_table, shifts, classes, log_prior):
     chosen = jnp.take(pool, picks, axis=0)
     count_local = chosen.shape[0]
     onehot_rows = (
@@ -143,6 +488,7 @@
         P(("groups", "cls")),
     )
     out_specs = (P(("groups", "cls"), None), P(("groups", "particle")))
+    quad = mesh.shape["particle"] == 4 and mesh.shape["cls"] == 4
     return jax.shard_map(
-        on_device, mesh=mesh, in_specs=in_specs, out_specs=out_specs, check_vma=False
-    )
+        halved if quad else whole_sum, mesh=mesh, in_specs=in_specs, out_specs=out_specs, check_vma=False
+    )

time: 362 us -> 84.6 us (0.23)
  matrix products: 152 us -> 0 us
  loops' own time: 45.8 us -> 0 us
  blocking collectives: 41.6 us -> 0 us
  local copies, waits for them, and re-layouts: 39.3 us -> 7.99 us
  Pallas kernels: 0 us -> 28.6 us
  waiting for transfers between devices: 51.1 us -> 23.2 us
  starting transfers between devices: 0.04 us -> 23.4 us
  other arithmetic: 14.4 us -> 0.25 us
  between operations: 14.9 us -> 0.82 us
    dot_general x75 -> x0, matrix products: 152 us -> none  [the longest x36 112 us: advance(): jnp.dot(piece, weight_block[slot], preferred_element_type=jnp.float32)]
    psum x1 -> x0, waiting for transfers between devices: 51.1 us -> none  [on_device(): numerator, denominator = lax.psum((numerator, denominator), 'particle')]
    another operation x3 -> x0, loops' own time: 45.8 us -> none  [the longest x1 23.1 us: class_numerator(): lax.scan(advance, start_value, (shift_blocks, weight_blocks))]
    pallas_call x0 -> x15, Pallas kernels: none -> 28.6 us  [the longest x1 10.4 us: score(): pl.pallas_call(functools.partial(score_kernel, width, groups, span), out_...]
    ppermute x0 -> x17, starting transfers between devices: none -> 23.4 us  [swap(): return lax.ppermute(a, axes, [(i, i ^ mask) for i in range(16)])]
    ppermute x0 -> x17, waiting for transfers between devices: none -> 23.2 us  [swap(): return lax.ppermute(a, axes, [(i, i ^ mask) for i in range(16)])]
    psum x1 -> x0, blocking collectives: 19.5 us -> none  [on_device(): numerator, denominator = lax.psum((numerator, denominator), 'particle')]
    all_gather x2 -> x0, blocking collectives: 15.2 us -> none  [the longest x1 10 us: on_device(): lax.all_gather(weighted, 'cls', axis=0, tiled=True)]
  transfers between devices with their start and end apart: 1 -> 17, of which waited for: 1 -> 11; matrix products, arithmetic and copies ran while one was open for 1% -> 1% of each run, Pallas kernels for 0% -> 11%
where the time goes in v2:
time: 84.6 us; the launch traced here: 84.3 us
  Pallas kernels  28.6 us (34%)
  starting transfers between devices  23.4 us (28%)
  waiting for transfers between devices  23.2 us (27%)
  local copies, waits for them, and re-layouts  7.99 us (9%)
    ppermute x17, starting transfers between devices, swap(): return lax.ppermute(a, axes, [(i, i ^ mask) for i in range(16)])  23.4 us
    ppermute x17, waiting for transfers between devices, swap(): return lax.ppermute(a, axes, [(i, i ^ mask) for i in range(16)])  23.2 us
    pallas_call x1, Pallas kernels, score(): pl.pallas_call(functools.partial(score_kernel, width, groups, span), out_...  10.4 us
    pallas_call x4, Pallas kernels, update(): pl.pallas_call(later(functools.partial(update_kernel, width, rows, span),...  9.87 us
    unnamed x22, local copies, waits for them, and re-layouts  7.28 us
    pallas_call x4, Pallas kernels, blend(): pl.pallas_call(blend_kernel, grid=(1,), out_shape=jax.ShapeDtypeStruct(cl...  5.56 us
    pallas_call x1, Pallas kernels, weigh_classes(): pl.pallas_call(functools.partial(weight_kernel, width), grid=(1,), out_sh...  1.7 us
  transfers between devices with their start and end apart: 17, of which 11 were waited for; matrix products, arithmetic and copies ran while one was open for 1% of the time, Pallas kernels for 11%

profile of v2, /device:TPU:0, one launch (start us, length us, event | category | flops | bytes accessed | tf_op | source)
XLA Modules:
  0.0 84.3 jit_solution(8638922508260641699)
XLA Ops:
  4.1 3.1 %collective-permute-start = (bf16[24,4224]{1,0:T(8,128)(2,1)S(1)}, bf16[24,4224]{1,0:T(8,128)(2,1)S(1)}, u32[]{:S(2)}, u32[]{:S(2)}) collective-permute-start(bf16[24,4224]{1,0:T(8,128)(2,1)S(1)} %weigh.1), channel_id=1, source_target_pairs={{0,4},{1,5},{2,6},{3,7},{4,0},{5,1},{6,2},{7,3},{8,12},{9,13},{10,... | collective-permute-start | bytes 608264 | tf_op jit(solution)/shard_map/ppermute | solution.py:315
  7.2 1.5 %collective-permute-start.2 = (bf16[24,4224]{1,0:T(8,128)(2,1)S(1)}, bf16[24,4224]{1,0:T(8,128)(2,1)S(1)}, u32[]{:S(2)}, u32[]{:S(2)}) collective-permute-start(bf16[24,4224]{1,0:T(8,128)(2,1)S(1)} %weigh.1), channel_id=1, source_target_pairs={{0,2},{1,3},{2,0},{3,1},{4,6},{5,7},{6,4},{7,5},{8,10},{9,11},{10,... | collective-permute-start | bytes 608264 | tf_op jit(solution)/shard_map/ppermute | solution.py:315
  8.7 3.5 %collective-permute-done = bf16[24,4224]{1,0:T(8,128)(2,1)S(1)} collective-permute-done((bf16[24,4224]{1,0:T(8,128)(2,1)S(1)}, bf16[24,4224]{1,0:T(8,128)(2,1)S(1)}, u32[]{:S(2)}, u32[]{:S(2)}) %collective-permute-start) | collective-permute-done | bytes 202784 | tf_op jit(solution)/shard_map/ppermute | solution.py:315
  12.2 1.7 %collective-permute-start.1 = (bf16[24,4224]{1,0:T(8,128)(2,1)S(1)}, bf16[24,4224]{1,0:T(8,128)(2,1)S(1)}, u32[]{:S(2)}, u32[]{:S(2)}) collective-permute-start(bf16[24,4224]{1,0:T(8,128)(2,1)S(1)} %collective-permute-done), channel_id=1, source_target_pairs={{0,2},{1,3},{2,0},{3,1},{4,6},{5,7},{6,4},{7,5},{8,10},{9,11},{10,... | collective-permute-start | bytes 608264 | tf_op jit(solution)/shard_map/ppermute | solution.py:315
  13.9 4.6 %collective-permute-done.1 = bf16[24,4224]{1,0:T(8,128)(2,1)S(1)} collective-permute-done((bf16[24,4224]{1,0:T(8,128)(2,1)S(1)}, bf16[24,4224]{1,0:T(8,128)(2,1)S(1)}, u32[]{:S(2)}, u32[]{:S(2)}) %collective-permute-start.1) | collective-permute-done | bytes 202784 | tf_op jit(solution)/shard_map/ppermute | solution.py:315
  18.8 2.2 %collective-permute-done.3.across = bf16[96,4224]{1,0:T(8,128)(2,1)S(1)} collective-permute-done((bf16[96,4224]{1,0:T(8,128)(2,1)S(1)}, bf16[96,4224]{1,0:T(8,128)(2,1)S(1)}, u32[]{:S(2)}, u32[]{:S(2)}) %collective-permute-start.3) | collective-permute-done | bytes 811040 | tf_op jit(solution)/shard_map/ppermute | solution.py:315
  21.0 10.4 %score.1 = (f32[2304,192]{1,0:T(8,128)}, f32[8,192]{1,0:T(8,128)S(1)}, bf16[192,4224]{1,0:T(8,128)(2,1)S(1)}) custom-call(s32[3]{0:T(128)S(1)} %pad_add_fusion.place, s32[36]{0:T(128)S(1)} %copy-done.5, f32[1,128]{1,0:T(1,128)S(1)} %pad_bitcast_fusion.prior, f32[100,4096]{1,0:T(8,128)S(1)} %copy-done, bf16[96,4224]{1,0:T(8,128)(2,1)S(1)} %pad_maximum_fusion.same, ...), custom_call_target="tpu_custom_call" | custom-call | flops 10737418240 | bytes 20971520 | tf_op jit(solution)/shard_map/score/pallas_call | solution.py:154
  33.8 1.4 %collective-permute-start.5 = (f32[8,192]{1,0:T(8,128)S(1)}, f32[8,192]{1,0:T(8,128)S(1)}, u32[]{:S(2)}, u32[]{:S(2)}) collective-permute-start(f32[8,192]{1,0:T(8,128)S(1)} %pad_maximum_fusion.1.refs_0_), channel_id=1, source_target_pairs={{0,2},{1,3},{2,0},{3,1},{4,6},{5,7},{6,4},{7,5},{8,10},{9,11},{10,... | collective-permute-start | bytes 18440 | tf_op jit(solution)/shard_map/ppermute | solution.py:315
  35.2 1.6 %collective-permute-start.6 = (f32[8,192]{1,0:T(8,128)S(1)}, f32[8,192]{1,0:T(8,128)S(1)}, u32[]{:S(2)}, u32[]{:S(2)}) collective-permute-start(f32[8,192]{1,0:T(8,128)S(1)} %pad_maximum_fusion.1.refs_0_), channel_id=1, source_target_pairs={{0,4},{1,5},{2,6},{3,7},{4,0},{5,1},{6,2},{7,3},{8,12},{9,13},{10,... | collective-permute-start | bytes 18440 | tf_op jit(solution)/shard_map/ppermute | solution.py:315
  38.9 2.5 %collective-permute-done.7.refs_3_ = f32[8,192]{1,0:T(8,128)S(1)} collective-permute-done((f32[8,192]{1,0:T(8,128)S(1)}, f32[8,192]{1,0:T(8,128)S(1)}, u32[]{:S(2)}, u32[]{:S(2)}) %collective-permute-start.7) | collective-permute-done | bytes 6176 | tf_op jit(solution)/shard_map/ppermute | solution.py:315
  41.3 1.4 %copy-done.7 = bf16[192,4224]{1,0:T(8,128)(2,1)S(1)} copy-done((bf16[192,4224]{1,0:T(8,128)(2,1)S(1)}, bf16[192,4224]{1,0:T(8,128)(2,1)}, u32[]{:S(2)}) %copy-start.7) | copy-done | bytes 1622040
  42.8 1.7 %copy-done.9 = f32[2304,192]{1,0:T(8,128)S(1)} copy-done((f32[2304,192]{1,0:T(8,128)S(1)}, f32[2304,192]{1,0:T(8,128)}, u32[]{:S(2)}) %copy-start.9) | copy-done | bytes 1769496
  44.4 1.7 %weights.1 = (bf16[2304,192]{1,0:T(8,128)(2,1)S(1)}, f32[8,192]{1,0:T(8,128)S(1)}, f32[64,128]{1,0:T(8,128)S(1)}) custom-call(s32[3]{0:T(128)S(1)} %pad_add_fusion.place, f32[2304,192]{1,0:T(8,128)S(1)} %copy-done.9, bf16[192,4224]{1,0:T(8,128)(2,1)S(1)} %copy-done.7, f32[8,192]{1,0:T(8,128)S(1)} %pad_maximum_fusion.1.refs_0_, ...), custom_call_target="tpu_custom_call" | custom-call | flops 4294967296 | bytes 8388608 | tf_op jit(solution)/shard_map/weights/pallas_call | solution.py:200
  46.2 2.5 %update.4.refs_0_.one = bf16[56,1024]{1,0:T(8,128)(2,1)S(1)} custom-call(s32[36]{0:T(128)S(1)} %copy-done.5, bf16[2304,192]{1,0:T(8,128)(2,1)S(1)} %get-tuple-element.11.refs_1_.refs_2_.refs_3_, bf16[192,4224]{1,0:T(8,128)(2,1)S(1)} %copy-done.8), custom_call_target="tpu_custom_call" | custom-call | flops 3221225472 | bytes 4194304 | tf_op jit(solution)/shard_map/update/pallas_call | solution.py:229
  48.6 2.5 %collective-permute-start.8 = (bf16[56,1024]{1,0:T(8,128)(2,1)S(1)}, bf16[56,1024]{1,0:T(8,128)(2,1)S(1)}, u32[]{:S(2)}, u32[]{:S(2)}) collective-permute-start(bf16[56,1024]{1,0:T(8,128)(2,1)S(1)} %update.4.refs_0_.one), channel_id=1, source_target_pairs={{0,12},{1,13},{2,14},{3,15},{4,8},{5,9},{6,10},{7,11},{8,4},{9,5},... | collective-permute-start | bytes 344072 | tf_op jit(solution)/shard_map/ppermute | solution.py:315
  52.5 2.5 %update.5.refs_0_.one = bf16[56,1024]{1,0:T(8,128)(2,1)S(1)} custom-call(bf16[56,1024]{1,0:T(8,128)(2,1)S(1)} %update.4.refs_0_.one, s32[36]{0:T(128)S(1)} %copy-done.5, bf16[2304,192]{1,0:T(8,128)(2,1)S(1)} %get-tuple-element.11.refs_1_.refs_2_.refs_3_, bf16[192,4224]{1,0:T(8,128)(2,1)S(1)} %copy-done.8), custom_call_target="tpu_custom_call" | custom-call | flops 3221225472 | bytes 4194304 | tf_op jit(solution)/shard_map/update/pallas_call | solution.py:229
  55.0 2.5 %collective-permute-start.10 = (bf16[56,1024]{1,0:T(8,128)(2,1)S(1)}, bf16[56,1024]{1,0:T(8,128)(2,1)S(1)}, u32[]{:S(2)}, u32[]{:S(2)}) collective-permute-start(bf16[56,1024]{1,0:T(8,128)(2,1)S(1)} %update.5.refs_0_.one), channel_id=1, source_target_pairs={{0,12},{1,13},{2,14},{3,15},{4,8},{5,9},{6,10},{7,11},{8,4},{9,5},... | collective-permute-start | bytes 344072 | tf_op jit(solution)/shard_map/ppermute | solution.py:315
  57.7 2.5 %update.6.refs_0_.one = bf16[56,1024]{1,0:T(8,128)(2,1)S(1)} custom-call(bf16[56,1024]{1,0:T(8,128)(2,1)S(1)} %update.5.refs_0_.one, bf16[56,1024]{1,0:T(8,128)(2,1)S(1)} %divide.4.refs_1_.mine, s32[36]{0:T(128)S(1)} %copy-done.5, bf16[2304,192]{1,0:T(8,128)(2,1)S(1)} %get-tuple-element.11.refs_1_.refs_2_.refs_3_, bf16[192,4224]{1,0:T(8,128)(2,1)S(1)} %copy-done.8), custom_call_target="tpu_custom_call" | custom-call | flops 3221225472 | bytes 4194304 | tf_op jit(solution)/shard_map/update/pallas_call | solution.py:229
  60.2 1.6 %collective-permute-done.10.two = bf16[56,1024]{1,0:T(8,128)(2,1)S(1)} collective-permute-done((bf16[56,1024]{1,0:T(8,128)(2,1)S(1)}, bf16[56,1024]{1,0:T(8,128)(2,1)S(1)}, u32[]{:S(2)}, u32[]{:S(2)}) %collective-permute-start.10) | collective-permute-done | bytes 114720 | tf_op jit(solution)/shard_map/ppermute | solution.py:315
  61.9 2.5 %update.7.one = bf16[56,1024]{1,0:T(8,128)(2,1)S(1)} custom-call(bf16[56,1024]{1,0:T(8,128)(2,1)S(1)} %update.6.refs_0_.one, bf16[56,1024]{1,0:T(8,128)(2,1)S(1)} %divide.5.refs_1_.mine, s32[36]{0:T(128)S(1)} %copy-done.5, bf16[2304,192]{1,0:T(8,128)(2,1)S(1)} %get-tuple-element.11.refs_1_.refs_2_.refs_3_, bf16[192,4224]{1,0:T(8,128)(2,1)S(1)} %copy-done.8), custom_call_target="tpu_custom_call" | custom-call | flops 3221225472 | bytes 4194304 | tf_op jit(solution)/shard_map/update/pallas_call | solution.py:229
  64.4 2.5 %collective-permute-start.11 = (bf16[56,1024]{1,0:T(8,128)(2,1)S(1)}, bf16[56,1024]{1,0:T(8,128)(2,1)S(1)}, u32[]{:S(2)}, u32[]{:S(2)}) collective-permute-start(bf16[56,1024]{1,0:T(8,128)(2,1)S(1)} %update.7.one), channel_id=1, source_target_pairs={{0,12},{1,13},{2,14},{3,15},{4,8},{5,9},{6,10},{7,11},{8,4},{9,5},... | collective-permute-start | bytes 344072 | tf_op jit(solution)/shard_map/ppermute | solution.py:315
  69.0 2.0 %collective-permute-start.16 = (bf16[56,1024]{1,0:T(8,128)(2,1)S(1)}, bf16[56,1024]{1,0:T(8,128)(2,1)S(1)}, u32[]{:S(2)}, u32[]{:S(2)}) collective-permute-start(bf16[56,1024]{1,0:T(8,128)(2,1)S(1)} %divide.4.refs_1_.mine), channel_id=1, source_target_pairs={{0,4},{1,5},{2,6},{3,7},{4,0},{5,1},{6,2},{7,3},{8,12},{9,13},{10,... | collective-permute-start | bytes 344072 | tf_op jit(solution)/shard_map/ppermute | solution.py:315
  73.1 1.8 %collective-permute-done.13.two = bf16[56,1024]{1,0:T(8,128)(2,1)S(1)} collective-permute-done((bf16[56,1024]{1,0:T(8,128)(2,1)S(1)}, bf16[56,1024]{1,0:T(8,128)(2,1)S(1)}, u32[]{:S(2)}, u32[]{:S(2)}) %collective-permute-start.13) | collective-permute-done | bytes 114720 | tf_op jit(solution)/shard_map/ppermute | solution.py:315
  75.5 3.2 %collective-permute-done.16.other = bf16[56,1024]{1,0:T(8,128)(2,1)S(1)} collective-permute-done((bf16[56,1024]{1,0:T(8,128)(2,1)S(1)}, bf16[56,1024]{1,0:T(8,128)(2,1)S(1)}, u32[]{:S(2)}, u32[]{:S(2)}) %collective-permute-start.16) | collective-permute-done | bytes 114720 | tf_op jit(solution)/shard_map/ppermute | solution.py:315
  (60 shorter events, 20.2 us)
Async XLA Ops:
  4.1 8.1 %collective-permute-start = (bf16[24,4224]{1,0:T(8,128)(2,1)S(1)}, bf16[24,4224]{1,0:T(8,128)(2,1)S(1)}, u32[]{:S(2)}, u32[]{:S(2)}) collective-permute-start(bf16[24,4224]{1,0:T(8,128)(2,1)S(1)} %weigh.1), channel_id=1, source_target_pairs={{0,4},{1,5},{2,6},{3,7},{4,0},{5,1},{6,2},{7,3},{8,12},{9,13},{10,... | collective-permute-start | bytes 608264 | tf_op jit(solution)/shard_map/ppermute | solution.py:315
  7.2 6.7 %collective-permute-start.2 = (bf16[24,4224]{1,0:T(8,128)(2,1)S(1)}, bf16[24,4224]{1,0:T(8,128)(2,1)S(1)}, u32[]{:S(2)}, u32[]{:S(2)}) collective-permute-start(bf16[24,4224]{1,0:T(8,128)(2,1)S(1)} %weigh.1), channel_id=1, source_target_pairs={{0,2},{1,3},{2,0},{3,1},{4,6},{5,7},{6,4},{7,5},{8,10},{9,11},{10,... | collective-permute-start | bytes 608264 | tf_op jit(solution)/shard_map/ppermute | solution.py:315
  12.2 6.2 %collective-permute-start.1 = (bf16[24,4224]{1,0:T(8,128)(2,1)S(1)}, bf16[24,4224]{1,0:T(8,128)(2,1)S(1)}, u32[]{:S(2)}, u32[]{:S(2)}) collective-permute-start(bf16[24,4224]{1,0:T(8,128)(2,1)S(1)} %collective-permute-done), channel_id=1, source_target_pairs={{0,2},{1,3},{2,0},{3,1},{4,6},{5,7},{6,4},{7,5},{8,10},{9,11},{10,... | collective-permute-start | bytes 608264 | tf_op jit(solution)/shard_map/ppermute | solution.py:315
  13.9 4.8 %copy-start.10 = (f32[100]{0:T(128)S(1)}, f32[100]{0:T(128)}, u32[]{:S(2)}) copy-start(f32[100]{0:T(128)} %param.13) | copy-start | bytes 1204
  13.9 7.1 %copy-start = (f32[100,4096]{1,0:T(8,128)S(1)}, f32[100,4096]{1,0:T(8,128)}, u32[]{:S(2)}) copy-start(f32[100,4096]{1,0:T(8,128)} %classes.9) | copy-start | bytes 4915204
  13.9 7.1 %copy-start.5 = (s32[36]{0:T(128)S(1)}, s32[36]{0:T(128)}, u32[]{:S(2)}) copy-start(s32[36]{0:T(128)} %refs_2_.3) | copy-start | bytes 436
  18.6 2.4 %collective-permute-start.3 = (bf16[96,4224]{1,0:T(8,128)(2,1)S(1)}, bf16[96,4224]{1,0:T(8,128)(2,1)S(1)}, u32[]{:S(2)}, u32[]{:S(2)}) collective-permute-start(bf16[96,4224]{1,0:T(8,128)(2,1)S(1)} %pad_maximum_fusion.same), channel_id=1, source_target_pairs={{0,1},{1,0},{2,3},{3,2},{4,5},{5,4},{6,7},{7,6},{8,9},{9,8},{10,11... | collective-permute-start | bytes 2433032 | tf_op jit(solution)/shard_map/ppermute | solution.py:315
  31.4 1.2 %copy-start.6 = (bf16[192,4224]{1,0:T(8,128)(2,1)}, bf16[192,4224]{1,0:T(8,128)(2,1)S(1)}, u32[]{:S(2)}) copy-start(bf16[192,4224]{1,0:T(8,128)(2,1)S(1)} %get-tuple-element.9.squares.refs_2_.refs_3_.refs_4_) | copy-start | bytes 4866052
  32.6 1.2 %collective-permute-start.4 = (f32[8,192]{1,0:T(8,128)S(1)}, f32[8,192]{1,0:T(8,128)S(1)}, u32[]{:S(2)}, u32[]{:S(2)}) collective-permute-start(f32[8,192]{1,0:T(8,128)S(1)} %get-tuple-element.10), channel_id=1, source_target_pairs={{0,1},{1,0},{2,3},{3,2},{4,5},{5,4},{6,7},{7,6},{8,9},{9,8},{10,11... | collective-permute-start | bytes 18440 | tf_op jit(solution)/shard_map/ppermute | solution.py:315
  33.8 3.7 %collective-permute-start.5 = (f32[8,192]{1,0:T(8,128)S(1)}, f32[8,192]{1,0:T(8,128)S(1)}, u32[]{:S(2)}, u32[]{:S(2)}) collective-permute-start(f32[8,192]{1,0:T(8,128)S(1)} %pad_maximum_fusion.1.refs_0_), channel_id=1, source_target_pairs={{0,2},{1,3},{2,0},{3,1},{4,6},{5,7},{6,4},{7,5},{8,10},{9,11},{10,... | collective-permute-start | bytes 18440 | tf_op jit(solution)/shard_map/ppermute | solution.py:315
  35.2 3.7 %collective-permute-start.6 = (f32[8,192]{1,0:T(8,128)S(1)}, f32[8,192]{1,0:T(8,128)S(1)}, u32[]{:S(2)}, u32[]{:S(2)}) collective-permute-start(f32[8,192]{1,0:T(8,128)S(1)} %pad_maximum_fusion.1.refs_0_), channel_id=1, source_target_pairs={{0,4},{1,5},{2,6},{3,7},{4,0},{5,1},{6,2},{7,3},{8,12},{9,13},{10,... | collective-permute-start | bytes 18440 | tf_op jit(solution)/shard_map/ppermute | solution.py:315
  36.8 4.5 %collective-permute-start.7 = (f32[8,192]{1,0:T(8,128)S(1)}, f32[8,192]{1,0:T(8,128)S(1)}, u32[]{:S(2)}, u32[]{:S(2)}) collective-permute-start(f32[8,192]{1,0:T(8,128)S(1)} %pad_maximum_fusion.1.refs_0_), channel_id=1, source_target_pairs={{0,6},{1,7},{2,4},{3,5},{4,2},{5,3},{6,0},{7,1},{8,14},{9,15},{10,... | collective-permute-start | bytes 18440 | tf_op jit(solution)/shard_map/ppermute | solution.py:315
  41.3 1.4 %copy-start.7 = (bf16[192,4224]{1,0:T(8,128)(2,1)S(1)}, bf16[192,4224]{1,0:T(8,128)(2,1)}, u32[]{:S(2)}) copy-start(bf16[192,4224]{1,0:T(8,128)(2,1)} %copy-done.6) | copy-start | bytes 4866052
  42.8 1.7 %copy-start.9 = (f32[2304,192]{1,0:T(8,128)S(1)}, f32[2304,192]{1,0:T(8,128)}, u32[]{:S(2)}) copy-start(f32[2304,192]{1,0:T(8,128)} %get-tuple-element.8.logits) | copy-start | bytes 5308420
  44.4 1.7 %copy-start.8 = (bf16[192,4224]{1,0:T(8,128)(2,1)S(1)}, bf16[192,4224]{1,0:T(8,128)(2,1)}, u32[]{:S(2)}) copy-start(bf16[192,4224]{1,0:T(8,128)(2,1)} %copy-done.6) | copy-start | bytes 4866052
  48.6 8.9 %collective-permute-start.8 = (bf16[56,1024]{1,0:T(8,128)(2,1)S(1)}, bf16[56,1024]{1,0:T(8,128)(2,1)S(1)}, u32[]{:S(2)}, u32[]{:S(2)}) collective-permute-start(bf16[56,1024]{1,0:T(8,128)(2,1)S(1)} %update.4.refs_0_.one), channel_id=1, source_target_pairs={{0,12},{1,13},{2,14},{3,15},{4,8},{5,9},{6,10},{7,11},{8,4},{9,5},... | collective-permute-start | bytes 344072 | tf_op jit(solution)/shard_map/ppermute | solution.py:315
  51.2 6.4 %collective-permute-start.9 = (f32[64,128]{1,0:T(8,128)S(1)}, f32[64,128]{1,0:T(8,128)S(1)}, u32[]{:S(2)}, u32[]{:S(2)}) collective-permute-start(f32[64,128]{1,0:T(8,128)S(1)} %get-tuple-element.12.one_below), channel_id=1, source_target_pairs={{0,12},{1,13},{2,14},{3,15},{4,8},{5,9},{6,10},{7,11},{8,4},{9,5},... | collective-permute-start | bytes 98312 | tf_op jit(solution)/shard_map/ppermute | solution.py:315
  55.0 6.8 %collective-permute-start.10 = (bf16[56,1024]{1,0:T(8,128)(2,1)S(1)}, bf16[56,1024]{1,0:T(8,128)(2,1)S(1)}, u32[]{:S(2)}, u32[]{:S(2)}) collective-permute-start(bf16[56,1024]{1,0:T(8,128)(2,1)S(1)} %update.5.refs_0_.one), channel_id=1, source_target_pairs={{0,12},{1,13},{2,14},{3,15},{4,8},{5,9},{6,10},{7,11},{8,4},{9,5},... | collective-permute-start | bytes 344072 | tf_op jit(solution)/shard_map/ppermute | solution.py:315
  64.4 7.9 %collective-permute-start.11 = (bf16[56,1024]{1,0:T(8,128)(2,1)S(1)}, bf16[56,1024]{1,0:T(8,128)(2,1)S(1)}, u32[]{:S(2)}, u32[]{:S(2)}) collective-permute-start(bf16[56,1024]{1,0:T(8,128)(2,1)S(1)} %update.7.one), channel_id=1, source_target_pairs={{0,12},{1,13},{2,14},{3,15},{4,8},{5,9},{6,10},{7,11},{8,4},{9,5},... | collective-permute-start | bytes 344072 | tf_op jit(solution)/shard_map/ppermute | solution.py:315
  67.0 7.9 %collective-permute-start.13 = (bf16[56,1024]{1,0:T(8,128)(2,1)S(1)}, bf16[56,1024]{1,0:T(8,128)(2,1)S(1)}, u32[]{:S(2)}, u32[]{:S(2)}) collective-permute-start(bf16[56,1024]{1,0:T(8,128)(2,1)S(1)} %update.6.refs_0_.one), channel_id=1, source_target_pairs={{0,12},{1,13},{2,14},{3,15},{4,8},{5,9},{6,10},{7,11},{8,4},{9,5},... | collective-permute-start | bytes 344072 | tf_op jit(solution)/shard_map/ppermute | solution.py:315
  69.0 11.1 %collective-permute-start.15 = (bf16[56,1024]{1,0:T(8,128)(2,1)S(1)}, bf16[56,1024]{1,0:T(8,128)(2,1)S(1)}, u32[]{:S(2)}, u32[]{:S(2)}) collective-permute-start(bf16[56,1024]{1,0:T(8,128)(2,1)S(1)} %divide.5.refs_1_.mine), channel_id=1, source_target_pairs={{0,4},{1,5},{2,6},{3,7},{4,0},{5,1},{6,2},{7,3},{8,12},{9,13},{10,... | collective-permute-start | bytes 344072 | tf_op jit(solution)/shard_map/ppermute | solution.py:315
  69.0 9.7 %collective-permute-start.16 = (bf16[56,1024]{1,0:T(8,128)(2,1)S(1)}, bf16[56,1024]{1,0:T(8,128)(2,1)S(1)}, u32[]{:S(2)}, u32[]{:S(2)}) collective-permute-start(bf16[56,1024]{1,0:T(8,128)(2,1)S(1)} %divide.4.refs_1_.mine), channel_id=1, source_target_pairs={{0,4},{1,5},{2,6},{3,7},{4,0},{5,1},{6,2},{7,3},{8,12},{9,13},{10,... | collective-permute-start | bytes 344072 | tf_op jit(solution)/shard_map/ppermute | solution.py:315
  72.5 10.4 %collective-permute-start.12 = (bf16[56,1024]{1,0:T(8,128)(2,1)S(1)}, bf16[56,1024]{1,0:T(8,128)(2,1)S(1)}, u32[]{:S(2)}, u32[]{:S(2)}) collective-permute-start(bf16[56,1024]{1,0:T(8,128)(2,1)S(1)} %divide.6.mine), channel_id=1, source_target_pairs={{0,4},{1,5},{2,6},{3,7},{4,0},{5,1},{6,2},{7,3},{8,12},{9,13},{10,... | collective-permute-start | bytes 344072 | tf_op jit(solution)/shard_map/ppermute | solution.py:315
  75.1 6.4 %collective-permute-start.14 = (bf16[56,1024]{1,0:T(8,128)(2,1)S(1)}, bf16[56,1024]{1,0:T(8,128)(2,1)S(1)}, u32[]{:S(2)}, u32[]{:S(2)}) collective-permute-start(bf16[56,1024]{1,0:T(8,128)(2,1)S(1)} %divide.7.mine), channel_id=1, source_target_pairs={{0,4},{1,5},{2,6},{3,7},{4,0},{5,1},{6,2},{7,3},{8,12},{9,13},{10,... | collective-permute-start | bytes 344072 | tf_op jit(solution)/shard_map/ppermute | solution.py:315
  (4 other events, 3.0 us)

commit v3 on v2

--- a/solution.py
+++ b/solution.py
@@ -26,7 +26,7 @@
 EXACT = lax.Precision.HIGHEST
 NEGATIVE = -1e30
 CHUNKS = (8, 8, 8, 8)
-LARGE = 48
+LARGE = 58
 
 
 def later(kernel, count):
@@ -68,44 +68,63 @@
         out_shape=jax.ShapeDtypeStruct((count, PIX + ANG), BF16),
         in_specs=[VMEM] * 4,
         out_specs=VMEM,
-        compiler_params=params(),
+        compiler_params=params(LARGE),
         cost_estimate=cost(2 * count * 48 * PIX, 2**20),
         name="weigh",
     )(picks.reshape(1, -1), groups.reshape(1, -1), pool, table.T)
 
 
-def score_kernel(width, groups, span, place, shifts, prior, classes, same, across, *refs):
-    (logits, stats, images), (halved, bias, *turned) = refs[:3], refs[3:]
-    one = same.shape[0]
-    count = images.shape[0]
-    core = place[2]
+def prepare_kernel(width, place, classes, prior, halved, power, column):
     upper = place[0] == 1
     total = classes.shape[0]
     start, cut, _, _ = halves(total)
-    images[pl.ds(pl.multiple_of(core * one, 16), one), :] = same[...]
-    images[pl.ds(pl.multiple_of((1 - core) * one, 16), one), :] = across[...]
-
     pad = jnp.zeros((width - (total - start), ANG), F32)
     lane = lax.broadcasted_iota(jnp.int32, (width, ANG), 1)
-    power = jnp.zeros((width, ANG), F32)
+    kept = jnp.zeros((width, ANG), F32)
     for c in range(CYCLES):
         here = slice(c * ANG, (c + 1) * ANG)
         high = jnp.concatenate([classes[start:total, here], pad], axis=0)
         mine = jnp.where(upper, high, classes[0:width, here]).astype(BF16)
         halved[:, here] = mine
         wide = mine.astype(F32)
-        power = jnp.where(lane == c, jnp.sum(wide * wide, axis=1, keepdims=True), power)
-
-    squares = images[:, PIX:].astype(F32)
-    norm = lax.dot_general(power, squares, NT, precision=EXACT, preferred_element_type=F32)
-    column = jnp.broadcast_to(prior[...], (8, ANG)).T[:, 0:1]
-    high = jnp.concatenate([column[start:total, :], pad[:, 0:1]], axis=0)
-    value = jnp.where(upper, high, column[0:width, :]) - 0.5 * norm
-    row = lax.broadcasted_iota(jnp.int32, norm.shape, 0)
+        kept = jnp.where(lane == c, jnp.sum(wide * wide, axis=1, keepdims=True), kept)
+    power[...] = kept
+    turned = jnp.broadcast_to(prior[...], (ANG, ANG)).T
+    high = jnp.concatenate([turned[start:total, :], pad], axis=0)
+    row = lax.broadcasted_iota(jnp.int32, (width, ANG), 0)
     mine = (row >= jnp.where(upper, cut - start, 0)) & (
         row < jnp.where(upper, total - start, cut)
     )
-    bias[...] = jnp.where(mine, value, NEGATIVE)
+    column[...] = jnp.where(mine, jnp.where(upper, high, turned[0:width, :]), NEGATIVE)
+
+
+def prepare(width, place, classes, prior, after):
+    return pl.pallas_call(
+        later(functools.partial(prepare_kernel, width), len(after)),
+        out_shape=(
+            jax.ShapeDtypeStruct((width, PIX), BF16),
+            jax.ShapeDtypeStruct((width, ANG), F32),
+            jax.ShapeDtypeStruct((width, ANG), F32),
+        ),
+        in_specs=[ANY] * len(after) + [SMEM, VMEM, VMEM],
+        out_specs=(VMEM,) * 3,
+        compiler_params=params(LARGE),
+        cost_estimate=cost(2 * 2**30, 2 * 2**20),
+        name="prepare",
+    )(*after, place, classes, prior)
+
+
+def score_kernel(width, groups, span, place, shifts, halved, power, column, same, across, *refs):
+    (terms, summed, stats, sides), (images, logits, *turned) = refs[:4], refs[4:]
+    one = same.shape[0]
+    count = images.shape[0]
+    core = place[2]
+    images[pl.ds(pl.multiple_of(core * one, 16), one), :] = same[...]
+    images[pl.ds(pl.multiple_of((1 - core) * one, 16), one), :] = across[...]
+    squares = images[:, PIX:].astype(F32)
+    sides[...] = squares
+    norm = lax.dot_general(power[...], squares, NT, precision=EXACT, preferred_element_type=F32)
+    bias = column[:, 0:1] - 0.5 * norm
 
     each = ROT // groups
     top = jnp.full((width, count), NEGATIVE, F32)
@@ -128,45 +147,52 @@
             )
             scores = part if scores is None else scores + part
         for r in range(each):
-            value = scores[r * width : (r + 1) * width, :] + bias[...]
+            value = scores[r * width : (r + 1) * width, :] + bias
             logits[(g * each + r) * width : (g * each + r + 1) * width, :] = value
             top = jnp.maximum(top, value)
     top = jnp.max(top, axis=0, keepdims=True)
 
-    def add(r, total):
-        return total + jnp.exp(logits[pl.ds(pl.multiple_of(r * width, 8), width), :] - top)
-
-    total = lax.fori_loop(0, ROT, add, jnp.zeros((width, count), F32))
+    def add(r, sums):
+        block = pl.ds(pl.multiple_of(r * width, 16), width)
+        value = jnp.exp(logits[block, :] - top)
+        rounded = value.astype(BF16)
+        terms[block, :] = rounded
+        return sums[0] + value, sums[1] + rounded.astype(F32)
+
+    zero = jnp.zeros((width, count), F32)
+    total, rounded = lax.fori_loop(0, ROT, add, (zero, zero))
+    summed[...] = rounded
     stats[0:1, :] = top
     stats[1:2, :] = jnp.sum(total, axis=0, keepdims=True)
     stats[2:, :] = jnp.zeros((6, count), F32)
 
 
-def score(width, place, shifts, prior, classes, same, across):
+def score(width, place, shifts, halved, power, column, same, across):
     groups, span = 4, 4
     one, full = same.shape
     count = 2 * one
     outs = (
-        jax.ShapeDtypeStruct((ROT * width, count), F32),
+        jax.ShapeDtypeStruct((ROT * width, count), BF16),
+        jax.ShapeDtypeStruct((width, count), F32),
         jax.ShapeDtypeStruct((8, count), F32),
-        jax.ShapeDtypeStruct((count, full), BF16),
+        jax.ShapeDtypeStruct((count, ANG), F32),
     )
     return pl.pallas_call(
         functools.partial(score_kernel, width, groups, span),
         out_shape=outs,
-        in_specs=[SMEM, SMEM] + [VMEM] * 4,
-        out_specs=(VMEM,) * 3,
-        scratch_shapes=[pltpu.VMEM((width, PIX), BF16), pltpu.VMEM((width, count), F32)]
+        in_specs=[SMEM, SMEM] + [VMEM] * 5,
+        out_specs=(VMEM,) * 4,
+        scratch_shapes=[pltpu.VMEM((count, full), BF16), pltpu.VMEM((ROT * width, count), F32)]
         + [pltpu.VMEM((ROT // groups * width, span * ANG), BF16)] * 2,
-        compiler_params=params(LARGE),
+        compiler_params=params(24),
         cost_estimate=cost(10 * 2**30, 20 * 2**20),
         name="score",
-    )(place, shifts, prior, classes, same, across)
-
-
-def weight_kernel(width, place, logits, squares, *refs):
-    stats, (weights, evidence, denominator, joined) = refs[:-4], refs[-4:]
-    count = logits.shape[1]
+    )(place, shifts, halved, power, column, same, across)
+
+
+def normalize_kernel(place, own, summed, squares, *refs):
+    stats, (scales, evidence, denominator, joined) = refs[:-4], refs[-4:]
+    count = own.shape[1]
     for m, stat in enumerate(stats):
         joined[pl.ds(pl.multiple_of((place[1] ^ m) * 8, 8), 8), :] = stat[...]
     tops = [joined[8 * j : 8 * j + 1, :] for j in range(len(stats))]
@@ -174,44 +200,63 @@
     top = functools.reduce(jnp.maximum, tops)
     total = sum(t * jnp.exp(h - top) for h, t in zip(tops, totals))
     evidence[...] = jnp.broadcast_to(top + jnp.log(total), (8, count))
-    scale = 1.0 / total
-
-    def single(r, summed):
-        block = pl.ds(pl.multiple_of(r * width, 16), width)
-        value = (jnp.exp(logits[block, :] - top) * scale).astype(BF16)
-        weights[block, :] = value
-        return summed + value.astype(F32)
-
-    summed = lax.fori_loop(0, ROT, single, jnp.zeros((width, count), F32))
+    scale = jnp.exp(own[0:1, :] - top) / total
+    scales[...] = jnp.broadcast_to(scale, (ANG, count)).T
     denominator[...] = jnp.dot(
-        summed, squares[...].astype(F32), precision=EXACT, preferred_element_type=F32
-    )
-
-
-def weigh_classes(width, place, logits, images, stats):
-    count = logits.shape[1]
-    squares = pl.BlockSpec((count, ANG), lambda i: (0, PIX // ANG))
-    whole = lambda a: pl.BlockSpec(a.shape, lambda i: (0, 0))
-    outs = (
-        jax.ShapeDtypeStruct((ROT * width, count), BF16),
-        jax.ShapeDtypeStruct((8, count), F32),
-        jax.ShapeDtypeStruct((width, ANG), F32),
-    )
-    return pl.pallas_call(
-        functools.partial(weight_kernel, width),
-        grid=(1,),
-        out_shape=outs,
-        in_specs=[SMEM, whole(logits), squares] + [whole(s) for s in stats],
-        out_specs=tuple(whole(o) for o in outs),
+        summed[...] * scale, squares[...], precision=EXACT, preferred_element_type=F32
+    )
+
+
+def normalize(place, own, summed, squares, stats):
+    width, count = summed.shape
+    return pl.pallas_call(
+        normalize_kernel,
+        out_shape=(
+            jax.ShapeDtypeStruct((count, ANG), F32),
+            jax.ShapeDtypeStruct((8, count), F32),
+            jax.ShapeDtypeStruct((width, ANG), F32),
+        ),
+        in_specs=[SMEM] + [VMEM] * (3 + len(stats)),
+        out_specs=(VMEM,) * 3,
         scratch_shapes=[pltpu.VMEM((8 * len(stats), count), F32)],
-        compiler_params=params(LARGE),
-        cost_estimate=cost(4 * 2**30, 8 * 2**20),
-        name="weights",
-    )(place, logits, images, *stats)
-
-
-def update_kernel(width, rows, span, shifts, weights, images, out, product):
-    product[...] = jnp.dot(weights[...], images[...], preferred_element_type=F32).astype(BF16)
+        compiler_params=params(),
+        cost_estimate=cost(2**30, 2**20),
+        name="normalize",
+    )(place, own, summed, squares, *stats)
+
+
+def merge_kernel(place, own, other, out):
+    lower = place[2] == 0
+    first, second = (jnp.where(lower, a[...], b[...]) for a, b in ((own, other), (other, own)))
+    top = jnp.maximum(first[0:1], second[0:1])
+    out[...] = jnp.zeros_like(out)
+    out[0:1, :] = top
+    out[1:2, :] = first[1:2] * jnp.exp(first[0:1] - top) + second[1:2] * jnp.exp(second[0:1] - top)
+
+
+def merge(place, own, other):
+    return pl.pallas_call(
+        merge_kernel,
+        out_shape=jax.ShapeDtypeStruct(own.shape, F32),
+        in_specs=[SMEM, VMEM, VMEM],
+        out_specs=VMEM,
+        compiler_params=params(4),
+        cost_estimate=cost(0, 0),
+        name="merge",
+    )(place, own, other)
+
+
+def update_kernel(width, rows, span, place, shifts, terms, same, across, scales, *refs):
+    below, (out, product) = refs[:-2], refs[-2:]
+    for b in below:
+        high = b[...].astype(BF16).astype(F32)
+        both = high + pltpu.roll(b[...] - high, CYCLES, 1)
+        out[:, span * ANG :] = both[:rows].astype(BF16)
+    lower = place[2] == 0
+    images = [jnp.where(lower, a[...], b[...]) for a, b in ((same, across), (across, same))]
+    images = jnp.concatenate(images, axis=0).astype(F32)
+    scaled = (images * scales[:, 0:1]).astype(BF16)
+    product[...] = jnp.dot(terms[...], scaled, preferred_element_type=F32).astype(BF16)
     for j in range(span):
         here = slice(j * ANG, (j + 1) * ANG)
         total = jnp.zeros((width, ANG), F32)
@@ -222,83 +267,102 @@
         out[:, here] = total[:rows].astype(BF16)
 
 
-def update(width, rows, first, cycles, shifts, weights, images, after):
-    count = images.shape[0]
-    span = math.gcd(cycles, 8)
-    base = first // span
-    return pl.pallas_call(
-        later(functools.partial(update_kernel, width, rows, span), len(after)),
-        grid=(cycles // span,),
-        out_shape=jax.ShapeDtypeStruct((rows, cycles * ANG), BF16),
+def update(width, rows, first, cycles, place, shifts, terms, same, across, scales, below, after):
+    one = same.shape[0]
+    block = pl.BlockSpec((one, cycles * ANG), lambda i: (0, base))
+    base = first // cycles
+    whole = lambda a: pl.BlockSpec(a.shape, lambda i: (0, 0))
+    out = jax.ShapeDtypeStruct((rows, (cycles + len(below)) * ANG), BF16)
+    return pl.pallas_call(
+        later(functools.partial(update_kernel, width, rows, cycles), len(after)),
+        grid=(1,),
+        out_shape=out,
         in_specs=[ANY] * len(after)
         + [
             SMEM,
-            pl.BlockSpec(weights.shape, lambda i: (0, 0)),
-            pl.BlockSpec((count, span * ANG), lambda i: (0, base + i)),
-        ],
-        out_specs=pl.BlockSpec((rows, span * ANG), lambda i: (0, i)),
-        scratch_shapes=[pltpu.VMEM((ROT * width, span * ANG), BF16)],
-        compiler_params=params(LARGE),
+            SMEM,
+            whole(terms),
+            block,
+            block,
+            whole(scales),
+        ]
+        + [whole(b) for b in below],
+        out_specs=whole(out),
+        scratch_shapes=[pltpu.VMEM((ROT * width, cycles * ANG), BF16)],
+        compiler_params=params(20),
         cost_estimate=cost(3 * 2**30, 4 * 2**20),
         name="update",
-    )(*after, shifts, weights, images)
-
-
-def divide_kernel(first, one, two, one_below, two_below, out):
+    )(*after, place, shifts, terms, same, across, scales, *below)
+
+
+def divide_kernel(first, one, two, *refs):
+    share, out = refs[0], refs[-1]
     rows, span = out.shape
-    below = one_below[0:rows, :] + two_below[0:rows, :]
-    share = 1.0 / (below + PRIOR_WEIGHT)
-    lane = lax.broadcasted_iota(jnp.int32, share.shape, 1)
+    lane = lax.broadcasted_iota(jnp.int32, (rows, ANG), 1)
+    if len(refs) == 2 and first == 0:
+        below = one[:, span:].astype(F32) + two[:, span:].astype(F32)
+        below = below + pltpu.roll(below, ANG - CYCLES, 1)
+        share[...] = 1.0 / (below + PRIOR_WEIGHT)
     for j in range(span // ANG):
         here = slice(j * ANG, (j + 1) * ANG)
         total = one[:, here].astype(F32) + two[:, here].astype(F32)
-        cycle = jnp.where(lane == first + j, share, 0.0)
+        cycle = jnp.where(lane == first + j, share[...], 0.0)
         out[:, here] = (total * jnp.sum(cycle, axis=1, keepdims=True)).astype(BF16)
 
 
-def divide(first, one, two, one_below, two_below):
-    return pl.pallas_call(
-        functools.partial(divide_kernel, first),
-        out_shape=jax.ShapeDtypeStruct(one.shape, BF16),
-        in_specs=[VMEM] * 4,
-        out_specs=VMEM,
+def divide(first, cycles, one, two, share, after):
+    rows = one.shape[0]
+    outs = () if share else (jax.ShapeDtypeStruct((rows, ANG), F32),)
+    outs += (jax.ShapeDtypeStruct((rows, cycles * ANG), BF16),)
+    return pl.pallas_call(
+        later(functools.partial(divide_kernel, first), len(after)),
+        out_shape=outs,
+        in_specs=[ANY] * len(after) + [VMEM] * (2 + len(share)),
+        out_specs=(VMEM,) * len(outs),
         compiler_params=params(8),
-        cost_estimate=cost(2**30, 2**20),
+        cost_estimate=cost(2**28, 0),
         name="divide",
-    )(one, two, one_below, two_below)
-
-
-def blend_kernel(place, classes, mine, other, *refs):
+    )(*after, one, two, *share)
+
+
+def blend_kernel(chunks, place, classes, *refs):
     out = refs[-1]
-    total, span = classes.shape
-    width = mine.shape[0]
-    start, cut, _, _ = halves(total)
+    total = classes.shape[0]
+    start, cut, rows, _ = halves(total)
     upper = place[0] == 1
-    row = lax.broadcasted_iota(jnp.int32, (total, span), 0)
-    first, second = mine[...].astype(F32), other[...].astype(F32)
-    low = jnp.where(upper, second, first)
-    high = jnp.where(upper, first, second)
-    low_all = jnp.concatenate([low, jnp.zeros((total - width, span), F32)], axis=0)
-    high_all = jnp.concatenate([jnp.zeros((start, span), F32), high[: total - start]], axis=0)
-    step = jnp.where(row < cut, low_all, high_all)
-    out[...] = (1.0 - STEP_WEIGHT) * classes[...] + STEP_WEIGHT * step
-
-
-def blend(first, place, classes, mine, other, before):
-    span = mine.shape[1]
-    rows = pl.BlockSpec((classes.shape[0], span), lambda i: (0, first * ANG // span))
-    update = pl.BlockSpec(mine.shape, lambda i: (0, 0))
-    return pl.pallas_call(
-        blend_kernel,
+    at = 0
+    for p in range(chunks):
+        mine, other = refs[2 * p : 2 * p + 2]
+        span = mine.shape[1]
+        here = slice(at, at + span)
+        at += span
+        first, second = mine[...].astype(F32), other[...].astype(F32)
+        low = jnp.where(upper, second, first)
+        high = jnp.where(upper, first, second)
+        low = jnp.concatenate([low, jnp.zeros((total - rows, span), F32)], axis=0)
+        high = jnp.concatenate([jnp.zeros((start, span), F32), high[: total - start]], axis=0)
+        row = lax.broadcasted_iota(jnp.int32, (total, span), 0)
+        step = jnp.where(row < cut, low, high)
+        out[:, here] = (1.0 - STEP_WEIGHT) * classes[:, here] + STEP_WEIGHT * step
+
+
+def blend(first, place, classes, updates, before):
+    span = sum(mine.shape[1] for mine, _ in updates)
+    block = pl.BlockSpec((classes.shape[0], span), lambda i: (0, first * ANG // span))
+    flat = [u for pair in updates for u in pair]
+    return pl.pallas_call(
+        functools.partial(blend_kernel, len(updates)),
         grid=(1,),
         out_shape=jax.ShapeDtypeStruct(classes.shape, F32),
-        in_specs=[SMEM, rows, update, update] + [ANY] * len(before),
-        out_specs=rows,
-        input_output_aliases={4: 0} if before else {},
+        in_specs=[SMEM, block]
+        + [pl.BlockSpec(u.shape, lambda i: (0, 0)) for u in flat]
+        + [ANY] * len(before),
+        out_specs=block,
+        input_output_aliases={2 + len(flat): 0} if before else {},
         compiler_params=params(),
         cost_estimate=cost(2**30, 2**20),
         name="blend",
-    )(place, classes, mine, other, *before)
+    )(place, classes, *flat, *before)
 
 
 def halved(pool, picks, groups, ctf_table, shifts, classes, log_prior):
@@ -307,19 +371,21 @@
     axes = ("particle", "cls")
     z, cls = lax.axis_index("particle"), lax.axis_index("cls")
     chip, core = cls // 2, cls % 2
-    half = jnp.where((z == 1) | (z == 2), 1, 0)
+    half = z % 2
     place = jnp.stack([half, half * 2 + chip, core]).astype(jnp.int32)
     prior = jnp.pad(log_prior, (0, ANG - total)).reshape(1, ANG)
 
     def swap(a, mask):
         return lax.ppermute(a, axes, [(i, i ^ mask) for i in range(16)])
 
-    CORE, CHIP, NEXT, SAME = 1, 2, 4, 12
+    CORE, CHIP, NEXT, SAME = 1, 2, 4, 8
 
     own = weigh(picks, groups, pool, ctf_table)
     beside = swap(own, NEXT)
     own_x = swap(own, CHIP)
-    beside_x = swap(beside, CHIP)
+    beside_x = swap(own, NEXT + CHIP)
+    halved, power, column = prepare(width, place, classes, prior, (own,))
+    own_x, beside, beside_x, halved = lax.optimization_barrier((own_x, beside, beside_x, halved))
     pairs = [
         (jnp.where(chip == 1, x, a), jnp.where(chip == 1, a, x))
         for a, x in ((own, own_x), (beside, beside_x))
@@ -330,33 +396,41 @@
     same = jnp.concatenate(low + high, axis=0)
     across = swap(same, CORE)
 
-    logits, stat, images = score(width, place, shifts, prior, classes, same, across)
-
-    stat_core = swap(stat, CORE)
-    first = jnp.where(core == 0, stat, stat_core)
-    second = jnp.where(core == 0, stat_core, stat)
-    top = jnp.maximum(first[0], second[0])
-    both = first[1] * jnp.exp(first[0] - top) + second[1] * jnp.exp(second[0] - top)
-    stat = jnp.concatenate([top[None], both[None], stat[2:]], axis=0)
+    terms, summed, own_stat, squares = score(
+        width, place, shifts, halved, power, column, same, across
+    )
+
+    stat = merge(place, own_stat, swap(own_stat, CORE))
     stats = [stat] + [swap(stat, m) for m in (CHIP, NEXT, NEXT + CHIP)]
-    weights, evidence, below = weigh_classes(width, place, logits, images, stats)
-    other_below = swap(below, SAME)
-
-    mine, other, ratios, others, firsts = [], [], [], [], []
+    scales, evidence, below = normalize(place, own_stat, summed, squares, stats)
+
+    mine, other, ratios, others, share = [], [], [], [], []
+    last = len(CHUNKS) - 1
+    firsts = [sum(CHUNKS[:p]) for p in range(len(CHUNKS))]
+
+    def finish(p):
+        after = tuple(ratios[-1:])
+        *new, ratio = divide(firsts[p], CHUNKS[p], mine[p], other[p], tuple(share), after)
+        share.extend(new)
+        ratios.append(ratio)
+        others.append(swap(ratios[p], NEXT))
+
     for p, cycles in enumerate(CHUNKS):
-        firsts.append(sum(CHUNKS[:p]))
-        after = tuple(mine[-1:]) + tuple(ratios[: p - 1][-1:] if p > 1 else ())
-        mine.append(update(width, rows, firsts[p], cycles, shifts, weights, images, after))
-        other.append(swap(mine[p], SAME))
-        ratios.append(divide(firsts[p], mine[p], other[p], below, other_below))
-        others.append(swap(ratios[p], NEXT))
-    updated = ()
-    for p in range(len(CHUNKS)):
-        updated = (blend(firsts[p], place, classes, ratios[p], others[p], updated),)
+        after, extra = tuple(mine[-1:]), () if p else (below,)
+        part = update(
+            width, rows, firsts[p], cycles, place, shifts, terms, same, across, scales, extra, after
+        )
+        mine.append(part)
+        other.append(swap(part, SAME))
+    for p in range(last + 1):
+        finish(p)
+    both = list(zip(ratios, others))
+    updated = blend(0, place, classes, both[:last], ())
+    updated = blend(firsts[last], place, classes, both[last:], (updated,))
     count = picks.shape[0]
     by_shard = evidence[0].reshape(2, 2, 2, count)
     log_evidence = jnp.take(by_shard, z % 2, axis=1)
-    return (updated[0], jnp.transpose(log_evidence, (1, 0, 2)).reshape(4 * count))
+    return (updated, jnp.transpose(log_evidence, (1, 0, 2)).reshape(4 * count))
 
 
 def joined(part, axis, combine):

time: 84.6 us -> 72.2 us (0.85)
  waiting for transfers between devices: 23.2 us -> 18.4 us
  local copies, waits for them, and re-layouts: 7.99 us -> 3.37 us
  starting transfers between devices: 23.4 us -> 19.7 us
    unnamed x22 -> x18, local copies, waits for them, and re-layouts: 7.28 us -> 1.52 us
    ppermute x17 -> x16, waiting for transfers between devices: 23.2 us -> 18.4 us  [swap(): return lax.ppermute(a, axes, [(i, i ^ mask) for i in range(16)])]
    ppermute x17 -> x16, starting transfers between devices: 23.4 us -> 19.7 us  [swap(): return lax.ppermute(a, axes, [(i, i ^ mask) for i in range(16)])]
    pallas_call x1, Pallas kernels: 10.4 us -> 8.58 us  [score(): pl.pallas_call(functools.partial(score_kernel, width, groups, span), out_...]
    pallas_call x1, Pallas kernels: 0.46 us -> 2.16 us  [weigh(): pl.pallas_call(weigh_kernel, out_shape=jax.ShapeDtypeStruct((count, PIX +...]
    reshape x1, local copies, waits for them, and re-layouts: 0.01 us -> 1.14 us  [halved(): prior = jnp.pad(log_prior, (0, ANG - total)).reshape(1, ANG)]
  transfers between devices with their start and end apart: 17 -> 16, of which waited for: 11 -> 11; matrix products, arithmetic and copies ran while one was open for 1% -> 3% of each run, Pallas kernels for 11% -> 18%
where the time goes in v3:
time: 72.2 us; the launch traced here: 71.8 us
  Pallas kernels  28.7 us (40%)
  starting transfers between devices  19.7 us (27%)
  waiting for transfers between devices  18.4 us (25%)
  local copies, waits for them, and re-layouts  3.37 us (5%)
  other arithmetic  0.8 us (1%)
  between operations  0.8 us (1%)
    ppermute x16, starting transfers between devices, swap(): return lax.ppermute(a, axes, [(i, i ^ mask) for i in range(16)])  19.7 us
    ppermute x16, waiting for transfers between devices, swap(): return lax.ppermute(a, axes, [(i, i ^ mask) for i in range(16)])  18.4 us
    pallas_call x4, Pallas kernels, update(): pl.pallas_call(later(functools.partial(update_kernel, width, rows, cycles...  10.2 us
    pallas_call x1, Pallas kernels, score(): pl.pallas_call(functools.partial(score_kernel, width, groups, span), out_...  8.58 us
    pallas_call x2, Pallas kernels, blend(): pl.pallas_call(functools.partial(blend_kernel, len(updates)), grid=(1,),...  3.26 us
    pallas_call x1, Pallas kernels, prepare(): pl.pallas_call(later(functools.partial(prepare_kernel, width), len(after)...  2.51 us
    pallas_call x1, Pallas kernels, weigh(): pl.pallas_call(weigh_kernel, out_shape=jax.ShapeDtypeStruct((count, PIX +...  2.16 us
    unnamed x18, local copies, waits for them, and re-layouts  1.52 us
  transfers between devices with their start and end apart: 16, of which 11 were waited for; matrix products, arithmetic and copies ran while one was open for 3% of the time, Pallas kernels for 18%

profile of v3, /device:TPU:0, one launch (start us, length us, event | category | flops | bytes accessed | tf_op | source)
XLA Modules:
  0.0 71.8 jit_solution(4671682182593978814)
XLA Ops:
  0.6 2.2 %weigh.1.refs_0_ = bf16[24,4224]{1,0:T(8,128)(2,1)} custom-call(s32[1,24]{1,0:T(1,128)} %bitcast.17, s32[1,24]{1,0:T(1,128)} %bitcast.18, bf16[48,4096]{1,0:T(8,128)(2,1)} %pool.1, f32[32,64]{1,0:T(8,128)} %bitcast.16), custom_call_target="tpu_custom_call" | custom-call | flops 9437184 | bytes 1048576 | tf_op jit(solution)/shard_map/weigh/pallas_call | solution.py:66
  2.8 4.0 %collective-permute-start.2 = (bf16[24,4224]{1,0:T(8,128)(2,1)}, bf16[24,4224]{1,0:T(8,128)(2,1)S(1)}, u32[]{:S(2)}, u32[]{:S(2)}) collective-permute-start(bf16[24,4224]{1,0:T(8,128)(2,1)} %weigh.1.refs_0_), channel_id=1, source_target_pairs={{0,6},{1,7},{2,4},{3,5},{4,2},{5,3},{6,0},{7,1},{8,14},{9,15},{10,... | collective-permute-start | bytes 608264 | tf_op jit(solution)/shard_map/ppermute | solution.py:379
  7.3 1.1 %pad_bitcast_fusion.refs_3_ = f32[1,128]{1,0:T(1,128)} fusion(f32[100]{0:T(128)} %param.13), kind=kLoop, calls=%fused_computation.13 | loop fusion | bytes 912 | tf_op jit(solution)/shard_map/reshape | solution.py:376
  9.1 2.5 %prepare.1 = (bf16[64,4096]{1,0:T(8,128)(2,1)}, f32[64,128]{1,0:T(8,128)}, f32[64,128]{1,0:T(8,128)}) custom-call(bf16[24,4224]{1,0:T(8,128)(2,1)} %weigh.1.refs_0_, s32[3]{0:T(128)} %pad_add_fusion.refs_1_.place.refs_0_, f32[100,4096]{1,0:T(8,128)} %classes.3, f32[1,128]{1,0:T(1,128)} %pad_bitcast_fusion.refs_3_), custom_call_target="tpu_custom_call" | custom-call | flops 2147483648 | bytes 2097152 | tf_op jit(solution)/shard_map/prepare/pallas_call | solution.py:102
  11.6 1.2 %collective-permute-done.2 = bf16[24,4224]{1,0:T(8,128)(2,1)S(1)} collective-permute-done((bf16[24,4224]{1,0:T(8,128)(2,1)}, bf16[24,4224]{1,0:T(8,128)(2,1)S(1)}, u32[]{:S(2)}, u32[]{:S(2)}) %collective-permute-start.2) | collective-permute-done | bytes 202784 | tf_op jit(solution)/shard_map/ppermute | solution.py:379
  12.9 3.7 %collective-permute-done.1 = bf16[24,4224]{1,0:T(8,128)(2,1)S(1)} collective-permute-done((bf16[24,4224]{1,0:T(8,128)(2,1)}, bf16[24,4224]{1,0:T(8,128)(2,1)S(1)}, u32[]{:S(2)}, u32[]{:S(2)}) %collective-permute-start.1) | collective-permute-done | bytes 202784 | tf_op jit(solution)/shard_map/ppermute | solution.py:379
  16.8 2.3 %collective-permute-done.3.across.refs_4_.refs_5_ = bf16[96,4224]{1,0:T(8,128)(2,1)S(1)} collective-permute-done((bf16[96,4224]{1,0:T(8,128)(2,1)S(1)}, bf16[96,4224]{1,0:T(8,128)(2,1)S(1)}, u32[]{:S(2)}, u32[]{:S(2)}) %collective-permute-start.3) | collective-permute-done | bytes 811040 | tf_op jit(solution)/shard_map/ppermute | solution.py:379
  19.2 8.6 %score.1 = (bf16[2304,192]{1,0:T(8,128)(2,1)S(1)}, f32[64,192]{1,0:T(8,128)S(1)}, f32[8,192]{1,0:T(8,128)S(1)}, f32[192,128]{1,0:T(8,128)S(1)}) custom-call(s32[3]{0:T(128)S(1)} %copy-done.1, s32[36]{0:T(128)S(1)} %copy-done.2, bf16[64,4096]{1,0:T(8,128)(2,1)S(1)} %copy-done.5, f32[64,128]{1,0:T(8,128)S(1)} %copy-done.6, f32[64,128]{1,0:T(8,128)S(1)} %copy-done.7, ...), custom_call_target="tpu_custom_call" | custom-call | flops 10737418240 | bytes 20971520 | tf_op jit(solution)/shard_map/score/pallas_call | solution.py:180
  30.5 2.5 %collective-permute-start.7 = (f32[8,192]{1,0:T(8,128)S(1)}, f32[8,192]{1,0:T(8,128)S(1)}, u32[]{:S(2)}, u32[]{:S(2)}) collective-permute-start(f32[8,192]{1,0:T(8,128)S(1)} %merge.1.refs_0_), channel_id=1, source_target_pairs={{0,6},{1,7},{2,4},{3,5},{4,2},{5,3},{6,0},{7,1},{8,14},{9,15},{10,... | collective-permute-start | bytes 18440 | tf_op jit(solution)/shard_map/ppermute | solution.py:379
  34.1 1.1 %collective-permute-done.7.refs_3_ = f32[8,192]{1,0:T(8,128)S(1)} collective-permute-done((f32[8,192]{1,0:T(8,128)S(1)}, f32[8,192]{1,0:T(8,128)S(1)}, u32[]{:S(2)}, u32[]{:S(2)}) %collective-permute-start.7) | collective-permute-done | bytes 6176 | tf_op jit(solution)/shard_map/ppermute | solution.py:379
  35.1 1.5 %collective-permute-done.6.refs_2_ = f32[8,192]{1,0:T(8,128)S(1)} collective-permute-done((f32[8,192]{1,0:T(8,128)S(1)}, f32[8,192]{1,0:T(8,128)S(1)}, u32[]{:S(2)}, u32[]{:S(2)}) %collective-permute-start.6) | collective-permute-done | bytes 6176 | tf_op jit(solution)/shard_map/ppermute | solution.py:379
  38.4 2.5 %update.4.refs_0_ = bf16[56,1152]{1,0:T(8,128)(2,1)S(1)} custom-call(s32[3]{0:T(128)S(1)} %copy-done.1, s32[36]{0:T(128)S(1)} %copy-done.2, bf16[2304,192]{1,0:T(8,128)(2,1)S(1)} %copy-done.4, bf16[96,4224]{1,0:T(8,128)(2,1)S(1)} %pad_maximum_fusion.same.refs_3_.refs_4_, bf16[96,4224]{1,0:T(8,128)(2,1)S(1)} %collective-permute-done.3.across.refs_4_.refs_5_, ...), custom_call_target="tpu_custom_call" | custom-call | flops 3221225472 | bytes 4194304 | tf_op jit(solution)/shard_map/update/pallas_call | solution.py:276
  40.9 2.7 %collective-permute-start.8 = (bf16[56,1152]{1,0:T(8,128)(2,1)S(1)}, bf16[56,1152]{1,0:T(8,128)(2,1)S(1)}, u32[]{:S(2)}, u32[]{:S(2)}) collective-permute-start(bf16[56,1152]{1,0:T(8,128)(2,1)S(1)} %update.4.refs_0_), channel_id=1, source_target_pairs={{0,8},{1,9},{2,10},{3,11},{4,12},{5,13},{6,14},{7,15},{8,0},{9,1},... | collective-permute-start | bytes 387080 | tf_op jit(solution)/shard_map/ppermute | solution.py:379
  43.6 2.5 %update.5.refs_1_.refs_0_ = bf16[56,1024]{1,0:T(8,128)(2,1)S(1)} custom-call(bf16[56,1152]{1,0:T(8,128)(2,1)S(1)} %update.4.refs_0_, s32[3]{0:T(128)S(1)} %copy-done.1, s32[36]{0:T(128)S(1)} %copy-done.2, bf16[2304,192]{1,0:T(8,128)(2,1)S(1)} %copy-done.4, bf16[96,4224]{1,0:T(8,128)(2,1)S(1)} %pad_maximum_fusion.same.refs_3_.refs_4_, ...), custom_call_target="tpu_custom_call" | custom-call | flops 3221225472 | bytes 4194304 | tf_op jit(solution)/shard_map/update/pallas_call | solution.py:276
  46.5 2.5 %update.6.refs_1_.refs_0_ = bf16[56,1024]{1,0:T(8,128)(2,1)S(1)} custom-call(bf16[56,1024]{1,0:T(8,128)(2,1)S(1)} %update.5.refs_1_.refs_0_, s32[3]{0:T(128)S(1)} %copy-done.1, s32[36]{0:T(128)S(1)} %copy-done.2, bf16[2304,192]{1,0:T(8,128)(2,1)S(1)} %copy-done.4, bf16[96,4224]{1,0:T(8,128)(2,1)S(1)} %pad_maximum_fusion.same.refs_3_.refs_4_, ...), custom_call_target="tpu_custom_call" | custom-call | flops 3221225472 | bytes 4194304 | tf_op jit(solution)/shard_map/update/pallas_call | solution.py:276
  49.1 2.6 %collective-permute-start.10 = (bf16[56,1024]{1,0:T(8,128)(2,1)S(1)}, bf16[56,1024]{1,0:T(8,128)(2,1)S(1)}, u32[]{:S(2)}, u32[]{:S(2)}) collective-permute-start(bf16[56,1024]{1,0:T(8,128)(2,1)S(1)} %update.6.refs_1_.refs_0_), channel_id=1, source_target_pairs={{0,8},{1,9},{2,10},{3,11},{4,12},{5,13},{6,14},{7,15},{8,0},{9,1},... | collective-permute-start | bytes 344072 | tf_op jit(solution)/shard_map/ppermute | solution.py:379
  51.7 2.5 %update.7.refs_1_ = bf16[56,1024]{1,0:T(8,128)(2,1)S(1)} custom-call(bf16[56,1024]{1,0:T(8,128)(2,1)S(1)} %update.6.refs_1_.refs_0_, s32[3]{0:T(128)S(1)} %copy-done.1, s32[36]{0:T(128)S(1)} %copy-done.2, bf16[2304,192]{1,0:T(8,128)(2,1)S(1)} %copy-done.4, bf16[96,4224]{1,0:T(8,128)(2,1)S(1)} %pad_maximum_fusion.same.refs_3_.refs_4_, ...), custom_call_target="tpu_custom_call" | custom-call | flops 3221225472 | bytes 4194304 | tf_op jit(solution)/shard_map/update/pallas_call | solution.py:276
  55.0 1.6 %collective-permute-start.13 = (bf16[56,1024]{1,0:T(8,128)(2,1)S(1)}, bf16[56,1024]{1,0:T(8,128)(2,1)S(1)}, u32[]{:S(2)}, u32[]{:S(2)}) collective-permute-start(bf16[56,1024]{1,0:T(8,128)(2,1)S(1)} %get-tuple-element.31.refs_0_), channel_id=1, source_target_pairs={{0,4},{1,5},{2,6},{3,7},{4,0},{5,1},{6,2},{7,3},{8,12},{9,13},{10,... | collective-permute-start | bytes 344072 | tf_op jit(solution)/shard_map/ppermute | solution.py:379
  56.7 1.5 %collective-permute-done.9.refs_2_ = bf16[56,1024]{1,0:T(8,128)(2,1)S(1)} collective-permute-done((bf16[56,1024]{1,0:T(8,128)(2,1)S(1)}, bf16[56,1024]{1,0:T(8,128)(2,1)S(1)}, u32[]{:S(2)}, u32[]{:S(2)}) %collective-permute-start.9) | collective-permute-done | bytes 114720 | tf_op jit(solution)/shard_map/ppermute | solution.py:379
  58.3 2.0 %collective-permute-start.14 = (bf16[56,1024]{1,0:T(8,128)(2,1)S(1)}, bf16[56,1024]{1,0:T(8,128)(2,1)S(1)}, u32[]{:S(2)}, u32[]{:S(2)}) collective-permute-start(bf16[56,1024]{1,0:T(8,128)(2,1)S(1)} %divide.5.refs_0_.refs_2_), channel_id=1, source_target_pairs={{0,4},{1,5},{2,6},{3,7},{4,0},{5,1},{6,2},{7,3},{8,12},{9,13},{10,... | collective-permute-start | bytes 344072 | tf_op jit(solution)/shard_map/ppermute | solution.py:379
  60.3 1.4 %collective-permute-done.10.refs_2_ = bf16[56,1024]{1,0:T(8,128)(2,1)S(1)} collective-permute-done((bf16[56,1024]{1,0:T(8,128)(2,1)S(1)}, bf16[56,1024]{1,0:T(8,128)(2,1)S(1)}, u32[]{:S(2)}, u32[]{:S(2)}) %collective-permute-start.10) | collective-permute-done | bytes 114720 | tf_op jit(solution)/shard_map/ppermute | solution.py:379
  64.7 3.7 %collective-permute-done.15.refs_5_ = bf16[56,1024]{1,0:T(8,128)(2,1)S(1)} collective-permute-done((bf16[56,1024]{1,0:T(8,128)(2,1)S(1)}, bf16[56,1024]{1,0:T(8,128)(2,1)S(1)}, u32[]{:S(2)}, u32[]{:S(2)}) %collective-permute-start.15) | collective-permute-done | bytes 114720 | tf_op jit(solution)/shard_map/ppermute | solution.py:379
  68.5 1.9 %blend.2.refs_2_ = f32[100,4096]{1,0:T(8,128)} custom-call(s32[3]{0:T(128)S(1)} %copy-done.1, f32[100,4096]{1,0:T(8,128)S(1)} %copy-done, bf16[56,1024]{1,0:T(8,128)(2,1)S(1)} %get-tuple-element.31.refs_0_, bf16[56,1024]{1,0:T(8,128)(2,1)S(1)} %collective-permute-done.13.refs_1_, bf16[56,1024]{1,0:T(8,128)(2,1)S(1)} %divide.5.refs_0_.refs_2_, ...), custom_call_target="tpu_custom_call" | custom-call | flops 1073741824 | bytes 1048576 | tf_op jit(solution)/shard_map/blend/pallas_call | solution.py:353
  70.4 1.4 %blend.3 = f32[100,4096]{1,0:T(8,128)} custom-call(s32[3]{0:T(128)S(1)} %copy-done.1, f32[100,4096]{1,0:T(8,128)S(1)} %copy-done, bf16[56,1024]{1,0:T(8,128)(2,1)S(1)} %divide.7.refs_0_, bf16[56,1024]{1,0:T(8,128)(2,1)S(1)} %collective-permute-done.12.refs_1_, f32[100,4096]{1,0:T(8,128)} %blend.2.refs_2_), custom_call_target="tpu_custom_call", output_to_operand_aliasing={{}: (4, {})} | custom-call | flops 1073741824 | bytes 1048576 | tf_op jit(solution)/shard_map/blend/pallas_call | solution.py:353
  (50 shorter events, 11.3 us)
Async XLA Ops:
  2.8 10.1 %collective-permute-start.2 = (bf16[24,4224]{1,0:T(8,128)(2,1)}, bf16[24,4224]{1,0:T(8,128)(2,1)S(1)}, u32[]{:S(2)}, u32[]{:S(2)}) collective-permute-start(bf16[24,4224]{1,0:T(8,128)(2,1)} %weigh.1.refs_0_), channel_id=1, source_target_pairs={{0,6},{1,7},{2,4},{3,5},{4,2},{5,3},{6,0},{7,1},{8,14},{9,15},{10,... | collective-permute-start | bytes 608264 | tf_op jit(solution)/shard_map/ppermute | solution.py:379
  6.7 9.8 %collective-permute-start.1 = (bf16[24,4224]{1,0:T(8,128)(2,1)}, bf16[24,4224]{1,0:T(8,128)(2,1)S(1)}, u32[]{:S(2)}, u32[]{:S(2)}) collective-permute-start(bf16[24,4224]{1,0:T(8,128)(2,1)} %weigh.1.refs_0_), channel_id=1, source_target_pairs={{0,4},{1,5},{2,6},{3,7},{4,0},{5,1},{6,2},{7,3},{8,12},{9,13},{10,... | collective-permute-start | bytes 608264 | tf_op jit(solution)/shard_map/ppermute | solution.py:379
  7.2 9.3 %collective-permute-start = (bf16[24,4224]{1,0:T(8,128)(2,1)}, bf16[24,4224]{1,0:T(8,128)(2,1)S(1)}, u32[]{:S(2)}, u32[]{:S(2)}) collective-permute-start(bf16[24,4224]{1,0:T(8,128)(2,1)} %weigh.1.refs_0_), channel_id=1, source_target_pairs={{0,2},{1,3},{2,0},{3,1},{4,6},{5,7},{6,4},{7,5},{8,10},{9,11},{10,... | collective-permute-start | bytes 608264 | tf_op jit(solution)/shard_map/ppermute | solution.py:379
  9.1 7.4 %copy-start.8 = (bf16[24,4224]{1,0:T(8,128)(2,1)S(1)}, bf16[24,4224]{1,0:T(8,128)(2,1)}, u32[]{:S(2)}) copy-start(bf16[24,4224]{1,0:T(8,128)(2,1)} %weigh.1.refs_0_) | copy-start | bytes 608260
  16.5 2.6 %copy-start.1 = (s32[3]{0:T(128)S(1)}, s32[3]{0:T(128)}, u32[]{:S(2)}) copy-start(s32[3]{0:T(128)} %pad_add_fusion.refs_1_.place.refs_0_) | copy-start | bytes 40
  16.6 2.6 %copy-start.2 = (s32[36]{0:T(128)S(1)}, s32[36]{0:T(128)}, u32[]{:S(2)}) copy-start(s32[36]{0:T(128)} %refs_2_.7) | copy-start | bytes 436
  16.6 2.6 %copy-start.5 = (bf16[64,4096]{1,0:T(8,128)(2,1)S(1)}, bf16[64,4096]{1,0:T(8,128)(2,1)}, u32[]{:S(2)}) copy-start(bf16[64,4096]{1,0:T(8,128)(2,1)} %get-tuple-element.19.halved) | copy-start | bytes 1572868
  16.6 2.6 %copy-start.6 = (f32[64,128]{1,0:T(8,128)S(1)}, f32[64,128]{1,0:T(8,128)}, u32[]{:S(2)}) copy-start(f32[64,128]{1,0:T(8,128)} %get-tuple-element.20.power) | copy-start | bytes 98308
  16.6 2.6 %copy-start.7 = (f32[64,128]{1,0:T(8,128)S(1)}, f32[64,128]{1,0:T(8,128)}, u32[]{:S(2)}) copy-start(f32[64,128]{1,0:T(8,128)} %get-tuple-element.21.column) | copy-start | bytes 98308
  16.7 2.4 %collective-permute-start.3 = (bf16[96,4224]{1,0:T(8,128)(2,1)S(1)}, bf16[96,4224]{1,0:T(8,128)(2,1)S(1)}, u32[]{:S(2)}, u32[]{:S(2)}) collective-permute-start(bf16[96,4224]{1,0:T(8,128)(2,1)S(1)} %pad_maximum_fusion.same.refs_3_.refs_4_), channel_id=1, source_target_pairs={{0,1},{1,0},{2,3},{3,2},{4,5},{5,4},{6,7},{7,6},{8,9},{9,8},{10,11... | collective-permute-start | bytes 2433032 | tf_op jit(solution)/shard_map/ppermute | solution.py:379
  28.8 1.2 %collective-permute-start.4 = (f32[8,192]{1,0:T(8,128)S(1)}, f32[8,192]{1,0:T(8,128)S(1)}, u32[]{:S(2)}, u32[]{:S(2)}) collective-permute-start(f32[8,192]{1,0:T(8,128)S(1)} %get-tuple-element.26.own), channel_id=1, source_target_pairs={{0,1},{1,0},{2,3},{3,2},{4,5},{5,4},{6,7},{7,6},{8,9},{9,8},{10,11... | collective-permute-start | bytes 18440 | tf_op jit(solution)/shard_map/ppermute | solution.py:379
  30.5 4.6 %collective-permute-start.7 = (f32[8,192]{1,0:T(8,128)S(1)}, f32[8,192]{1,0:T(8,128)S(1)}, u32[]{:S(2)}, u32[]{:S(2)}) collective-permute-start(f32[8,192]{1,0:T(8,128)S(1)} %merge.1.refs_0_), channel_id=1, source_target_pairs={{0,6},{1,7},{2,4},{3,5},{4,2},{5,3},{6,0},{7,1},{8,14},{9,15},{10,... | collective-permute-start | bytes 18440 | tf_op jit(solution)/shard_map/ppermute | solution.py:379
  33.0 3.7 %collective-permute-start.6 = (f32[8,192]{1,0:T(8,128)S(1)}, f32[8,192]{1,0:T(8,128)S(1)}, u32[]{:S(2)}, u32[]{:S(2)}) collective-permute-start(f32[8,192]{1,0:T(8,128)S(1)} %merge.1.refs_0_), channel_id=1, source_target_pairs={{0,4},{1,5},{2,6},{3,7},{4,0},{5,1},{6,2},{7,3},{8,12},{9,13},{10,... | collective-permute-start | bytes 18440 | tf_op jit(solution)/shard_map/ppermute | solution.py:379
  33.4 3.7 %collective-permute-start.5 = (f32[8,192]{1,0:T(8,128)S(1)}, f32[8,192]{1,0:T(8,128)S(1)}, u32[]{:S(2)}, u32[]{:S(2)}) collective-permute-start(f32[8,192]{1,0:T(8,128)S(1)} %merge.1.refs_0_), channel_id=1, source_target_pairs={{0,2},{1,3},{2,0},{3,1},{4,6},{5,7},{6,4},{7,5},{8,10},{9,11},{10,... | collective-permute-start | bytes 18440 | tf_op jit(solution)/shard_map/ppermute | solution.py:379
  37.1 1.3 %copy-start.4 = (bf16[2304,192]{1,0:T(8,128)(2,1)S(1)}, bf16[2304,192]{1,0:T(8,128)(2,1)}, u32[]{:S(2)}) copy-start(bf16[2304,192]{1,0:T(8,128)(2,1)} %copy-done.3) | copy-start | bytes 2654212
  40.9 13.9 %collective-permute-start.8 = (bf16[56,1152]{1,0:T(8,128)(2,1)S(1)}, bf16[56,1152]{1,0:T(8,128)(2,1)S(1)}, u32[]{:S(2)}, u32[]{:S(2)}) collective-permute-start(bf16[56,1152]{1,0:T(8,128)(2,1)S(1)} %update.4.refs_0_), channel_id=1, source_target_pairs={{0,8},{1,9},{2,10},{3,11},{4,12},{5,13},{6,14},{7,15},{8,0},{9,1},... | collective-permute-start | bytes 387080 | tf_op jit(solution)/shard_map/ppermute | solution.py:379
  46.1 12.1 %collective-permute-start.9 = (bf16[56,1024]{1,0:T(8,128)(2,1)S(1)}, bf16[56,1024]{1,0:T(8,128)(2,1)S(1)}, u32[]{:S(2)}, u32[]{:S(2)}) collective-permute-start(bf16[56,1024]{1,0:T(8,128)(2,1)S(1)} %update.5.refs_1_.refs_0_), channel_id=1, source_target_pairs={{0,8},{1,9},{2,10},{3,11},{4,12},{5,13},{6,14},{7,15},{8,0},{9,1},... | collective-permute-start | bytes 344072 | tf_op jit(solution)/shard_map/ppermute | solution.py:379
  49.1 12.6 %collective-permute-start.10 = (bf16[56,1024]{1,0:T(8,128)(2,1)S(1)}, bf16[56,1024]{1,0:T(8,128)(2,1)S(1)}, u32[]{:S(2)}, u32[]{:S(2)}) collective-permute-start(bf16[56,1024]{1,0:T(8,128)(2,1)S(1)} %update.6.refs_1_.refs_0_), channel_id=1, source_target_pairs={{0,8},{1,9},{2,10},{3,11},{4,12},{5,13},{6,14},{7,15},{8,0},{9,1},... | collective-permute-start | bytes 344072 | tf_op jit(solution)/shard_map/ppermute | solution.py:379
  54.3 9.0 %collective-permute-start.11 = (bf16[56,1024]{1,0:T(8,128)(2,1)S(1)}, bf16[56,1024]{1,0:T(8,128)(2,1)S(1)}, u32[]{:S(2)}, u32[]{:S(2)}) collective-permute-start(bf16[56,1024]{1,0:T(8,128)(2,1)S(1)} %update.7.refs_1_), channel_id=1, source_target_pairs={{0,8},{1,9},{2,10},{3,11},{4,12},{5,13},{6,14},{7,15},{8,0},{9,1},... | collective-permute-start | bytes 344072 | tf_op jit(solution)/shard_map/ppermute | solution.py:379
  55.0 13.5 %copy-start = (f32[100,4096]{1,0:T(8,128)S(1)}, f32[100,4096]{1,0:T(8,128)}, u32[]{:S(2)}) copy-start(f32[100,4096]{1,0:T(8,128)} %classes.3) | copy-start | bytes 4915204
  55.0 13.5 %collective-permute-start.13 = (bf16[56,1024]{1,0:T(8,128)(2,1)S(1)}, bf16[56,1024]{1,0:T(8,128)(2,1)S(1)}, u32[]{:S(2)}, u32[]{:S(2)}) collective-permute-start(bf16[56,1024]{1,0:T(8,128)(2,1)S(1)} %get-tuple-element.31.refs_0_), channel_id=1, source_target_pairs={{0,4},{1,5},{2,6},{3,7},{4,0},{5,1},{6,2},{7,3},{8,12},{9,13},{10,... | collective-permute-start | bytes 344072 | tf_op jit(solution)/shard_map/ppermute | solution.py:379
  58.3 10.2 %collective-permute-start.14 = (bf16[56,1024]{1,0:T(8,128)(2,1)S(1)}, bf16[56,1024]{1,0:T(8,128)(2,1)S(1)}, u32[]{:S(2)}, u32[]{:S(2)}) collective-permute-start(bf16[56,1024]{1,0:T(8,128)(2,1)S(1)} %divide.5.refs_0_.refs_2_), channel_id=1, source_target_pairs={{0,4},{1,5},{2,6},{3,7},{4,0},{5,1},{6,2},{7,3},{8,12},{9,13},{10,... | collective-permute-start | bytes 344072 | tf_op jit(solution)/shard_map/ppermute | solution.py:379
  61.8 6.7 %collective-permute-start.15 = (bf16[56,1024]{1,0:T(8,128)(2,1)S(1)}, bf16[56,1024]{1,0:T(8,128)(2,1)S(1)}, u32[]{:S(2)}, u32[]{:S(2)}) collective-permute-start(bf16[56,1024]{1,0:T(8,128)(2,1)S(1)} %divide.6.refs_0_.refs_4_), channel_id=1, source_target_pairs={{0,4},{1,5},{2,6},{3,7},{4,0},{5,1},{6,2},{7,3},{8,12},{9,13},{10,... | collective-permute-start | bytes 344072 | tf_op jit(solution)/shard_map/ppermute | solution.py:379
  63.4 6.9 %collective-permute-start.12 = (bf16[56,1024]{1,0:T(8,128)(2,1)S(1)}, bf16[56,1024]{1,0:T(8,128)(2,1)S(1)}, u32[]{:S(2)}, u32[]{:S(2)}) collective-permute-start(bf16[56,1024]{1,0:T(8,128)(2,1)S(1)} %divide.7.refs_0_), channel_id=1, source_target_pairs={{0,4},{1,5},{2,6},{3,7},{4,0},{5,1},{6,2},{7,3},{8,12},{9,13},{10,... | collective-permute-start | bytes 344072 | tf_op jit(solution)/shard_map/ppermute | solution.py:379
  (1 other events, 1.0 us)

commit v4 on v3

--- a/solution.py
+++ b/solution.py
@@ -27,6 +27,7 @@
 NEGATIVE = -1e30
 CHUNKS = (8, 8, 8, 8)
 LARGE = 58
+QUARTERS = 4
 
 
 def later(kernel, count):
@@ -34,9 +35,9 @@
 
 
 def halves(total):
-    start = total // 2 // 8 * 8
-    rows = -(-(total - start) // 8) * 8
-    return start, (start + rows) // 2, rows, -(-rows // 16) * 16
+    half = total // 2
+    full = half // 8 * 8
+    return half, full, half - full, -(-half // 16) * 16
 
 
 def cost(flops, moved):
@@ -77,25 +78,25 @@
 def prepare_kernel(width, place, classes, prior, halved, power, column):
     upper = place[0] == 1
     total = classes.shape[0]
-    start, cut, _, _ = halves(total)
-    pad = jnp.zeros((width - (total - start), ANG), F32)
+    half, full, rest, _ = halves(total)
+    pad = jnp.zeros((width - (total - full), ANG), F32)
     lane = lax.broadcasted_iota(jnp.int32, (width, ANG), 1)
+
+    def mine(low, high):
+        high = pltpu.roll(jnp.concatenate([high, pad], axis=0), width - rest, 0)
+        return jnp.where(upper, high, low)
+
     kept = jnp.zeros((width, ANG), F32)
     for c in range(CYCLES):
         here = slice(c * ANG, (c + 1) * ANG)
-        high = jnp.concatenate([classes[start:total, here], pad], axis=0)
-        mine = jnp.where(upper, high, classes[0:width, here]).astype(BF16)
-        halved[:, here] = mine
-        wide = mine.astype(F32)
+        part = mine(classes[0:width, here], classes[full:total, here]).astype(BF16)
+        halved[:, here] = part
+        wide = part.astype(F32)
         kept = jnp.where(lane == c, jnp.sum(wide * wide, axis=1, keepdims=True), kept)
     power[...] = kept
     turned = jnp.broadcast_to(prior[...], (ANG, ANG)).T
-    high = jnp.concatenate([turned[start:total, :], pad], axis=0)
     row = lax.broadcasted_iota(jnp.int32, (width, ANG), 0)
-    mine = (row >= jnp.where(upper, cut - start, 0)) & (
-        row < jnp.where(upper, total - start, cut)
-    )
-    column[...] = jnp.where(mine, jnp.where(upper, high, turned[0:width, :]), NEGATIVE)
+    column[...] = jnp.where(row < half, mine(turned[0:width], turned[full:total]), NEGATIVE)
 
 
 def prepare(width, place, classes, prior, after):
@@ -246,48 +247,50 @@
     )(place, own, other)
 
 
-def update_kernel(width, rows, span, place, shifts, terms, same, across, scales, *refs):
+def update_kernel(total, first, span, place, shifts, terms, same, across, scales, *refs):
     below, (out, product) = refs[:-2], refs[-2:]
-    for b in below:
-        high = b[...].astype(BF16).astype(F32)
-        both = high + pltpu.roll(b[...] - high, CYCLES, 1)
-        out[:, span * ANG :] = both[:rows].astype(BF16)
+    _, full, rest, width = halves(total)
+    wide = span // QUARTERS
+    sent = QUARTERS * full + 8
     lower = place[2] == 0
-    images = [jnp.where(lower, a[...], b[...]) for a, b in ((same, across), (across, same))]
+    part = slice(first * ANG, (first + span) * ANG)
+    images = [jnp.where(lower, a[:, part], b[:, part]) for a, b in ((same, across), (across, same))]
     images = jnp.concatenate(images, axis=0).astype(F32)
     scaled = (images * scales[:, 0:1]).astype(BF16)
     product[...] = jnp.dot(terms[...], scaled, preferred_element_type=F32).astype(BF16)
-    for j in range(span):
-        here = slice(j * ANG, (j + 1) * ANG)
-        total = jnp.zeros((width, ANG), F32)
-        for r in range(ROT):
-            back = (ANG - shifts[r]) & (ANG - 1)
-            turned = pltpu.roll(product[r * width : (r + 1) * width, here], back, 1)
-            total = total + turned.astype(F32)
-        out[:, here] = total[:rows].astype(BF16)
-
-
-def update(width, rows, first, cycles, place, shifts, terms, same, across, scales, below, after):
-    one = same.shape[0]
-    block = pl.BlockSpec((one, cycles * ANG), lambda i: (0, base))
-    base = first // cycles
-    whole = lambda a: pl.BlockSpec(a.shape, lambda i: (0, 0))
-    out = jax.ShapeDtypeStruct((rows, (cycles + len(below)) * ANG), BF16)
-    return pl.pallas_call(
-        later(functools.partial(update_kernel, width, rows, cycles), len(after)),
-        grid=(1,),
-        out_shape=out,
-        in_specs=[ANY] * len(after)
-        + [
-            SMEM,
-            SMEM,
-            whole(terms),
-            block,
-            block,
-            whole(scales),
-        ]
-        + [whole(b) for b in below],
-        out_specs=whole(out),
+    row = lax.broadcasted_iota(jnp.int32, (8, ANG), 0)
+    for i in range(wide):
+        there = slice(i * ANG, (i + 1) * ANG)
+        tail = jnp.zeros((8, ANG), F32)
+        for q in range(QUARTERS):
+            j = q * wide + i
+            sums = jnp.zeros((width, ANG), F32)
+            for r in range(ROT):
+                back = (ANG - shifts[r]) & (ANG - 1)
+                turned = pltpu.roll(
+                    product[r * width : (r + 1) * width, j * ANG : (j + 1) * ANG], back, 1
+                )
+                sums = sums + turned.astype(F32)
+            out[q * full : (q + 1) * full, there] = sums[:full].astype(BF16)
+            moved = pltpu.roll(sums[full : full + 8], q * rest, 0) if q else sums[full : full + 8]
+            tail = jnp.where((row >= q * rest) & (row < (q + 1) * rest), moved, tail)
+        out[sent - 8 : sent, there] = tail.astype(BF16)
+    for b in below:
+        value = b[0 : full + 8, :]
+        high = value.astype(BF16).astype(F32)
+        both = high + pltpu.roll(value - high, CYCLES, 1)
+        out[sent : sent + 32, 0:ANG] = both[0:32].astype(BF16)
+        out[sent : sent + 32, ANG : 2 * ANG] = both[full - 24 : full + 8].astype(BF16)
+
+
+def update(total, first, cycles, place, shifts, terms, same, across, scales, below, after):
+    _, full, _, width = halves(total)
+    rows = QUARTERS * full + 8 + 32 * len(below)
+    return pl.pallas_call(
+        later(functools.partial(update_kernel, total, first, cycles), len(after)),
+        out_shape=jax.ShapeDtypeStruct((rows, cycles // QUARTERS * ANG), BF16),
+        in_specs=[ANY] * len(after) + [SMEM, SMEM] + [VMEM] * (4 + len(below)),
+        out_specs=VMEM,
         scratch_shapes=[pltpu.VMEM((ROT * width, cycles * ANG), BF16)],
         compiler_params=params(20),
         cost_estimate=cost(3 * 2**30, 4 * 2**20),
@@ -295,27 +298,38 @@
     )(*after, place, shifts, terms, same, across, scales, *below)
 
 
-def divide_kernel(first, one, two, *refs):
+def divide_kernel(total, first, one, two, *refs):
     share, out = refs[0], refs[-1]
-    rows, span = out.shape
-    lane = lax.broadcasted_iota(jnp.int32, (rows, ANG), 1)
-    if len(refs) == 2 and first == 0:
-        below = one[:, span:].astype(F32) + two[:, span:].astype(F32)
+    _, full, rest, _ = halves(total)
+    sent, wide = out.shape[0], out.shape[1] // ANG
+    lane = lax.broadcasted_iota(jnp.int32, (full + 8, ANG), 1)
+    row = lax.broadcasted_iota(jnp.int32, (8, ANG), 0)
+    if first == 0:
+        below = one[sent:, :].astype(F32) + two[sent:, :].astype(F32)
+        below = jnp.concatenate([below[0:24, 0:ANG], below[32 - (full - 16) :, ANG:]], axis=0)
         below = below + pltpu.roll(below, ANG - CYCLES, 1)
         share[...] = 1.0 / (below + PRIOR_WEIGHT)
-    for j in range(span // ANG):
-        here = slice(j * ANG, (j + 1) * ANG)
-        total = one[:, here].astype(F32) + two[:, here].astype(F32)
-        cycle = jnp.where(lane == first + j, share[...], 0.0)
-        out[:, here] = (total * jnp.sum(cycle, axis=1, keepdims=True)).astype(BF16)
-
-
-def divide(first, cycles, one, two, share, after):
-    rows = one.shape[0]
-    outs = () if share else (jax.ShapeDtypeStruct((rows, ANG), F32),)
-    outs += (jax.ShapeDtypeStruct((rows, cycles * ANG), BF16),)
-    return pl.pallas_call(
-        later(functools.partial(divide_kernel, first), len(after)),
+    for i in range(wide):
+        there = slice(i * ANG, (i + 1) * ANG)
+        tail = jnp.zeros((8, ANG), F32)
+        for q in range(QUARTERS):
+            cycle = jnp.where(lane == first + q * wide + i, share[...], 0.0)
+            factor = jnp.broadcast_to(jnp.sum(cycle, axis=1, keepdims=True), (full + 8, ANG))
+            here = slice(q * full, (q + 1) * full)
+            sums = one[here, there].astype(F32) + two[here, there].astype(F32)
+            out[here, there] = (sums * factor[:full]).astype(BF16)
+            moved = pltpu.roll(factor[full:], q * rest, 0) if q else factor[full:]
+            tail = jnp.where((row >= q * rest) & (row < (q + 1) * rest), moved, tail)
+        sums = one[sent - 8 : sent, there].astype(F32) + two[sent - 8 : sent, there].astype(F32)
+        out[sent - 8 : sent, there] = (sums * tail).astype(BF16)
+
+
+def divide(total, first, cycles, one, two, share, after):
+    _, full, _, _ = halves(total)
+    outs = () if share else (jax.ShapeDtypeStruct((full + 8, ANG), F32),)
+    outs += (jax.ShapeDtypeStruct((QUARTERS * full + 8, cycles // QUARTERS * ANG), BF16),)
+    return pl.pallas_call(
+        later(functools.partial(divide_kernel, total, first), len(after)),
         out_shape=outs,
         in_specs=[ANY] * len(after) + [VMEM] * (2 + len(share)),
         out_specs=(VMEM,) * len(outs),
@@ -328,26 +342,31 @@
 def blend_kernel(chunks, place, classes, *refs):
     out = refs[-1]
     total = classes.shape[0]
-    start, cut, rows, _ = halves(total)
+    half, full, rest, _ = halves(total)
     upper = place[0] == 1
-    at = 0
+    span = refs[0].shape[1]
+    row = lax.broadcasted_iota(jnp.int32, (full + 16, span), 0)
+    none = jnp.zeros((8, span), F32)
     for p in range(chunks):
         mine, other = refs[2 * p : 2 * p + 2]
-        span = mine.shape[1]
-        here = slice(at, at + span)
-        at += span
-        first, second = mine[...].astype(F32), other[...].astype(F32)
-        low = jnp.where(upper, second, first)
-        high = jnp.where(upper, first, second)
-        low = jnp.concatenate([low, jnp.zeros((total - rows, span), F32)], axis=0)
-        high = jnp.concatenate([jnp.zeros((start, span), F32), high[: total - start]], axis=0)
-        row = lax.broadcasted_iota(jnp.int32, (total, span), 0)
-        step = jnp.where(row < cut, low, high)
-        out[:, here] = (1.0 - STEP_WEIGHT) * classes[:, here] + STEP_WEIGHT * step
+        ends = [a[QUARTERS * full :, :].astype(F32) for a in (mine, other)]
+        for q in range(QUARTERS):
+            rows = []
+            for a, end in zip((mine, other), ends):
+                end = pltpu.roll(end, 8 - q * rest, 0) if q else end
+                rows.append((a[q * full : (q + 1) * full, :].astype(F32), end))
+            low, low_end = (jnp.where(upper, b, a) for a, b in zip(*rows))
+            high, high_end = (jnp.where(upper, a, b) for a, b in zip(*rows))
+            high = pltpu.roll(jnp.concatenate([high, high_end, none], axis=0), rest, 0)
+            low_end = jnp.concatenate([low_end, jnp.zeros((full + 8, span), F32)], axis=0)
+            upper_rows = jnp.where(row < rest, low_end, high)
+            step = jnp.concatenate([low, upper_rows[: total - full]], axis=0)
+            at = slice((p * QUARTERS + q) * span, (p * QUARTERS + q + 1) * span)
+            out[:, at] = (1.0 - STEP_WEIGHT) * classes[:, at] + STEP_WEIGHT * step
 
 
 def blend(first, place, classes, updates, before):
-    span = sum(mine.shape[1] for mine, _ in updates)
+    span = QUARTERS * sum(mine.shape[1] for mine, _ in updates)
     block = pl.BlockSpec((classes.shape[0], span), lambda i: (0, first * ANG // span))
     flat = [u for pair in updates for u in pair]
     return pl.pallas_call(
@@ -367,7 +386,7 @@
 
 def halved(pool, picks, groups, ctf_table, shifts, classes, log_prior):
     total = classes.shape[0]
-    _, _, rows, width = halves(total)
+    width = halves(total)[-1]
     axes = ("particle", "cls")
     z, cls = lax.axis_index("particle"), lax.axis_index("cls")
     chip, core = cls // 2, cls % 2
@@ -410,7 +429,7 @@
 
     def finish(p):
         after = tuple(ratios[-1:])
-        *new, ratio = divide(firsts[p], CHUNKS[p], mine[p], other[p], tuple(share), after)
+        *new, ratio = divide(total, firsts[p], CHUNKS[p], mine[p], other[p], tuple(share), after)
         share.extend(new)
         ratios.append(ratio)
         others.append(swap(ratios[p], NEXT))
@@ -418,15 +437,16 @@
     for p, cycles in enumerate(CHUNKS):
         after, extra = tuple(mine[-1:]), () if p else (below,)
         part = update(
-            width, rows, firsts[p], cycles, place, shifts, terms, same, across, scales, extra, after
+            total, firsts[p], cycles, place, shifts, terms, same, across, scales, extra, after
         )
         mine.append(part)
         other.append(swap(part, SAME))
     for p in range(last + 1):
         finish(p)
     both = list(zip(ratios, others))
-    updated = blend(0, place, classes, both[:last], ())
-    updated = blend(firsts[last], place, classes, both[last:], (updated,))
+    cut = 2
+    updated = blend(0, place, classes, both[:cut], ())
+    updated = blend(firsts[cut], place, classes, both[cut:], (updated,))
     count = picks.shape[0]
     by_shard = evidence[0].reshape(2, 2, 2, count)
     log_evidence = jnp.take(by_shard, z % 2, axis=1)
@@ -551,6 +571,15 @@
     return (updated, log_evidence)
 
 
+def on_device(pool, picks, groups, ctf_table, shifts, classes, log_prior):
+    total = classes.shape[0]
+    _, full, rest, _ = halves(total)
+    quad = lax.axis_size("particle") == 4 and lax.axis_size("cls") == 4
+    fits = total % 2 == 0 and QUARTERS * rest <= 8 and 32 <= full <= 48 and total <= ANG
+    plan = halved if quad and fits else whole_sum
+    return plan(pool, picks, groups, ctf_table, shifts, classes, log_prior)
+
+
 def solution(mesh):
     in_specs = (
         P(("groups", "particle", "cls"), None),
@@ -562,7 +591,6 @@
         P(("groups", "cls")),
     )
     out_specs = (P(("groups", "cls"), None), P(("groups", "particle")))
-    quad = mesh.shape["particle"] == 4 and mesh.shape["cls"] == 4
     return jax.shard_map(
-        halved if quad else whole_sum, mesh=mesh, in_specs=in_specs, out_specs=out_specs, check_vma=False
-    )
+        on_device, mesh=mesh, in_specs=in_specs, out_specs=out_specs, check_vma=False
+    )

time: 72.2 us -> 69 us (0.956)
  waiting for transfers between devices: 18.4 us -> 16.9 us
  starting transfers between devices: 19.7 us -> 18.4 us
    ppermute x16, waiting for transfers between devices: 18.4 us -> 16.9 us  [swap(): return lax.ppermute(a, axes, [(i, i ^ mask) for i in range(16)])]
    ppermute x16, starting transfers between devices: 19.7 us -> 18.4 us  [swap(): return lax.ppermute(a, axes, [(i, i ^ mask) for i in range(16)])]
  transfers between devices with their start and end apart: 16 -> 16, of which waited for: 11 -> 11; matrix products, arithmetic and copies ran while one was open for 3% -> 4% of each run, Pallas kernels for 18% -> 18%
where the time goes in v4:
time: 69 us; the launch traced here: 68.8 us
  Pallas kernels  28.7 us (42%)
  starting transfers between devices  18.4 us (27%)
  waiting for transfers between devices  16.9 us (24%)
  local copies, waits for them, and re-layouts  3.16 us (5%)
  between operations  0.82 us (1%)
  other arithmetic  0.8 us (1%)
    ppermute x16, starting transfers between devices, swap(): return lax.ppermute(a, axes, [(i, i ^ mask) for i in range(16)])  18.4 us
    ppermute x16, waiting for transfers between devices, swap(): return lax.ppermute(a, axes, [(i, i ^ mask) for i in range(16)])  16.9 us
    pallas_call x4, Pallas kernels, update(): pl.pallas_call(later(functools.partial(update_kernel, total, first, cycle...  10.2 us
    pallas_call x1, Pallas kernels, score(): pl.pallas_call(functools.partial(score_kernel, width, groups, span), out_...  8.58 us
    pallas_call x2, Pallas kernels, blend(): pl.pallas_call(functools.partial(blend_kernel, len(updates)), grid=(1,),...  3.26 us
    pallas_call x1, Pallas kernels, prepare(): pl.pallas_call(later(functools.partial(prepare_kernel, width), len(after)...  2.54 us
    pallas_call x1, Pallas kernels, weigh(): pl.pallas_call(weigh_kernel, out_shape=jax.ShapeDtypeStruct((count, PIX +...  2.16 us
  transfers between devices with their start and end apart: 16, of which 11 were waited for; matrix products, arithmetic and copies ran while one was open for 4% of the time, Pallas kernels for 18%

profile of v4, /device:TPU:0, one launch (start us, length us, event | category | flops | bytes accessed | tf_op | source)
XLA Modules:
  0.0 68.8 jit_solution(14683357628440683720)
XLA Ops:
  0.6 2.2 %weigh.1.refs_0_ = bf16[24,4224]{1,0:T(8,128)(2,1)} custom-call(s32[1,24]{1,0:T(1,128)} %bitcast.17, s32[1,24]{1,0:T(1,128)} %bitcast.18, bf16[48,4096]{1,0:T(8,128)(2,1)} %pool.1, f32[32,64]{1,0:T(8,128)} %bitcast.16), custom_call_target="tpu_custom_call" | custom-call | flops 9437184 | bytes 1048576 | tf_op jit(solution)/shard_map/weigh/pallas_call | solution.py:67
  2.8 4.0 %collective-permute-start.2 = (bf16[24,4224]{1,0:T(8,128)(2,1)}, bf16[24,4224]{1,0:T(8,128)(2,1)S(1)}, u32[]{:S(2)}, u32[]{:S(2)}) collective-permute-start(bf16[24,4224]{1,0:T(8,128)(2,1)} %weigh.1.refs_0_), channel_id=1, source_target_pairs={{0,6},{1,7},{2,4},{3,5},{4,2},{5,3},{6,0},{7,1},{8,14},{9,15},{10,... | collective-permute-start | bytes 608264 | tf_op jit(solution)/shard_map/ppermute | solution.py:398
  7.3 1.1 %pad_bitcast_fusion.refs_3_ = f32[1,128]{1,0:T(1,128)} fusion(f32[100]{0:T(128)} %param.13), kind=kLoop, calls=%fused_computation.13 | loop fusion | bytes 912 | tf_op jit(solution)/shard_map/reshape | solution.py:395
  9.1 2.5 %prepare.1 = (bf16[64,4096]{1,0:T(8,128)(2,1)}, f32[64,128]{1,0:T(8,128)}, f32[64,128]{1,0:T(8,128)}) custom-call(bf16[24,4224]{1,0:T(8,128)(2,1)} %weigh.1.refs_0_, s32[3]{0:T(128)} %pad_add_fusion.refs_1_.place.refs_0_, f32[100,4096]{1,0:T(8,128)} %classes.3, f32[1,128]{1,0:T(1,128)} %pad_bitcast_fusion.refs_3_), custom_call_target="tpu_custom_call" | custom-call | flops 2147483648 | bytes 2097152 | tf_op jit(solution)/shard_map/prepare/pallas_call | solution.py:103
  11.6 1.2 %collective-permute-done.2 = bf16[24,4224]{1,0:T(8,128)(2,1)S(1)} collective-permute-done((bf16[24,4224]{1,0:T(8,128)(2,1)}, bf16[24,4224]{1,0:T(8,128)(2,1)S(1)}, u32[]{:S(2)}, u32[]{:S(2)}) %collective-permute-start.2) | collective-permute-done | bytes 202784 | tf_op jit(solution)/shard_map/ppermute | solution.py:398
  12.9 3.7 %collective-permute-done.1 = bf16[24,4224]{1,0:T(8,128)(2,1)S(1)} collective-permute-done((bf16[24,4224]{1,0:T(8,128)(2,1)}, bf16[24,4224]{1,0:T(8,128)(2,1)S(1)}, u32[]{:S(2)}, u32[]{:S(2)}) %collective-permute-start.1) | collective-permute-done | bytes 202784 | tf_op jit(solution)/shard_map/ppermute | solution.py:398
  16.8 2.3 %collective-permute-done.3.across.refs_4_.refs_5_ = bf16[96,4224]{1,0:T(8,128)(2,1)S(1)} collective-permute-done((bf16[96,4224]{1,0:T(8,128)(2,1)S(1)}, bf16[96,4224]{1,0:T(8,128)(2,1)S(1)}, u32[]{:S(2)}, u32[]{:S(2)}) %collective-permute-start.3) | collective-permute-done | bytes 811040 | tf_op jit(solution)/shard_map/ppermute | solution.py:398
  19.2 8.6 %score.1 = (bf16[2304,192]{1,0:T(8,128)(2,1)S(1)}, f32[64,192]{1,0:T(8,128)S(1)}, f32[8,192]{1,0:T(8,128)S(1)}, f32[192,128]{1,0:T(8,128)S(1)}) custom-call(s32[3]{0:T(128)S(1)} %copy-done.1, s32[36]{0:T(128)S(1)} %copy-done.2, bf16[64,4096]{1,0:T(8,128)(2,1)S(1)} %copy-done.5, f32[64,128]{1,0:T(8,128)S(1)} %copy-done.6, f32[64,128]{1,0:T(8,128)S(1)} %copy-done.7, ...), custom_call_target="tpu_custom_call" | custom-call | flops 10737418240 | bytes 20971520 | tf_op jit(solution)/shard_map/score/pallas_call | solution.py:181
  29.6 2.5 %collective-permute-start.7 = (f32[8,192]{1,0:T(8,128)S(1)}, f32[8,192]{1,0:T(8,128)S(1)}, u32[]{:S(2)}, u32[]{:S(2)}) collective-permute-start(f32[8,192]{1,0:T(8,128)S(1)} %merge.1.refs_0_), channel_id=1, source_target_pairs={{0,6},{1,7},{2,4},{3,5},{4,2},{5,3},{6,0},{7,1},{8,14},{9,15},{10,... | collective-permute-start | bytes 18440 | tf_op jit(solution)/shard_map/ppermute | solution.py:398
  34.2 1.5 %collective-permute-done.6.refs_2_ = f32[8,192]{1,0:T(8,128)S(1)} collective-permute-done((f32[8,192]{1,0:T(8,128)S(1)}, f32[8,192]{1,0:T(8,128)S(1)}, u32[]{:S(2)}, u32[]{:S(2)}) %collective-permute-start.6) | collective-permute-done | bytes 6176 | tf_op jit(solution)/shard_map/ppermute | solution.py:398
  36.9 2.6 %update.4.refs_0_ = bf16[232,256]{1,0:T(8,128)(2,1)S(1)} custom-call(s32[3]{0:T(128)S(1)} %copy-done.1, s32[36]{0:T(128)S(1)} %copy-done.2, bf16[2304,192]{1,0:T(8,128)(2,1)S(1)} %get-tuple-element.25.refs_2_.refs_3_, bf16[96,4224]{1,0:T(8,128)(2,1)S(1)} %pad_maximum_fusion.same.refs_3_.refs_4_, ...), custom_call_target="tpu_custom_call" | custom-call | flops 3221225472 | bytes 4194304 | tf_op jit(solution)/shard_map/update/pallas_call | solution.py:289
  39.5 2.7 %collective-permute-start.8 = (bf16[232,256]{1,0:T(8,128)(2,1)S(1)}, bf16[232,256]{1,0:T(8,128)(2,1)S(1)}, u32[]{:S(2)}, u32[]{:S(2)}) collective-permute-start(bf16[232,256]{1,0:T(8,128)(2,1)S(1)} %update.4.refs_0_), channel_id=1, source_target_pairs={{0,8},{1,9},{2,10},{3,11},{4,12},{5,13},{6,14},{7,15},{8,0},{9,1},... | collective-permute-start | bytes 356360 | tf_op jit(solution)/shard_map/ppermute | solution.py:398
  42.2 1.3 %copy-done.4 = bf16[2304,192]{1,0:T(8,128)(2,1)S(1)} copy-done((bf16[2304,192]{1,0:T(8,128)(2,1)S(1)}, bf16[2304,192]{1,0:T(8,128)(2,1)}, u32[]{:S(2)}) %copy-start.4) | copy-done | bytes 884760
  43.4 2.6 %update.5.refs_1_.refs_0_ = bf16[200,256]{1,0:T(8,128)(2,1)S(1)} custom-call(bf16[232,256]{1,0:T(8,128)(2,1)S(1)} %update.4.refs_0_, s32[3]{0:T(128)S(1)} %copy-done.1, s32[36]{0:T(128)S(1)} %copy-done.2, bf16[2304,192]{1,0:T(8,128)(2,1)S(1)} %copy-done.4, bf16[96,4224]{1,0:T(8,128)(2,1)S(1)} %pad_maximum_fusion.same.refs_3_.refs_4_, ...), custom_call_target="tpu_custom_call" | custom-call | flops 3221225472 | bytes 4194304 | tf_op jit(solution)/shard_map/update/pallas_call | solution.py:289
  46.4 2.6 %update.6.refs_1_.refs_0_ = bf16[200,256]{1,0:T(8,128)(2,1)S(1)} custom-call(bf16[200,256]{1,0:T(8,128)(2,1)S(1)} %update.5.refs_1_.refs_0_, s32[3]{0:T(128)S(1)} %copy-done.1, s32[36]{0:T(128)S(1)} %copy-done.2, bf16[2304,192]{1,0:T(8,128)(2,1)S(1)} %copy-done.4, bf16[96,4224]{1,0:T(8,128)(2,1)S(1)} %pad_maximum_fusion.same.refs_3_.refs_4_, ...), custom_call_target="tpu_custom_call" | custom-call | flops 3221225472 | bytes 4194304 | tf_op jit(solution)/shard_map/update/pallas_call | solution.py:289
  49.0 2.7 %collective-permute-start.10 = (bf16[200,256]{1,0:T(8,128)(2,1)S(1)}, bf16[200,256]{1,0:T(8,128)(2,1)S(1)}, u32[]{:S(2)}, u32[]{:S(2)}) collective-permute-start(bf16[200,256]{1,0:T(8,128)(2,1)S(1)} %update.6.refs_1_.refs_0_), channel_id=1, source_target_pairs={{0,8},{1,9},{2,10},{3,11},{4,12},{5,13},{6,14},{7,15},{8,0},{9,1},... | collective-permute-start | bytes 307208 | tf_op jit(solution)/shard_map/ppermute | solution.py:398
  51.6 2.6 %update.7.refs_1_ = bf16[200,256]{1,0:T(8,128)(2,1)S(1)} custom-call(bf16[200,256]{1,0:T(8,128)(2,1)S(1)} %update.6.refs_1_.refs_0_, s32[3]{0:T(128)S(1)} %copy-done.1, s32[36]{0:T(128)S(1)} %copy-done.2, bf16[2304,192]{1,0:T(8,128)(2,1)S(1)} %copy-done.4, bf16[96,4224]{1,0:T(8,128)(2,1)S(1)} %pad_maximum_fusion.same.refs_3_.refs_4_, ...), custom_call_target="tpu_custom_call" | custom-call | flops 3221225472 | bytes 4194304 | tf_op jit(solution)/shard_map/update/pallas_call | solution.py:289
  54.9 1.6 %collective-permute-start.14 = (bf16[200,256]{1,0:T(8,128)(2,1)S(1)}, bf16[200,256]{1,0:T(8,128)(2,1)S(1)}, u32[]{:S(2)}, u32[]{:S(2)}) collective-permute-start(bf16[200,256]{1,0:T(8,128)(2,1)S(1)} %get-tuple-element.31.refs_0_), channel_id=1, source_target_pairs={{0,4},{1,5},{2,6},{3,7},{4,0},{5,1},{6,2},{7,3},{8,12},{9,13},{10,... | collective-permute-start | bytes 307208 | tf_op jit(solution)/shard_map/ppermute | solution.py:398
  57.2 2.1 %collective-permute-done.10.refs_2_ = bf16[200,256]{1,0:T(8,128)(2,1)S(1)} collective-permute-done((bf16[200,256]{1,0:T(8,128)(2,1)S(1)}, bf16[200,256]{1,0:T(8,128)(2,1)S(1)}, u32[]{:S(2)}, u32[]{:S(2)}) %collective-permute-start.10) | collective-permute-done | bytes 102432 | tf_op jit(solution)/shard_map/ppermute | solution.py:398
  59.5 1.4 %collective-permute-done.12.refs_2_ = bf16[200,256]{1,0:T(8,128)(2,1)S(1)} collective-permute-done((bf16[200,256]{1,0:T(8,128)(2,1)S(1)}, bf16[200,256]{1,0:T(8,128)(2,1)S(1)}, u32[]{:S(2)}, u32[]{:S(2)}) %collective-permute-start.12) | collective-permute-done | bytes 102432 | tf_op jit(solution)/shard_map/ppermute | solution.py:398
  61.0 1.7 %collective-permute-start.13 = (bf16[200,256]{1,0:T(8,128)(2,1)S(1)}, bf16[200,256]{1,0:T(8,128)(2,1)S(1)}, u32[]{:S(2)}, u32[]{:S(2)}) collective-permute-start(bf16[200,256]{1,0:T(8,128)(2,1)S(1)} %divide.7.refs_2_), channel_id=1, source_target_pairs={{0,4},{1,5},{2,6},{3,7},{4,0},{5,1},{6,2},{7,3},{8,12},{9,13},{10,... | collective-permute-start | bytes 307208 | tf_op jit(solution)/shard_map/ppermute | solution.py:398
  63.3 1.5 %collective-permute-done.15.refs_3_ = bf16[200,256]{1,0:T(8,128)(2,1)S(1)} collective-permute-done((bf16[200,256]{1,0:T(8,128)(2,1)S(1)}, bf16[200,256]{1,0:T(8,128)(2,1)S(1)}, u32[]{:S(2)}, u32[]{:S(2)}) %collective-permute-start.15) | collective-permute-done | bytes 102432 | tf_op jit(solution)/shard_map/ppermute | solution.py:398
  64.8 1.6 %blend.2.refs_4_ = f32[100,4096]{1,0:T(8,128)} custom-call(s32[3]{0:T(128)S(1)} %copy-done.1, f32[100,4096]{1,0:T(8,128)S(1)} %copy-done, bf16[200,256]{1,0:T(8,128)(2,1)S(1)} %get-tuple-element.31.refs_0_, bf16[200,256]{1,0:T(8,128)(2,1)S(1)} %collective-permute-done.14.refs_1_, bf16[200,256]{1,0:T(8,128)(2,1)S(1)} %divide.5.refs_0_.refs_2_, ...), custom_call_target="tpu_custom_call" | custom-call | flops 1073741824 | bytes 1048576 | tf_op jit(solution)/shard_map/blend/pallas_call | solution.py:372
  67.2 1.6 %blend.3 = f32[100,4096]{1,0:T(8,128)} custom-call(s32[3]{0:T(128)S(1)} %copy-done.1, f32[100,4096]{1,0:T(8,128)S(1)} %copy-done, bf16[200,256]{1,0:T(8,128)(2,1)S(1)} %divide.6.refs_0_, bf16[200,256]{1,0:T(8,128)(2,1)S(1)} %collective-permute-done.11.refs_1_, bf16[200,256]{1,0:T(8,128)(2,1)S(1)} %divide.7.refs_2_, ...), custom_call_target="tpu_custom_call", output_to_operand_aliasing={{}: (6, {})} | custom-call | flops 1073741824 | bytes 1048576 | tf_op jit(solution)/shard_map/blend/pallas_call | solution.py:372
  (50 shorter events, 10.1 us)
Async XLA Ops:
  2.8 10.1 %collective-permute-start.2 = (bf16[24,4224]{1,0:T(8,128)(2,1)}, bf16[24,4224]{1,0:T(8,128)(2,1)S(1)}, u32[]{:S(2)}, u32[]{:S(2)}) collective-permute-start(bf16[24,4224]{1,0:T(8,128)(2,1)} %weigh.1.refs_0_), channel_id=1, source_target_pairs={{0,6},{1,7},{2,4},{3,5},{4,2},{5,3},{6,0},{7,1},{8,14},{9,15},{10,... | collective-permute-start | bytes 608264 | tf_op jit(solution)/shard_map/ppermute | solution.py:398
  6.7 9.8 %collective-permute-start.1 = (bf16[24,4224]{1,0:T(8,128)(2,1)}, bf16[24,4224]{1,0:T(8,128)(2,1)S(1)}, u32[]{:S(2)}, u32[]{:S(2)}) collective-permute-start(bf16[24,4224]{1,0:T(8,128)(2,1)} %weigh.1.refs_0_), channel_id=1, source_target_pairs={{0,4},{1,5},{2,6},{3,7},{4,0},{5,1},{6,2},{7,3},{8,12},{9,13},{10,... | collective-permute-start | bytes 608264 | tf_op jit(solution)/shard_map/ppermute | solution.py:398
  7.2 9.3 %collective-permute-start = (bf16[24,4224]{1,0:T(8,128)(2,1)}, bf16[24,4224]{1,0:T(8,128)(2,1)S(1)}, u32[]{:S(2)}, u32[]{:S(2)}) collective-permute-start(bf16[24,4224]{1,0:T(8,128)(2,1)} %weigh.1.refs_0_), channel_id=1, source_target_pairs={{0,2},{1,3},{2,0},{3,1},{4,6},{5,7},{6,4},{7,5},{8,10},{9,11},{10,... | collective-permute-start | bytes 608264 | tf_op jit(solution)/shard_map/ppermute | solution.py:398
  9.1 7.4 %copy-start.8 = (bf16[24,4224]{1,0:T(8,128)(2,1)S(1)}, bf16[24,4224]{1,0:T(8,128)(2,1)}, u32[]{:S(2)}) copy-start(bf16[24,4224]{1,0:T(8,128)(2,1)} %weigh.1.refs_0_) | copy-start | bytes 608260
  16.5 2.6 %copy-start.1 = (s32[3]{0:T(128)S(1)}, s32[3]{0:T(128)}, u32[]{:S(2)}) copy-start(s32[3]{0:T(128)} %pad_add_fusion.refs_1_.place.refs_0_) | copy-start | bytes 40
  16.6 2.6 %copy-start.2 = (s32[36]{0:T(128)S(1)}, s32[36]{0:T(128)}, u32[]{:S(2)}) copy-start(s32[36]{0:T(128)} %refs_2_.7) | copy-start | bytes 436
  16.6 2.6 %copy-start.5 = (bf16[64,4096]{1,0:T(8,128)(2,1)S(1)}, bf16[64,4096]{1,0:T(8,128)(2,1)}, u32[]{:S(2)}) copy-start(bf16[64,4096]{1,0:T(8,128)(2,1)} %get-tuple-element.19.halved) | copy-start | bytes 1572868
  16.6 2.6 %copy-start.6 = (f32[64,128]{1,0:T(8,128)S(1)}, f32[64,128]{1,0:T(8,128)}, u32[]{:S(2)}) copy-start(f32[64,128]{1,0:T(8,128)} %get-tuple-element.20.power) | copy-start | bytes 98308
  16.6 2.6 %copy-start.7 = (f32[64,128]{1,0:T(8,128)S(1)}, f32[64,128]{1,0:T(8,128)}, u32[]{:S(2)}) copy-start(f32[64,128]{1,0:T(8,128)} %get-tuple-element.21.column) | copy-start | bytes 98308
  16.7 2.4 %collective-permute-start.3 = (bf16[96,4224]{1,0:T(8,128)(2,1)S(1)}, bf16[96,4224]{1,0:T(8,128)(2,1)S(1)}, u32[]{:S(2)}, u32[]{:S(2)}) collective-permute-start(bf16[96,4224]{1,0:T(8,128)(2,1)S(1)} %pad_maximum_fusion.same.refs_3_.refs_4_), channel_id=1, source_target_pairs={{0,1},{1,0},{2,3},{3,2},{4,5},{5,4},{6,7},{7,6},{8,9},{9,8},{10,11... | collective-permute-start | bytes 2433032 | tf_op jit(solution)/shard_map/ppermute | solution.py:398
  27.7 9.2 %copy-start.3 = (bf16[2304,192]{1,0:T(8,128)(2,1)}, bf16[2304,192]{1,0:T(8,128)(2,1)S(1)}, u32[]{:S(2)}) copy-start(bf16[2304,192]{1,0:T(8,128)(2,1)S(1)} %get-tuple-element.25.refs_2_.refs_3_) | copy-start | bytes 2654212
  27.8 1.2 %collective-permute-start.4 = (f32[8,192]{1,0:T(8,128)S(1)}, f32[8,192]{1,0:T(8,128)S(1)}, u32[]{:S(2)}, u32[]{:S(2)}) collective-permute-start(f32[8,192]{1,0:T(8,128)S(1)} %get-tuple-element.26.own), channel_id=1, source_target_pairs={{0,1},{1,0},{2,3},{3,2},{4,5},{5,4},{6,7},{7,6},{8,9},{9,8},{10,11... | collective-permute-start | bytes 18440 | tf_op jit(solution)/shard_map/ppermute | solution.py:398
  29.6 4.6 %collective-permute-start.7 = (f32[8,192]{1,0:T(8,128)S(1)}, f32[8,192]{1,0:T(8,128)S(1)}, u32[]{:S(2)}, u32[]{:S(2)}) collective-permute-start(f32[8,192]{1,0:T(8,128)S(1)} %merge.1.refs_0_), channel_id=1, source_target_pairs={{0,6},{1,7},{2,4},{3,5},{4,2},{5,3},{6,0},{7,1},{8,14},{9,15},{10,... | collective-permute-start | bytes 18440 | tf_op jit(solution)/shard_map/ppermute | solution.py:398
  32.0 3.7 %collective-permute-start.6 = (f32[8,192]{1,0:T(8,128)S(1)}, f32[8,192]{1,0:T(8,128)S(1)}, u32[]{:S(2)}, u32[]{:S(2)}) collective-permute-start(f32[8,192]{1,0:T(8,128)S(1)} %merge.1.refs_0_), channel_id=1, source_target_pairs={{0,4},{1,5},{2,6},{3,7},{4,0},{5,1},{6,2},{7,3},{8,12},{9,13},{10,... | collective-permute-start | bytes 18440 | tf_op jit(solution)/shard_map/ppermute | solution.py:398
  32.5 3.7 %collective-permute-start.5 = (f32[8,192]{1,0:T(8,128)S(1)}, f32[8,192]{1,0:T(8,128)S(1)}, u32[]{:S(2)}, u32[]{:S(2)}) collective-permute-start(f32[8,192]{1,0:T(8,128)S(1)} %merge.1.refs_0_), channel_id=1, source_target_pairs={{0,2},{1,3},{2,0},{3,1},{4,6},{5,7},{6,4},{7,5},{8,10},{9,11},{10,... | collective-permute-start | bytes 18440 | tf_op jit(solution)/shard_map/ppermute | solution.py:398
  39.5 15.2 %collective-permute-start.8 = (bf16[232,256]{1,0:T(8,128)(2,1)S(1)}, bf16[232,256]{1,0:T(8,128)(2,1)S(1)}, u32[]{:S(2)}, u32[]{:S(2)}) collective-permute-start(bf16[232,256]{1,0:T(8,128)(2,1)S(1)} %update.4.refs_0_), channel_id=1, source_target_pairs={{0,8},{1,9},{2,10},{3,11},{4,12},{5,13},{6,14},{7,15},{8,0},{9,1},... | collective-permute-start | bytes 356360 | tf_op jit(solution)/shard_map/ppermute | solution.py:398
  46.0 10.6 %collective-permute-start.9 = (bf16[200,256]{1,0:T(8,128)(2,1)S(1)}, bf16[200,256]{1,0:T(8,128)(2,1)S(1)}, u32[]{:S(2)}, u32[]{:S(2)}) collective-permute-start(bf16[200,256]{1,0:T(8,128)(2,1)S(1)} %update.5.refs_1_.refs_0_), channel_id=1, source_target_pairs={{0,8},{1,9},{2,10},{3,11},{4,12},{5,13},{6,14},{7,15},{8,0},{9,1},... | collective-permute-start | bytes 307208 | tf_op jit(solution)/shard_map/ppermute | solution.py:398
  49.0 10.3 %collective-permute-start.10 = (bf16[200,256]{1,0:T(8,128)(2,1)S(1)}, bf16[200,256]{1,0:T(8,128)(2,1)S(1)}, u32[]{:S(2)}, u32[]{:S(2)}) collective-permute-start(bf16[200,256]{1,0:T(8,128)(2,1)S(1)} %update.6.refs_1_.refs_0_), channel_id=1, source_target_pairs={{0,8},{1,9},{2,10},{3,11},{4,12},{5,13},{6,14},{7,15},{8,0},{9,1},... | collective-permute-start | bytes 307208 | tf_op jit(solution)/shard_map/ppermute | solution.py:398
  54.2 6.7 %collective-permute-start.12 = (bf16[200,256]{1,0:T(8,128)(2,1)S(1)}, bf16[200,256]{1,0:T(8,128)(2,1)S(1)}, u32[]{:S(2)}, u32[]{:S(2)}) collective-permute-start(bf16[200,256]{1,0:T(8,128)(2,1)S(1)} %update.7.refs_1_), channel_id=1, source_target_pairs={{0,8},{1,9},{2,10},{3,11},{4,12},{5,13},{6,14},{7,15},{8,0},{9,1},... | collective-permute-start | bytes 307208 | tf_op jit(solution)/shard_map/ppermute | solution.py:398
  54.9 9.9 %copy-start = (f32[100,4096]{1,0:T(8,128)S(1)}, f32[100,4096]{1,0:T(8,128)}, u32[]{:S(2)}) copy-start(f32[100,4096]{1,0:T(8,128)} %classes.3) | copy-start | bytes 4915204
  54.9 9.9 %collective-permute-start.14 = (bf16[200,256]{1,0:T(8,128)(2,1)S(1)}, bf16[200,256]{1,0:T(8,128)(2,1)S(1)}, u32[]{:S(2)}, u32[]{:S(2)}) collective-permute-start(bf16[200,256]{1,0:T(8,128)(2,1)S(1)} %get-tuple-element.31.refs_0_), channel_id=1, source_target_pairs={{0,4},{1,5},{2,6},{3,7},{4,0},{5,1},{6,2},{7,3},{8,12},{9,13},{10,... | collective-permute-start | bytes 307208 | tf_op jit(solution)/shard_map/ppermute | solution.py:398
  56.7 8.1 %collective-permute-start.15 = (bf16[200,256]{1,0:T(8,128)(2,1)S(1)}, bf16[200,256]{1,0:T(8,128)(2,1)S(1)}, u32[]{:S(2)}, u32[]{:S(2)}) collective-permute-start(bf16[200,256]{1,0:T(8,128)(2,1)S(1)} %divide.5.refs_0_.refs_2_), channel_id=1, source_target_pairs={{0,4},{1,5},{2,6},{3,7},{4,0},{5,1},{6,2},{7,3},{8,12},{9,13},{10,... | collective-permute-start | bytes 307208 | tf_op jit(solution)/shard_map/ppermute | solution.py:398
  59.4 7.8 %collective-permute-start.11 = (bf16[200,256]{1,0:T(8,128)(2,1)S(1)}, bf16[200,256]{1,0:T(8,128)(2,1)S(1)}, u32[]{:S(2)}, u32[]{:S(2)}) collective-permute-start(bf16[200,256]{1,0:T(8,128)(2,1)S(1)} %divide.6.refs_0_), channel_id=1, source_target_pairs={{0,4},{1,5},{2,6},{3,7},{4,0},{5,1},{6,2},{7,3},{8,12},{9,13},{10,... | collective-permute-start | bytes 307208 | tf_op jit(solution)/shard_map/ppermute | solution.py:398
  61.0 6.2 %collective-permute-start.13 = (bf16[200,256]{1,0:T(8,128)(2,1)S(1)}, bf16[200,256]{1,0:T(8,128)(2,1)S(1)}, u32[]{:S(2)}, u32[]{:S(2)}) collective-permute-start(bf16[200,256]{1,0:T(8,128)(2,1)S(1)} %divide.7.refs_2_), channel_id=1, source_target_pairs={{0,4},{1,5},{2,6},{3,7},{4,0},{5,1},{6,2},{7,3},{8,12},{9,13},{10,... | collective-permute-start | bytes 307208 | tf_op jit(solution)/shard_map/ppermute | solution.py:398
  (1 other events, 1.3 us)

commit v5 on v4

--- a/solution.py
+++ b/solution.py
@@ -37,7 +37,7 @@
 def halves(total):
     half = total // 2
     full = half // 8 * 8
-    return half, full, half - full, -(-half // 16) * 16
+    return half, full, half - full, full + 8
 
 
 def cost(flops, moved):
@@ -79,19 +79,21 @@
     upper = place[0] == 1
     total = classes.shape[0]
     half, full, rest, _ = halves(total)
-    pad = jnp.zeros((width - (total - full), ANG), F32)
+    none = jnp.zeros((8, ANG), F32)
+    pad = jnp.zeros((full + 16 - (total - full), ANG), F32)
     lane = lax.broadcasted_iota(jnp.int32, (width, ANG), 1)
 
     def mine(low, high):
-        high = pltpu.roll(jnp.concatenate([high, pad], axis=0), width - rest, 0)
-        return jnp.where(upper, high, low)
+        high = pltpu.roll(jnp.concatenate([high, pad], axis=0), full + 16 - rest, 0)
+        return jnp.where(upper, high[:width], low)
 
     kept = jnp.zeros((width, ANG), F32)
     for c in range(CYCLES):
         here = slice(c * ANG, (c + 1) * ANG)
-        part = mine(classes[0:width, here], classes[full:total, here]).astype(BF16)
-        halved[:, here] = part
-        wide = part.astype(F32)
+        part = mine(classes[0:width, here], classes[full:total, here])
+        halved[0 : width + 8, here] = jnp.concatenate([part, none], axis=0).astype(BF16)
+        halved[width + 8 :, here] = jnp.concatenate([none, part], axis=0).astype(BF16)
+        wide = part.astype(BF16).astype(F32)
         kept = jnp.where(lane == c, jnp.sum(wide * wide, axis=1, keepdims=True), kept)
     power[...] = kept
     turned = jnp.broadcast_to(prior[...], (ANG, ANG)).T
@@ -103,7 +105,7 @@
     return pl.pallas_call(
         later(functools.partial(prepare_kernel, width), len(after)),
         out_shape=(
-            jax.ShapeDtypeStruct((width, PIX), BF16),
+            jax.ShapeDtypeStruct((2 * (width + 8), PIX), BF16),
             jax.ShapeDtypeStruct((width, ANG), F32),
             jax.ShapeDtypeStruct((width, ANG), F32),
         ),
@@ -135,11 +137,18 @@
             block = turned[q % 2]
             for c in range(span):
                 cycle = q * span + c
-                image = halved[:, cycle * ANG : (cycle + 1) * ANG]
-                for r in range(each):
-                    block[r * width : (r + 1) * width, c * ANG : (c + 1) * ANG] = pltpu.roll(
-                        image, shifts[g * each + r], 1
+                here = slice(cycle * ANG, (cycle + 1) * ANG)
+                there = slice(c * ANG, (c + 1) * ANG)
+                first, second = halved[: width + 8, here], halved[width + 8 :, here]
+                for r in range(0, each, 2):
+                    at = r * width
+                    one_turned = pltpu.roll(first, shifts[g * each + r], 1)
+                    two_turned = pltpu.roll(second, shifts[g * each + r + 1], 1)
+                    block[at : at + width - 8, there] = one_turned[: width - 8]
+                    block[at + width - 8 : at + width + 8, there] = (
+                        one_turned[width - 8 :] + two_turned[:16]
                     )
+                    block[at + width + 8 : at + 2 * width, there] = two_turned[16:]
             part = lax.dot_general(
                 block[...],
                 images[:, q * span * ANG : (q + 1) * span * ANG],
@@ -154,14 +163,18 @@
     top = jnp.max(top, axis=0, keepdims=True)
 
     def add(r, sums):
-        block = pl.ds(pl.multiple_of(r * width, 16), width)
+        block = pl.ds(pl.multiple_of(r * 2 * width, 16), 2 * width)
         value = jnp.exp(logits[block, :] - top)
         rounded = value.astype(BF16)
         terms[block, :] = rounded
-        return sums[0] + value, sums[1] + rounded.astype(F32)
+        kept = rounded.astype(F32)
+        return (
+            sums[0] + (value[:width] + value[width:]),
+            sums[1] + (kept[:width] + kept[width:]),
+        )
 
     zero = jnp.zeros((width, count), F32)
-    total, rounded = lax.fori_loop(0, ROT, add, (zero, zero))
+    total, rounded = lax.fori_loop(0, ROT // 2, add, (zero, zero))
     summed[...] = rounded
     stats[0:1, :] = top
     stats[1:2, :] = jnp.sum(total, axis=0, keepdims=True)
@@ -169,7 +182,7 @@
 
 
 def score(width, place, shifts, halved, power, column, same, across):
-    groups, span = 4, 4
+    groups, span = 6,4
     one, full = same.shape
     count = 2 * one
     outs = (
@@ -194,7 +207,7 @@
 def normalize_kernel(place, own, summed, squares, *refs):
     stats, (scales, evidence, denominator, joined) = refs[:-4], refs[-4:]
     count = own.shape[1]
-    for m, stat in enumerate(stats):
+    for m, stat in zip((0, 3, 2, 1), stats):
         joined[pl.ds(pl.multiple_of((place[1] ^ m) * 8, 8), 8), :] = stat[...]
     tops = [joined[8 * j : 8 * j + 1, :] for j in range(len(stats))]
     totals = [joined[8 * j + 1 : 8 * j + 2, :] for j in range(len(stats))]
@@ -264,13 +277,13 @@
         tail = jnp.zeros((8, ANG), F32)
         for q in range(QUARTERS):
             j = q * wide + i
-            sums = jnp.zeros((width, ANG), F32)
+            sums = [jnp.zeros((width + 8, ANG), F32)] * 2
             for r in range(ROT):
                 back = (ANG - shifts[r]) & (ANG - 1)
-                turned = pltpu.roll(
-                    product[r * width : (r + 1) * width, j * ANG : (j + 1) * ANG], back, 1
-                )
-                sums = sums + turned.astype(F32)
+                at = r * width - 8 * (r % 2)
+                turned = pltpu.roll(product[at : at + width + 8, j * ANG : (j + 1) * ANG], back, 1)
+                sums[r % 2] = sums[r % 2] + turned.astype(F32)
+            sums = sums[0][:width] + sums[1][8:]
             out[q * full : (q + 1) * full, there] = sums[:full].astype(BF16)
             moved = pltpu.roll(sums[full : full + 8], q * rest, 0) if q else sums[full : full + 8]
             tail = jnp.where((row >= q * rest) & (row < (q + 1) * rest), moved, tail)
@@ -344,11 +357,12 @@
     total = classes.shape[0]
     half, full, rest, _ = halves(total)
     upper = place[0] == 1
-    span = refs[0].shape[1]
-    row = lax.broadcasted_iota(jnp.int32, (full + 16, span), 0)
-    none = jnp.zeros((8, span), F32)
+    done = 0
     for p in range(chunks):
         mine, other = refs[2 * p : 2 * p + 2]
+        span = mine.shape[1]
+        row = lax.broadcasted_iota(jnp.int32, (full + 16, span), 0)
+        none = jnp.zeros((8, span), F32)
         ends = [a[QUARTERS * full :, :].astype(F32) for a in (mine, other)]
         for q in range(QUARTERS):
             rows = []
@@ -361,7 +375,8 @@
             low_end = jnp.concatenate([low_end, jnp.zeros((full + 8, span), F32)], axis=0)
             upper_rows = jnp.where(row < rest, low_end, high)
             step = jnp.concatenate([low, upper_rows[: total - full]], axis=0)
-            at = slice((p * QUARTERS + q) * span, (p * QUARTERS + q + 1) * span)
+            at = slice(done, done + span)
+            done += span
             out[:, at] = (1.0 - STEP_WEIGHT) * classes[:, at] + STEP_WEIGHT * step
 
 
@@ -421,6 +436,7 @@
 
     stat = merge(place, own_stat, swap(own_stat, CORE))
     stats = [stat] + [swap(stat, m) for m in (CHIP, NEXT, NEXT + CHIP)]
+    stats = [stats[j] for j in (0, 3, 2, 1)]
     scales, evidence, below = normalize(place, own_stat, summed, squares, stats)
 
     mine, other, ratios, others, share = [], [], [], [], []
@@ -575,7 +591,7 @@
     total = classes.shape[0]
     _, full, rest, _ = halves(total)
     quad = lax.axis_size("particle") == 4 and lax.axis_size("cls") == 4
-    fits = total % 2 == 0 and QUARTERS * rest <= 8 and 32 <= full <= 48 and total <= ANG
+    fits = total % 2 == 0 and QUARTERS * rest <= 8 and full % 16 == 0 and 32 <= full <= 48 and total <= ANG
     plan = halved if quad and fits else whole_sum
     return plan(pool, picks, groups, ctf_table, shifts, classes, log_prior)
 

time: 69 us -> 67.1 us (0.972)
  Pallas kernels: 28.7 us -> 26.9 us
  waiting for transfers between devices: 16.9 us -> 18 us
  starting transfers between devices: 18.4 us -> 17.4 us
    pallas_call x4, Pallas kernels: 10.2 us -> 9.07 us  [update(): pl.pallas_call(later(functools.partial(update_kernel, total, first, cycle...]
    ppermute x16, waiting for transfers between devices: 16.9 us -> 18 us  [swap(): return lax.ppermute(a, axes, [(i, i ^ mask) for i in range(16)])]
    ppermute x16, starting transfers between devices: 18.4 us -> 17.4 us  [swap(): return lax.ppermute(a, axes, [(i, i ^ mask) for i in range(16)])]
    pallas_call x1, Pallas kernels: 8.58 us -> 7.62 us  [score(): pl.pallas_call(functools.partial(score_kernel, width, groups, span), out_...]
  transfers between devices with their start and end apart: 16 -> 16, of which waited for: 11 -> 12; matrix products, arithmetic and copies ran while one was open for 4% -> 4% of each run, Pallas kernels for 18% -> 18%
where the time goes in v5:
time: 67.1 us; the launch traced here: 66.9 us
  Pallas kernels  26.9 us (40%)
  waiting for transfers between devices  18 us (27%)
  starting transfers between devices  17.4 us (26%)
  local copies, waits for them, and re-layouts  3.09 us (5%)
  between operations  0.83 us (1%)
  other arithmetic  0.8 us (1%)
    ppermute x16, waiting for transfers between devices, swap(): return lax.ppermute(a, axes, [(i, i ^ mask) for i in range(16)])  18 us
    ppermute x16, starting transfers between devices, swap(): return lax.ppermute(a, axes, [(i, i ^ mask) for i in range(16)])  17.4 us
    pallas_call x4, Pallas kernels, update(): pl.pallas_call(later(functools.partial(update_kernel, total, first, cycle...  9.07 us
    pallas_call x1, Pallas kernels, score(): pl.pallas_call(functools.partial(score_kernel, width, groups, span), out_...  7.62 us
    pallas_call x2, Pallas kernels, blend(): pl.pallas_call(functools.partial(blend_kernel, len(updates)), grid=(1,),...  3.25 us
    pallas_call x1, Pallas kernels, prepare(): pl.pallas_call(later(functools.partial(prepare_kernel, width), len(after)...  2.78 us
    pallas_call x1, Pallas kernels, weigh(): pl.pallas_call(weigh_kernel, out_shape=jax.ShapeDtypeStruct((count, PIX +...  2.16 us
  transfers between devices with their start and end apart: 16, of which 12 were waited for; matrix products, arithmetic and copies ran while one was open for 4% of the time, Pallas kernels for 18%

profile of v5, /device:TPU:0, one launch (start us, length us, event | category | flops | bytes accessed | tf_op | source)
XLA Modules:
  0.0 66.9 jit_solution(6985353259055588653)
XLA Ops:
  0.6 2.2 %weigh.1.refs_0_ = bf16[24,4224]{1,0:T(8,128)(2,1)} custom-call(s32[1,24]{1,0:T(1,128)} %bitcast.17, s32[1,24]{1,0:T(1,128)} %bitcast.18, bf16[48,4096]{1,0:T(8,128)(2,1)} %pool.1, f32[32,64]{1,0:T(8,128)} %bitcast.16), custom_call_target="tpu_custom_call" | custom-call | flops 9437184 | bytes 1048576 | tf_op jit(solution)/shard_map/weigh/pallas_call | solution.py:67
  2.8 2.9 %collective-permute-start = (bf16[24,4224]{1,0:T(8,128)(2,1)}, bf16[24,4224]{1,0:T(8,128)(2,1)S(1)}, u32[]{:S(2)}, u32[]{:S(2)}) collective-permute-start(bf16[24,4224]{1,0:T(8,128)(2,1)} %weigh.1.refs_0_), channel_id=1, source_target_pairs={{0,2},{1,3},{2,0},{3,1},{4,6},{5,7},{6,4},{7,5},{8,10},{9,11},{10,... | collective-permute-start | bytes 608264 | tf_op jit(solution)/shard_map/ppermute | solution.py:413
  5.7 1.6 %collective-permute-start.1 = (bf16[24,4224]{1,0:T(8,128)(2,1)}, bf16[24,4224]{1,0:T(8,128)(2,1)S(1)}, u32[]{:S(2)}, u32[]{:S(2)}) collective-permute-start(bf16[24,4224]{1,0:T(8,128)(2,1)} %weigh.1.refs_0_), channel_id=1, source_target_pairs={{0,4},{1,5},{2,6},{3,7},{4,0},{5,1},{6,2},{7,3},{8,12},{9,13},{10,... | collective-permute-start | bytes 608264 | tf_op jit(solution)/shard_map/ppermute | solution.py:413
  7.3 1.1 %pad_bitcast_fusion.refs_3_ = f32[1,128]{1,0:T(1,128)} fusion(f32[100]{0:T(128)} %param.13), kind=kLoop, calls=%fused_computation.13 | loop fusion | bytes 912 | tf_op jit(solution)/shard_map/reshape | solution.py:410
  9.1 2.8 %prepare.1 = (bf16[128,4096]{1,0:T(8,128)(2,1)}, f32[56,128]{1,0:T(8,128)}, f32[56,128]{1,0:T(8,128)}) custom-call(bf16[24,4224]{1,0:T(8,128)(2,1)} %weigh.1.refs_0_, s32[3]{0:T(128)} %pad_add_fusion.refs_1_.place.refs_0_, f32[100,4096]{1,0:T(8,128)} %classes.3, f32[1,128]{1,0:T(1,128)} %pad_bitcast_fusion.refs_3_), custom_call_target="tpu_custom_call" | custom-call | flops 2147483648 | bytes 2097152 | tf_op jit(solution)/shard_map/prepare/pallas_call | solution.py:105
  11.9 2.0 %collective-permute-done.1 = bf16[24,4224]{1,0:T(8,128)(2,1)S(1)} collective-permute-done((bf16[24,4224]{1,0:T(8,128)(2,1)}, bf16[24,4224]{1,0:T(8,128)(2,1)S(1)}, u32[]{:S(2)}, u32[]{:S(2)}) %collective-permute-start.1) | collective-permute-done | bytes 202784 | tf_op jit(solution)/shard_map/ppermute | solution.py:413
  13.9 2.7 %collective-permute-done.2 = bf16[24,4224]{1,0:T(8,128)(2,1)S(1)} collective-permute-done((bf16[24,4224]{1,0:T(8,128)(2,1)}, bf16[24,4224]{1,0:T(8,128)(2,1)S(1)}, u32[]{:S(2)}, u32[]{:S(2)}) %collective-permute-start.2) | collective-permute-done | bytes 202784 | tf_op jit(solution)/shard_map/ppermute | solution.py:413
  16.9 2.3 %collective-permute-done.3.across.refs_4_.refs_5_ = bf16[96,4224]{1,0:T(8,128)(2,1)S(1)} collective-permute-done((bf16[96,4224]{1,0:T(8,128)(2,1)S(1)}, bf16[96,4224]{1,0:T(8,128)(2,1)S(1)}, u32[]{:S(2)}, u32[]{:S(2)}) %collective-permute-start.3) | collective-permute-done | bytes 811040 | tf_op jit(solution)/shard_map/ppermute | solution.py:413
  19.2 7.6 %score.1 = (bf16[2016,192]{1,0:T(8,128)(2,1)S(1)}, f32[56,192]{1,0:T(8,128)S(1)}, f32[8,192]{1,0:T(8,128)S(1)}, f32[192,128]{1,0:T(8,128)S(1)}) custom-call(s32[3]{0:T(128)S(1)} %copy-done.1, s32[36]{0:T(128)S(1)} %copy-done.2, bf16[128,4096]{1,0:T(8,128)(2,1)S(1)} %copy-done.3, f32[56,128]{1,0:T(8,128)S(1)} %copy-done.6, f32[56,128]{1,0:T(8,128)S(1)} %copy-done.7, ...), custom_call_target="tpu_custom_call" | custom-call | flops 10737418240 | bytes 20971520 | tf_op jit(solution)/shard_map/score/pallas_call | solution.py:194
  28.7 2.7 %collective-permute-start.5 = (f32[8,192]{1,0:T(8,128)S(1)}, f32[8,192]{1,0:T(8,128)S(1)}, u32[]{:S(2)}, u32[]{:S(2)}) collective-permute-start(f32[8,192]{1,0:T(8,128)S(1)} %merge.1.refs_0_), channel_id=1, source_target_pairs={{0,6},{1,7},{2,4},{3,5},{4,2},{5,3},{6,0},{7,1},{8,14},{9,15},{10,... | collective-permute-start | bytes 18440 | tf_op jit(solution)/shard_map/ppermute | solution.py:413
  33.3 1.7 %collective-permute-done.6.refs_2_ = f32[8,192]{1,0:T(8,128)S(1)} collective-permute-done((f32[8,192]{1,0:T(8,128)S(1)}, f32[8,192]{1,0:T(8,128)S(1)}, u32[]{:S(2)}, u32[]{:S(2)}) %collective-permute-start.6) | collective-permute-done | bytes 6176 | tf_op jit(solution)/shard_map/ppermute | solution.py:413
  36.3 2.3 %update.4.refs_0_ = bf16[232,256]{1,0:T(8,128)(2,1)S(1)} custom-call(s32[3]{0:T(128)S(1)} %copy-done.1, s32[36]{0:T(128)S(1)} %copy-done.2, bf16[2016,192]{1,0:T(8,128)(2,1)S(1)} %get-tuple-element.25.refs_2_.refs_3_, bf16[96,4224]{1,0:T(8,128)(2,1)S(1)} %pad_maximum_fusion.same.refs_3_.refs_4_, ...), custom_call_target="tpu_custom_call" | custom-call | flops 3221225472 | bytes 4194304 | tf_op jit(solution)/shard_map/update/pallas_call | solution.py:302
  38.5 2.6 %collective-permute-start.8 = (bf16[232,256]{1,0:T(8,128)(2,1)S(1)}, bf16[232,256]{1,0:T(8,128)(2,1)S(1)}, u32[]{:S(2)}, u32[]{:S(2)}) collective-permute-start(bf16[232,256]{1,0:T(8,128)(2,1)S(1)} %update.4.refs_0_), channel_id=1, source_target_pairs={{0,8},{1,9},{2,10},{3,11},{4,12},{5,13},{6,14},{7,15},{8,0},{9,1},... | collective-permute-start | bytes 356360 | tf_op jit(solution)/shard_map/ppermute | solution.py:413
  41.2 1.2 %copy-done.5 = bf16[2016,192]{1,0:T(8,128)(2,1)S(1)} copy-done((bf16[2016,192]{1,0:T(8,128)(2,1)S(1)}, bf16[2016,192]{1,0:T(8,128)(2,1)}, u32[]{:S(2)}) %copy-start.5) | copy-done | bytes 774168
  42.4 2.3 %update.5.refs_1_.refs_0_ = bf16[200,256]{1,0:T(8,128)(2,1)S(1)} custom-call(bf16[232,256]{1,0:T(8,128)(2,1)S(1)} %update.4.refs_0_, s32[3]{0:T(128)S(1)} %copy-done.1, s32[36]{0:T(128)S(1)} %copy-done.2, bf16[2016,192]{1,0:T(8,128)(2,1)S(1)} %copy-done.5, bf16[96,4224]{1,0:T(8,128)(2,1)S(1)} %pad_maximum_fusion.same.refs_3_.refs_4_, ...), custom_call_target="tpu_custom_call" | custom-call | flops 3221225472 | bytes 4194304 | tf_op jit(solution)/shard_map/update/pallas_call | solution.py:302
  45.1 2.3 %update.6.refs_1_.refs_0_ = bf16[200,256]{1,0:T(8,128)(2,1)S(1)} custom-call(bf16[200,256]{1,0:T(8,128)(2,1)S(1)} %update.5.refs_1_.refs_0_, s32[3]{0:T(128)S(1)} %copy-done.1, s32[36]{0:T(128)S(1)} %copy-done.2, bf16[2016,192]{1,0:T(8,128)(2,1)S(1)} %copy-done.5, bf16[96,4224]{1,0:T(8,128)(2,1)S(1)} %pad_maximum_fusion.same.refs_3_.refs_4_, ...), custom_call_target="tpu_custom_call" | custom-call | flops 3221225472 | bytes 4194304 | tf_op jit(solution)/shard_map/update/pallas_call | solution.py:302
  47.4 2.7 %collective-permute-start.10 = (bf16[200,256]{1,0:T(8,128)(2,1)S(1)}, bf16[200,256]{1,0:T(8,128)(2,1)S(1)}, u32[]{:S(2)}, u32[]{:S(2)}) collective-permute-start(bf16[200,256]{1,0:T(8,128)(2,1)S(1)} %update.6.refs_1_.refs_0_), channel_id=1, source_target_pairs={{0,8},{1,9},{2,10},{3,11},{4,12},{5,13},{6,14},{7,15},{8,0},{9,1},... | collective-permute-start | bytes 307208 | tf_op jit(solution)/shard_map/ppermute | solution.py:413
  50.0 2.3 %update.7.refs_1_ = bf16[200,256]{1,0:T(8,128)(2,1)S(1)} custom-call(bf16[200,256]{1,0:T(8,128)(2,1)S(1)} %update.6.refs_1_.refs_0_, s32[3]{0:T(128)S(1)} %copy-done.1, s32[36]{0:T(128)S(1)} %copy-done.2, bf16[2016,192]{1,0:T(8,128)(2,1)S(1)} %copy-done.5, bf16[96,4224]{1,0:T(8,128)(2,1)S(1)} %pad_maximum_fusion.same.refs_3_.refs_4_, ...), custom_call_target="tpu_custom_call" | custom-call | flops 3221225472 | bytes 4194304 | tf_op jit(solution)/shard_map/update/pallas_call | solution.py:302
  53.0 1.6 %collective-permute-start.14 = (bf16[200,256]{1,0:T(8,128)(2,1)S(1)}, bf16[200,256]{1,0:T(8,128)(2,1)S(1)}, u32[]{:S(2)}, u32[]{:S(2)}) collective-permute-start(bf16[200,256]{1,0:T(8,128)(2,1)S(1)} %get-tuple-element.31.refs_0_), channel_id=1, source_target_pairs={{0,4},{1,5},{2,6},{3,7},{4,0},{5,1},{6,2},{7,3},{8,12},{9,13},{10,... | collective-permute-start | bytes 307208 | tf_op jit(solution)/shard_map/ppermute | solution.py:413
  55.3 2.3 %collective-permute-done.10.refs_2_ = bf16[200,256]{1,0:T(8,128)(2,1)S(1)} collective-permute-done((bf16[200,256]{1,0:T(8,128)(2,1)S(1)}, bf16[200,256]{1,0:T(8,128)(2,1)S(1)}, u32[]{:S(2)}, u32[]{:S(2)}) %collective-permute-start.10) | collective-permute-done | bytes 102432 | tf_op jit(solution)/shard_map/ppermute | solution.py:413
  58.5 1.4 %collective-permute-done.12.refs_2_ = bf16[200,256]{1,0:T(8,128)(2,1)S(1)} collective-permute-done((bf16[200,256]{1,0:T(8,128)(2,1)S(1)}, bf16[200,256]{1,0:T(8,128)(2,1)S(1)}, u32[]{:S(2)}, u32[]{:S(2)}) %collective-permute-start.12) | collective-permute-done | bytes 102432 | tf_op jit(solution)/shard_map/ppermute | solution.py:413
  60.9 2.2 %collective-permute-done.15.refs_3_ = bf16[200,256]{1,0:T(8,128)(2,1)S(1)} collective-permute-done((bf16[200,256]{1,0:T(8,128)(2,1)S(1)}, bf16[200,256]{1,0:T(8,128)(2,1)S(1)}, u32[]{:S(2)}, u32[]{:S(2)}) %collective-permute-start.15) | collective-permute-done | bytes 102432 | tf_op jit(solution)/shard_map/ppermute | solution.py:413
  63.1 1.6 %blend.2.refs_4_ = f32[100,4096]{1,0:T(8,128)} custom-call(s32[3]{0:T(128)S(1)} %copy-done.1, f32[100,4096]{1,0:T(8,128)S(1)} %copy-done, bf16[200,256]{1,0:T(8,128)(2,1)S(1)} %get-tuple-element.31.refs_0_, bf16[200,256]{1,0:T(8,128)(2,1)S(1)} %collective-permute-done.14.refs_1_, bf16[200,256]{1,0:T(8,128)(2,1)S(1)} %divide.5.refs_0_.refs_2_, ...), custom_call_target="tpu_custom_call" | custom-call | flops 1073741824 | bytes 1048576 | tf_op jit(solution)/shard_map/blend/pallas_call | solution.py:387
  65.3 1.6 %blend.3 = f32[100,4096]{1,0:T(8,128)} custom-call(s32[3]{0:T(128)S(1)} %copy-done.1, f32[100,4096]{1,0:T(8,128)S(1)} %copy-done, bf16[200,256]{1,0:T(8,128)(2,1)S(1)} %divide.6.refs_0_, bf16[200,256]{1,0:T(8,128)(2,1)S(1)} %collective-permute-done.11.refs_1_, bf16[200,256]{1,0:T(8,128)(2,1)S(1)} %divide.7.refs_2_, ...), custom_call_target="tpu_custom_call", output_to_operand_aliasing={{}: (6, {})} | custom-call | flops 1073741824 | bytes 1048576 | tf_op jit(solution)/shard_map/blend/pallas_call | solution.py:387
  (50 shorter events, 10.0 us)
Async XLA Ops:
  2.8 9.1 %collective-permute-start = (bf16[24,4224]{1,0:T(8,128)(2,1)}, bf16[24,4224]{1,0:T(8,128)(2,1)S(1)}, u32[]{:S(2)}, u32[]{:S(2)}) collective-permute-start(bf16[24,4224]{1,0:T(8,128)(2,1)} %weigh.1.refs_0_), channel_id=1, source_target_pairs={{0,2},{1,3},{2,0},{3,1},{4,6},{5,7},{6,4},{7,5},{8,10},{9,11},{10,... | collective-permute-start | bytes 608264 | tf_op jit(solution)/shard_map/ppermute | solution.py:413
  5.7 8.2 %collective-permute-start.1 = (bf16[24,4224]{1,0:T(8,128)(2,1)}, bf16[24,4224]{1,0:T(8,128)(2,1)S(1)}, u32[]{:S(2)}, u32[]{:S(2)}) collective-permute-start(bf16[24,4224]{1,0:T(8,128)(2,1)} %weigh.1.refs_0_), channel_id=1, source_target_pairs={{0,4},{1,5},{2,6},{3,7},{4,0},{5,1},{6,2},{7,3},{8,12},{9,13},{10,... | collective-permute-start | bytes 608264 | tf_op jit(solution)/shard_map/ppermute | solution.py:413
  7.3 9.3 %collective-permute-start.2 = (bf16[24,4224]{1,0:T(8,128)(2,1)}, bf16[24,4224]{1,0:T(8,128)(2,1)S(1)}, u32[]{:S(2)}, u32[]{:S(2)}) collective-permute-start(bf16[24,4224]{1,0:T(8,128)(2,1)} %weigh.1.refs_0_), channel_id=1, source_target_pairs={{0,6},{1,7},{2,4},{3,5},{4,2},{5,3},{6,0},{7,1},{8,14},{9,15},{10,... | collective-permute-start | bytes 608264 | tf_op jit(solution)/shard_map/ppermute | solution.py:413
  9.1 7.5 %copy-start.8 = (bf16[24,4224]{1,0:T(8,128)(2,1)S(1)}, bf16[24,4224]{1,0:T(8,128)(2,1)}, u32[]{:S(2)}) copy-start(bf16[24,4224]{1,0:T(8,128)(2,1)} %weigh.1.refs_0_) | copy-start | bytes 608260
  16.6 2.6 %copy-start.1 = (s32[3]{0:T(128)S(1)}, s32[3]{0:T(128)}, u32[]{:S(2)}) copy-start(s32[3]{0:T(128)} %pad_add_fusion.refs_1_.place.refs_0_) | copy-start | bytes 40
  16.6 2.6 %copy-start.2 = (s32[36]{0:T(128)S(1)}, s32[36]{0:T(128)}, u32[]{:S(2)}) copy-start(s32[36]{0:T(128)} %refs_2_.7) | copy-start | bytes 436
  16.6 2.6 %copy-start.3 = (bf16[128,4096]{1,0:T(8,128)(2,1)S(1)}, bf16[128,4096]{1,0:T(8,128)(2,1)}, u32[]{:S(2)}) copy-start(bf16[128,4096]{1,0:T(8,128)(2,1)} %get-tuple-element.19.halved) | copy-start | bytes 3145732
  16.6 2.6 %copy-start.6 = (f32[56,128]{1,0:T(8,128)S(1)}, f32[56,128]{1,0:T(8,128)}, u32[]{:S(2)}) copy-start(f32[56,128]{1,0:T(8,128)} %get-tuple-element.20.power) | copy-start | bytes 86020
  16.6 2.6 %copy-start.7 = (f32[56,128]{1,0:T(8,128)S(1)}, f32[56,128]{1,0:T(8,128)}, u32[]{:S(2)}) copy-start(f32[56,128]{1,0:T(8,128)} %get-tuple-element.21.column) | copy-start | bytes 86020
  16.8 2.4 %collective-permute-start.3 = (bf16[96,4224]{1,0:T(8,128)(2,1)S(1)}, bf16[96,4224]{1,0:T(8,128)(2,1)S(1)}, u32[]{:S(2)}, u32[]{:S(2)}) collective-permute-start(bf16[96,4224]{1,0:T(8,128)(2,1)S(1)} %pad_maximum_fusion.same.refs_3_.refs_4_), channel_id=1, source_target_pairs={{0,1},{1,0},{2,3},{3,2},{4,5},{5,4},{6,7},{7,6},{8,9},{9,8},{10,11... | collective-permute-start | bytes 2433032 | tf_op jit(solution)/shard_map/ppermute | solution.py:413
  26.8 9.4 %copy-start.4 = (bf16[2016,192]{1,0:T(8,128)(2,1)}, bf16[2016,192]{1,0:T(8,128)(2,1)S(1)}, u32[]{:S(2)}) copy-start(bf16[2016,192]{1,0:T(8,128)(2,1)S(1)} %get-tuple-element.25.refs_2_.refs_3_) | copy-start | bytes 2322436
  26.9 1.2 %collective-permute-start.4 = (f32[8,192]{1,0:T(8,128)S(1)}, f32[8,192]{1,0:T(8,128)S(1)}, u32[]{:S(2)}, u32[]{:S(2)}) collective-permute-start(f32[8,192]{1,0:T(8,128)S(1)} %get-tuple-element.26.own), channel_id=1, source_target_pairs={{0,1},{1,0},{2,3},{3,2},{4,5},{5,4},{6,7},{7,6},{8,9},{9,8},{10,11... | collective-permute-start | bytes 18440 | tf_op jit(solution)/shard_map/ppermute | solution.py:413
  28.7 4.6 %collective-permute-start.5 = (f32[8,192]{1,0:T(8,128)S(1)}, f32[8,192]{1,0:T(8,128)S(1)}, u32[]{:S(2)}, u32[]{:S(2)}) collective-permute-start(f32[8,192]{1,0:T(8,128)S(1)} %merge.1.refs_0_), channel_id=1, source_target_pairs={{0,6},{1,7},{2,4},{3,5},{4,2},{5,3},{6,0},{7,1},{8,14},{9,15},{10,... | collective-permute-start | bytes 18440 | tf_op jit(solution)/shard_map/ppermute | solution.py:413
  31.4 3.7 %collective-permute-start.6 = (f32[8,192]{1,0:T(8,128)S(1)}, f32[8,192]{1,0:T(8,128)S(1)}, u32[]{:S(2)}, u32[]{:S(2)}) collective-permute-start(f32[8,192]{1,0:T(8,128)S(1)} %merge.1.refs_0_), channel_id=1, source_target_pairs={{0,4},{1,5},{2,6},{3,7},{4,0},{5,1},{6,2},{7,3},{8,12},{9,13},{10,... | collective-permute-start | bytes 18440 | tf_op jit(solution)/shard_map/ppermute | solution.py:413
  31.8 3.7 %collective-permute-start.7 = (f32[8,192]{1,0:T(8,128)S(1)}, f32[8,192]{1,0:T(8,128)S(1)}, u32[]{:S(2)}, u32[]{:S(2)}) collective-permute-start(f32[8,192]{1,0:T(8,128)S(1)} %merge.1.refs_0_), channel_id=1, source_target_pairs={{0,2},{1,3},{2,0},{3,1},{4,6},{5,7},{6,4},{7,5},{8,10},{9,11},{10,... | collective-permute-start | bytes 18440 | tf_op jit(solution)/shard_map/ppermute | solution.py:413
  38.5 14.3 %collective-permute-start.8 = (bf16[232,256]{1,0:T(8,128)(2,1)S(1)}, bf16[232,256]{1,0:T(8,128)(2,1)S(1)}, u32[]{:S(2)}, u32[]{:S(2)}) collective-permute-start(bf16[232,256]{1,0:T(8,128)(2,1)S(1)} %update.4.refs_0_), channel_id=1, source_target_pairs={{0,8},{1,9},{2,10},{3,11},{4,12},{5,13},{6,14},{7,15},{8,0},{9,1},... | collective-permute-start | bytes 356360 | tf_op jit(solution)/shard_map/ppermute | solution.py:413
  44.7 10.0 %collective-permute-start.9 = (bf16[200,256]{1,0:T(8,128)(2,1)S(1)}, bf16[200,256]{1,0:T(8,128)(2,1)S(1)}, u32[]{:S(2)}, u32[]{:S(2)}) collective-permute-start(bf16[200,256]{1,0:T(8,128)(2,1)S(1)} %update.5.refs_1_.refs_0_), channel_id=1, source_target_pairs={{0,8},{1,9},{2,10},{3,11},{4,12},{5,13},{6,14},{7,15},{8,0},{9,1},... | collective-permute-start | bytes 307208 | tf_op jit(solution)/shard_map/ppermute | solution.py:413
  47.4 10.3 %collective-permute-start.10 = (bf16[200,256]{1,0:T(8,128)(2,1)S(1)}, bf16[200,256]{1,0:T(8,128)(2,1)S(1)}, u32[]{:S(2)}, u32[]{:S(2)}) collective-permute-start(bf16[200,256]{1,0:T(8,128)(2,1)S(1)} %update.6.refs_1_.refs_0_), channel_id=1, source_target_pairs={{0,8},{1,9},{2,10},{3,11},{4,12},{5,13},{6,14},{7,15},{8,0},{9,1},... | collective-permute-start | bytes 307208 | tf_op jit(solution)/shard_map/ppermute | solution.py:413
  52.3 7.6 %collective-permute-start.12 = (bf16[200,256]{1,0:T(8,128)(2,1)S(1)}, bf16[200,256]{1,0:T(8,128)(2,1)S(1)}, u32[]{:S(2)}, u32[]{:S(2)}) collective-permute-start(bf16[200,256]{1,0:T(8,128)(2,1)S(1)} %update.7.refs_1_), channel_id=1, source_target_pairs={{0,8},{1,9},{2,10},{3,11},{4,12},{5,13},{6,14},{7,15},{8,0},{9,1},... | collective-permute-start | bytes 307208 | tf_op jit(solution)/shard_map/ppermute | solution.py:413
  53.0 10.1 %copy-start = (f32[100,4096]{1,0:T(8,128)S(1)}, f32[100,4096]{1,0:T(8,128)}, u32[]{:S(2)}) copy-start(f32[100,4096]{1,0:T(8,128)} %classes.3) | copy-start | bytes 4915204
  53.0 7.9 %collective-permute-start.14 = (bf16[200,256]{1,0:T(8,128)(2,1)S(1)}, bf16[200,256]{1,0:T(8,128)(2,1)S(1)}, u32[]{:S(2)}, u32[]{:S(2)}) collective-permute-start(bf16[200,256]{1,0:T(8,128)(2,1)S(1)} %get-tuple-element.31.refs_0_), channel_id=1, source_target_pairs={{0,4},{1,5},{2,6},{3,7},{4,0},{5,1},{6,2},{7,3},{8,12},{9,13},{10,... | collective-permute-start | bytes 307208 | tf_op jit(solution)/shard_map/ppermute | solution.py:413
  54.8 8.3 %collective-permute-start.15 = (bf16[200,256]{1,0:T(8,128)(2,1)S(1)}, bf16[200,256]{1,0:T(8,128)(2,1)S(1)}, u32[]{:S(2)}, u32[]{:S(2)}) collective-permute-start(bf16[200,256]{1,0:T(8,128)(2,1)S(1)} %divide.5.refs_0_.refs_2_), channel_id=1, source_target_pairs={{0,4},{1,5},{2,6},{3,7},{4,0},{5,1},{6,2},{7,3},{8,12},{9,13},{10,... | collective-permute-start | bytes 307208 | tf_op jit(solution)/shard_map/ppermute | solution.py:413
  57.8 6.9 %collective-permute-start.11 = (bf16[200,256]{1,0:T(8,128)(2,1)S(1)}, bf16[200,256]{1,0:T(8,128)(2,1)S(1)}, u32[]{:S(2)}, u32[]{:S(2)}) collective-permute-start(bf16[200,256]{1,0:T(8,128)(2,1)S(1)} %divide.6.refs_0_), channel_id=1, source_target_pairs={{0,4},{1,5},{2,6},{3,7},{4,0},{5,1},{6,2},{7,3},{8,12},{9,13},{10,... | collective-permute-start | bytes 307208 | tf_op jit(solution)/shard_map/ppermute | solution.py:413
  60.1 5.2 %collective-permute-start.13 = (bf16[200,256]{1,0:T(8,128)(2,1)S(1)}, bf16[200,256]{1,0:T(8,128)(2,1)S(1)}, u32[]{:S(2)}, u32[]{:S(2)}) collective-permute-start(bf16[200,256]{1,0:T(8,128)(2,1)S(1)} %divide.7.refs_2_), channel_id=1, source_target_pairs={{0,4},{1,5},{2,6},{3,7},{4,0},{5,1},{6,2},{7,3},{8,12},{9,13},{10,... | collective-permute-start | bytes 307208 | tf_op jit(solution)/shard_map/ppermute | solution.py:413
  (1 other events, 1.2 us)
